TPU v7x, 32 devices: a whole 2x2x4 slice. The times are simulated.
32 devices in a mesh: replica: 4 (over y, x), inner: 8 (over z, core).
Axes of the slice: x: 2, y: 2, z: 4, core: 2. Of those that a mesh axis runs over, the one named last changes fastest.
Arguments:
- tokens: bfloat16 [4096, 2048], P(('replica', 'inner')), may hold values from -6 to 6
- w_query: bfloat16 [2048, 2048], P('inner'), may hold values from -0.15625 to 0.15625
- w_key: bfloat16 [2048, 2048], P('inner'), may hold values from -0.15625 to 0.15625
- w_value: bfloat16 [2048, 2048], P('inner'), may hold values from -0.125 to 0.125
- w_out: bfloat16 [2048, 2048], P('inner'), may hold values from -0.75 to 0.75
- w_gate: bfloat16 [2048, 8192], P('inner'), may hold values from -0.125 to 0.125
- w_up: bfloat16 [2048, 8192], P('inner'), may hold values from -0.125 to 0.125
- w_down: bfloat16 [8192, 2048], P('inner'), may hold values from -0.0625 to 0.0625
- gain_attn: bfloat16 [2048], P('inner'), may hold values from 0.5 to 1.5
- gain_ffn: bfloat16 [2048], P('inner'), may hold values from 0.5 to 1.5
- pieces: int32 [4096], P(('replica', 'inner')), may hold values from -1 to 15, as said below
- positions: int32 [4096], P(('replica', 'inner')), may hold values from 0 to 783, as said below
- cotangent: bfloat16 [4096, 2048], P(('replica', 'inner')), may hold values from -6 to 6
Outputs:
- output: bfloat16 [4096, 2048], P(('replica', 'inner'))
- grad_tokens: float32 [4096, 2048], P(('replica', 'inner'))
- grad_query: float32 [2048, 2048], P('inner')
- grad_key: float32 [2048, 2048], P('inner')
- grad_value: float32 [2048, 2048], P('inner')
- grad_out: float32 [2048, 2048], P('inner')
- grad_gate: float32 [2048, 8192], P('inner')
- grad_up: float32 [2048, 8192], P('inner')
- grad_down: float32 [8192, 2048], P('inner')
- grad_gain_attn: float32 [2048], P('inner')
- grad_gain_ffn: float32 [2048], P('inner')
Inputs may be any that keep to these rules, and one draw needn't show every extreme that they name: `pieces`: image tokens come in aligned blocks of 256 tokens of one sequence (2048 on the larger slice) that share one id, the block's index among all 16 blocks; text tokens have -1. In every sequence the first block is text and the last block is an image. `positions`: A text token's position is its index within its sequence; an image token's is its block's first index within the sequence plus its index within the block modulo 16.
All inputs are finite; a program needn't handle non-finite values.
Results may differ from a plain program's by a relative error of at most 0.02.
Values may be sent and summed in bfloat16 or wider, within the bound.
A program may use at most 448 MiB of HBM per device.

v0:
```python
import math

import jax
import jax.numpy as jnp
from jax import lax
from jax.sharding import PartitionSpec as P

D = 2048
HEADS = 16
HEAD_DIM = 128
FF = 8192
PIECE = 256


epsilon = 1e-06
rope_base = 10000.0
dims_rows = (((1,), (1,)), ((), ()))
dims_cols = (((0,), (0,)), ((), ()))


def rope_tables(positions):
    half_dim = HEAD_DIM // 2
    frequency = rope_base ** (-jnp.arange(half_dim, dtype=jnp.float32) * 2.0 / HEAD_DIM)
    angle = positions.astype(jnp.float32)[:, None] * frequency[None, :]
    return (jnp.cos(angle), jnp.sin(angle))


def rotate(heads, cosine, sine):
    half_dim = HEAD_DIM // 2
    first_half = heads[..., :half_dim]
    second_half = heads[..., half_dim:]
    cosine = cosine[:, None, :]
    sine = sine[:, None, :]
    return jnp.concatenate(
        [first_half * cosine - second_half * sine, first_half * sine + second_half * cosine],
        axis=-1,
    )


def rms_scale(values):
    return lax.rsqrt(jnp.mean(values * values, axis=1, keepdims=True) + epsilon)


def norm_back(grad_normed, unit, scale, gain):
    grad_unit = grad_normed * gain
    gain_term = jnp.sum(grad_normed * unit, axis=0)
    grad_input = scale * (grad_unit - unit * jnp.mean(grad_unit * unit, axis=1, keepdims=True))
    return (grad_input, gain_term)


def sigmoid_scores(query, all_keys, visible, score_bias):
    score = (
        jnp.einsum("qhd,khd->hqk", query, all_keys, preferred_element_type=jnp.float32)
        / math.sqrt(HEAD_DIM)
        + score_bias
    )
    squashed = jax.nn.sigmoid(score)
    return (squashed, (squashed * visible).astype(jnp.bfloat16))


def local(
    tokens,
    w_query,
    w_key,
    w_value,
    w_out,
    w_gate,
    w_up,
    w_down,
    gain_attn,
    gain_ffn,
    pieces,
    positions,
    cotangent,
):
    tok_rows = tokens.shape[0]
    row_share = w_query.shape[0]
    length = tok_rows * lax.axis_size("inner")
    device_place = lax.axis_index("inner")
    score_bias = -math.log(length)
    widen = FF // D
    whole = (
        lax.all_gather(w_query, "inner", axis=0, tiled=True),
        lax.all_gather(w_key, "inner", axis=0, tiled=True),
        lax.all_gather(w_value, "inner", axis=0, tiled=True),
        lax.all_gather(w_out, "inner", axis=0, tiled=True),
        lax.all_gather(gain_attn, "inner", axis=0, tiled=True),
        lax.all_gather(gain_ffn, "inner", axis=0, tiled=True),
    )
    query_full, key_full, value_full, out_full = (whole[0], whole[1], whole[2], whole[3])
    attn_gain = whole[4].astype(jnp.float32)
    ffn_gain = whole[5].astype(jnp.float32)
    inputs = tokens.astype(jnp.float32)
    cosine, sine = rope_tables(positions)
    scale_one = rms_scale(inputs)
    unit_one = inputs * scale_one
    normed_one = (unit_one * attn_gain).astype(jnp.bfloat16)
    query_lin = jnp.dot(normed_one, query_full, preferred_element_type=jnp.float32)
    key_lin = jnp.dot(normed_one, key_full, preferred_element_type=jnp.float32)
    value_own = jnp.dot(normed_one, value_full, preferred_element_type=jnp.float32).astype(
        jnp.bfloat16
    )
    query = rotate(query_lin.reshape(tok_rows, HEADS, HEAD_DIM), cosine, sine).astype(jnp.bfloat16)
    key_own = (
        rotate(key_lin.reshape(tok_rows, HEADS, HEAD_DIM), cosine, sine)
        .astype(jnp.bfloat16)
        .reshape(tok_rows, D)
    )
    all_keys, all_values = (
        lax.all_gather(key_own, "inner", axis=0, tiled=True),
        lax.all_gather(value_own, "inner", axis=0, tiled=True),
    )
    all_keys = all_keys.reshape(length, HEADS, HEAD_DIM)
    all_values = all_values.reshape(length, HEADS, HEAD_DIM)
    query_index = device_place * tok_rows + jnp.arange(tok_rows)
    key_index = jnp.arange(length)
    visible = (key_index[None, :] <= query_index[:, None]) | (
        key_index[None, :] // PIECE == query_index[:, None] // PIECE
    ) & (pieces[:, None] >= 0)
    visible = visible.astype(jnp.float32)[None]
    squashed, prob_weights = sigmoid_scores(query, all_keys, visible, score_bias)
    attended = (
        jnp.einsum("hqk,khd->qhd", prob_weights, all_values, preferred_element_type=jnp.float32)
        .reshape(tok_rows, D)
        .astype(jnp.bfloat16)
    )
    middle = inputs + jnp.dot(attended, out_full, preferred_element_type=jnp.float32)
    scale_two = rms_scale(middle)
    unit_two = middle * scale_two
    normed_two = (unit_two * ffn_gain).astype(jnp.bfloat16)
    slabs = (
        lax.all_gather(w_gate, "inner", axis=0, tiled=True),
        lax.all_gather(w_up, "inner", axis=0, tiled=True),
    )
    columns = normed_two
    gate = jnp.dot(columns, slabs[0], preferred_element_type=jnp.float32)
    up_lin = jnp.dot(columns, slabs[1], preferred_element_type=jnp.float32)
    gate_sigmoid = jax.nn.sigmoid(gate)
    silu_gate = gate * gate_sigmoid
    hidden = (silu_gate * up_lin).astype(jnp.bfloat16)
    columns = hidden
    mlp = jnp.dot(
        columns,
        lax.all_gather(w_down, "inner", axis=0, tiled=True),
        preferred_element_type=jnp.float32,
    )
    output = (middle + mlp).astype(jnp.bfloat16)
    upstream = cotangent.astype(jnp.float32)
    grad_hidden = lax.dot_general(
        cotangent,
        lax.all_gather(w_down, "inner", axis=0, tiled=True),
        dims_rows,
        preferred_element_type=jnp.float32,
    )
    grad_gate = (grad_hidden * up_lin * gate_sigmoid * (1.0 + gate * (1.0 - gate_sigmoid))).astype(
        jnp.bfloat16
    )
    grad_up = (grad_hidden * silu_gate).astype(jnp.bfloat16)
    group_acts = (
        lax.all_gather(grad_gate, "inner", axis=0, tiled=True),
        lax.all_gather(grad_up, "inner", axis=0, tiled=True),
        lax.all_gather(cotangent, "inner", axis=0, tiled=True),
    )
    owner_cols = (
        lax.all_to_all(normed_two, "inner", split_axis=1, concat_axis=0, tiled=True),
        lax.all_to_all(hidden, "inner", split_axis=1, concat_axis=0, tiled=True),
    )
    gate_rows = lax.dot_general(
        owner_cols[0], group_acts[0], dims_cols, preferred_element_type=jnp.float32
    )
    up_rows = lax.dot_general(
        owner_cols[0], group_acts[1], dims_cols, preferred_element_type=jnp.float32
    )
    down_rows = lax.dot_general(
        owner_cols[1], group_acts[2], dims_cols, preferred_element_type=jnp.float32
    ).reshape(row_share, widen * D)
    ffn_share = jnp.concatenate((gate_rows, up_rows, down_rows), axis=1)
    slabs = (
        lax.all_gather(w_gate, "inner", axis=0, tiled=True),
        lax.all_gather(w_up, "inner", axis=0, tiled=True),
    )
    columns = lax.dot_general(
        grad_gate, slabs[0], dims_rows, preferred_element_type=jnp.float32
    ) + lax.dot_general(grad_up, slabs[1], dims_rows, preferred_element_type=jnp.float32)
    grad_from_two, ffn_gain_term = norm_back(columns, unit_two, scale_two, ffn_gain)
    grad_middle = upstream + grad_from_two
    grad_attn = grad_middle.astype(jnp.bfloat16)
    grad_attended = (
        lax.dot_general(grad_attn, out_full, dims_rows, preferred_element_type=jnp.float32)
        .astype(jnp.bfloat16)
        .reshape(tok_rows, HEADS, HEAD_DIM)
    )
    squashed, prob_weights = sigmoid_scores(query, all_keys, visible, score_bias)
    grad_prob = jnp.einsum(
        "qhd,khd->hqk", grad_attended, all_values, preferred_element_type=jnp.float32
    )
    grad_score = (grad_prob * squashed * (1.0 - squashed) * visible).astype(jnp.bfloat16)
    grad_query_rot = jnp.einsum(
        "hqk,khd->qhd", grad_score, all_keys, preferred_element_type=jnp.float32
    ) / math.sqrt(HEAD_DIM)
    key_term = jnp.einsum(
        "hqk,qhd->khd", grad_score, query, preferred_element_type=jnp.float32
    ).reshape(tok_rows * lax.axis_size("inner"), D) / math.sqrt(HEAD_DIM)
    value_term = jnp.einsum(
        "hqk,qhd->khd", prob_weights, grad_attended, preferred_element_type=jnp.float32
    ).reshape(tok_rows * lax.axis_size("inner"), D)
    kv_share = lax.psum_scatter(
        jnp.concatenate((key_term, value_term), axis=1).astype(jnp.bfloat16),
        "inner",
        scatter_dimension=0,
        tiled=True,
    ).astype(jnp.float32)
    grad_query_lin = rotate(grad_query_rot, cosine, -sine).astype(jnp.bfloat16).reshape(tok_rows, D)
    grad_key_lin = (
        rotate(kv_share[:, :D].reshape(tok_rows, HEADS, HEAD_DIM), cosine, -sine)
        .astype(jnp.bfloat16)
        .reshape(tok_rows, D)
    )
    grad_value_lin = kv_share[:, D:].astype(jnp.bfloat16)
    group_grads = (
        lax.all_gather(grad_query_lin, "inner", axis=0, tiled=True),
        lax.all_gather(grad_key_lin, "inner", axis=0, tiled=True),
        lax.all_gather(grad_value_lin, "inner", axis=0, tiled=True),
        lax.all_gather(grad_attn, "inner", axis=0, tiled=True),
    )
    owner_attn = (
        lax.all_to_all(normed_one, "inner", split_axis=1, concat_axis=0, tiled=True),
        lax.all_to_all(attended, "inner", split_axis=1, concat_axis=0, tiled=True),
    )
    attn_share = jnp.concatenate(
        (
            lax.dot_general(
                owner_attn[0], group_grads[0], dims_cols, preferred_element_type=jnp.float32
            ),
            lax.dot_general(
                owner_attn[0], group_grads[1], dims_cols, preferred_element_type=jnp.float32
            ),
            lax.dot_general(
                owner_attn[0], group_grads[2], dims_cols, preferred_element_type=jnp.float32
            ),
            lax.dot_general(
                owner_attn[1], group_grads[3], dims_cols, preferred_element_type=jnp.float32
            ),
        ),
        axis=1,
    )
    grad_normed_one = lax.dot_general(
        grad_query_lin, query_full, dims_rows, preferred_element_type=jnp.float32
    )
    grad_normed_one = grad_normed_one + lax.dot_general(
        grad_key_lin, key_full, dims_rows, preferred_element_type=jnp.float32
    )
    grad_normed_one = grad_normed_one + lax.dot_general(
        grad_value_lin, value_full, dims_rows, preferred_element_type=jnp.float32
    )
    grad_from_one, attn_gain_term = norm_back(grad_normed_one, unit_one, scale_one, attn_gain)
    grad_tokens = grad_middle + grad_from_one
    gain_parts = (
        lax.psum_scatter(attn_gain_term, "inner", scatter_dimension=0, tiled=True),
        lax.psum_scatter(ffn_gain_term, "inner", scatter_dimension=0, tiled=True),
    )
    summed = (
        lax.psum(attn_share.astype(jnp.bfloat16), "replica").astype(jnp.float32),
        lax.psum(ffn_share.astype(jnp.bfloat16), "replica").astype(jnp.float32),
        lax.psum(gain_parts[0].astype(jnp.bfloat16), "replica").astype(jnp.float32),
        lax.psum(gain_parts[1].astype(jnp.bfloat16), "replica").astype(jnp.float32),
    )
    attn_sum, ffn_sum = (summed[0], summed[1])
    return (
        output,
        grad_tokens,
        attn_sum[:, :D],
        attn_sum[:, D : 2 * D],
        attn_sum[:, 2 * D : 3 * D],
        attn_sum[:, 3 * D :],
        ffn_sum[:, :FF],
        ffn_sum[:, FF : 2 * FF],
        ffn_sum[:, 2 * FF :].reshape(row_share * widen, D),
        summed[2],
        summed[3],
    )


def solution(mesh):
    return jax.shard_map(
        local,
        mesh=mesh,
        in_specs=(
            P(("replica", "inner"), None),
            P("inner", None),
            P("inner", None),
            P("inner", None),
            P("inner", None),
            P("inner", None),
            P("inner", None),
            P("inner", None),
            P("inner"),
            P("inner"),
            P(("replica", "inner")),
            P(("replica", "inner")),
            P(("replica", "inner"), None),
        ),
        out_specs=(
            P(("replica", "inner"), None),
            P(("replica", "inner"), None),
            P("inner", None),
            P("inner", None),
            P("inner", None),
            P("inner", None),
            P("inner", None),
            P("inner", None),
            P("inner", None),
            P("inner"),
            P("inner"),
        ),
        check_vma=False,
    )
```

profile of v0, /device:TPU:0, one launch (start us, length us, event | category | flops | bytes accessed | tf_op | source)
XLA Modules:
  0.0 2461.3 jit_solution(2208580539851227002)
XLA Ops:
  10.1 13.4 all-gather
  26.0 68.4 %all-gather.23.cloned.1.call-done = bf16[2048,2048]{1,0:T(8,128)(2,1)} async-done(((bf16[256,2048]{1,0:T(8,128)(2,1)}), bf16[2048,2048]{1,0:T(8,128)(2,1)}) %all-gather.23.cloned.1.call-update) | async-done | bytes 8388624 | tf_op jit(solution)/shard_map/all_gather | solution.py:83
  99.3 77.4 %all-gather.25.cloned.1.call-done = bf16[2048,2048]{1,0:T(8,128)(2,1)} async-done(((bf16[256,2048]{1,0:T(8,128)(2,1)}), bf16[2048,2048]{1,0:T(8,128)(2,1)}) %all-gather.25.cloned.1.call-update) | async-done | bytes 8388624 | tf_op jit(solution)/shard_map/all_gather | solution.py:84
  184.9 73.9 %all-gather.19.cloned.1.call-done = bf16[2048,2048]{1,0:T(8,128)(2,1)} async-done(((bf16[256,2048]{1,0:T(8,128)(2,1)}), bf16[2048,2048]{1,0:T(8,128)(2,1)}) %all-gather.19.cloned.1.call-update) | async-done | bytes 8388624 | tf_op jit(solution)/shard_map/all_gather | solution.py:85
  258.9 5.4 convolution_convert_fusion.9
  267.2 9.1 all-gather.1
  276.6 30.7 %all-gather.27.cloned.1.call-done = bf16[1024,2048]{0,1:T(8,128)(2,1)} async-done(((bf16[128,2048]{0,1:T(8,128)(2,1)}), bf16[1024,2048]{0,1:T(8,128)(2,1)}) %all-gather.27.cloned.1.call-update) | async-done | bytes 4194320 | tf_op jit(solution)/shard_map/all_gather | solution.py:110
  307.3 8.0 add_divide_fusion
  315.3 39.4 %all-gather.21.cloned.1.call-done = bf16[1024,2048]{1,0:T(8,128)(2,1)} async-done(((bf16[128,2048]{1,0:T(8,128)(2,1)}), bf16[1024,2048]{1,0:T(8,128)(2,1)}) %all-gather.21.cloned.1.call-update) | async-done | bytes 4194320 | tf_op jit(solution)/shard_map/all_gather | solution.py:111
  354.7 6.5 fusion.15
  361.3 75.7 %all-gather.29.cloned.1.call-done = bf16[2048,2048]{1,0:T(8,128)(2,1)} async-done(((bf16[256,2048]{1,0:T(8,128)(2,1)}), bf16[2048,2048]{1,0:T(8,128)(2,1)}) %all-gather.29.cloned.1.call-update) | async-done | bytes 8388624 | tf_op jit(solution)/shard_map/all_gather | solution.py:86
  441.9 283.9 %all-gather.31.cloned.1.call-done = bf16[2048,8192]{1,0:T(8,128)(2,1)} async-done(((bf16[256,8192]{1,0:T(8,128)(2,1)}), bf16[2048,8192]{1,0:T(8,128)(2,1)}) %all-gather.31.cloned.1.call-update) | async-done | bytes 33554448 | tf_op jit(solution)/shard_map/all_gather | solution.py:132
  725.8 19.6 fusion.41
  745.4 268.8 %all-gather.33.cloned.1.call-done = bf16[2048,8192]{1,0:T(8,128)(2,1)} async-done(((bf16[256,8192]{1,0:T(8,128)(2,1)}), bf16[2048,8192]{1,0:T(8,128)(2,1)}) %all-gather.33.cloned.1.call-update) | async-done | bytes 33554448 | tf_op jit(solution)/shard_map/all_gather | solution.py:133
  1014.2 19.8 fusion.42
  1034.1 268.6 %all-gather.35.cloned.1.call-done = bf16[8192,2048]{1,0:T(8,128)(2,1)} async-done(((bf16[1024,2048]{1,0:T(8,128)(2,1)}), bf16[8192,2048]{1,0:T(8,128)(2,1)}) %all-gather.35.cloned.1.call-update) | async-done | bytes 33554448 | tf_op jit(solution)/shard_map/all_gather | solution.py:144
  1302.7 20.9 multiply_convert_fusion.3
  1323.6 17.3 fusion.43
  1340.9 16.9 multiply_reduce_fusion
  1359.9 7.3 convolution_convert_fusion.8
  1368.5 6.8 convolution_convert_fusion.3
  1375.3 5.1 multiply_convert_fusion.1
  1383.9 7.8 pad_maximum_fusion.1
  1391.7 11.9 copy.78
  1405.0 5.2 fusion.14
  1410.3 81.3 %reduce-scatter.4.cloned.1.call-done = bf16[128,4096]{1,0:T(8,128)(2,1)} async-done(((bf16[1024,4096]{1,0:T(8,128)(2,1)}), bf16[128,4096]{1,0:T(8,128)(2,1)}) %reduce-scatter.4.cloned.1.call-update) | async-done | bytes 1048592
  1520.8 25.3 %all-to-all-done.1 = bf16[128,8,256]{2,0,1:T(8,128)(2,1)S(1)} async-done(((bf16[128,8,256]{2,0,1:T(8,128)(2,1)}), bf16[128,8,256]{2,0,1:T(8,128)(2,1)S(1)}, u32[]{:S(2)}, u32[]{:S(2)}) %all-to-all-start.1) | async-done | bytes 524320 | tf_op jit(solution)/shard_map/all_to_all | solution.py:228
  1552.1 81.1 %all-to-all-done.3 = bf16[128,8,1024]{2,0,1:T(8,128)(2,1)} async-done(((bf16[128,8,1024]{2,0,1:T(8,128)(2,1)}), bf16[128,8,1024]{2,0,1:T(8,128)(2,1)}, u32[]{:S(2)}, u32[]{:S(2)}) %all-to-all-start.3) | async-done | bytes 2097184 | tf_op jit(solution)/shard_map/all_to_all | solution.py:166
  1636.9 9.4 convolution_convert_fusion.2
  1646.3 7.9 reshape.326
  1661.4 8.5 all-to-all-start.2
  1670.0 29.0 %all-gather.39.cloned.1.call-done = bf16[1024,2048]{0,1:T(8,128)(2,1)} async-done(((bf16[128,2048]{0,1:T(8,128)(2,1)}), bf16[1024,2048]{0,1:T(8,128)(2,1)}) %all-gather.39.cloned.1.call-update) | async-done | bytes 4194320 | tf_op jit(solution)/shard_map/all_gather | solution.py:222
  1703.4 43.8 %all-gather.37.cloned.1.call-done = bf16[1024,2048]{0,1:T(8,128)(2,1)} async-done(((bf16[128,2048]{0,1:T(8,128)(2,1)}), bf16[1024,2048]{0,1:T(8,128)(2,1)}) %all-gather.37.cloned.1.call-update) | async-done | bytes 4194320 | tf_op jit(solution)/shard_map/all_gather | solution.py:221
  1751.7 43.0 %all-gather.41.cloned.1.call-done = bf16[1024,2048]{0,1:T(8,128)(2,1)} async-done(((bf16[128,2048]{0,1:T(8,128)(2,1)}), bf16[1024,2048]{0,1:T(8,128)(2,1)}) %all-gather.41.cloned.1.call-update) | async-done | bytes 4194320 | tf_op jit(solution)/shard_map/all_gather | solution.py:223
  1800.9 145.3 %all-gather.47.cloned.1.call-done = bf16[1024,8192]{1,0:T(8,128)(2,1)} async-done(((bf16[128,8192]{1,0:T(8,128)(2,1)}), bf16[1024,8192]{1,0:T(8,128)(2,1)}) %all-gather.47.cloned.1.call-update) | async-done | bytes 16777232 | tf_op jit(solution)/shard_map/all_gather | solution.py:161
  1946.2 12.1 convolution_convert_fusion
  1958.3 139.3 %all-gather.45.cloned.1.call-done = bf16[1024,8192]{1,0:T(8,128)(2,1)} async-done(((bf16[128,8192]{1,0:T(8,128)(2,1)}), bf16[1024,8192]{1,0:T(8,128)(2,1)}) %all-gather.45.cloned.1.call-update) | async-done | bytes 16777232 | tf_op jit(solution)/shard_map/all_gather | solution.py:160
  2097.6 10.9 convolution_convert_fusion.1
  2108.5 11.2 pad_maximum_fusion
  2121.6 15.6 fusion.9
  2137.3 6.5 fusion.44
  2143.8 6.9 convolution_add_fusion.3
  2154.8 26.2 %all-reduce.2 = (bf16[2048]{0:T(1024)(128)(2,1)S(1)}, bf16[2048]{0:T(1024)(128)(2,1)S(1)}) all-reduce(f32[2048]{0:T(1024)S(1)} %get-tuple-element.13, f32[2048]{0:T(1024)S(1)} %get-tuple-element.11), channel_id=3, replica_groups=mesh['replica'=4,'inner'=8] {'inner'}, use_global_device_ids=true, to_apply=%region_8.9.clone | all-reduce | flops 4096 | bytes 24576
  2181.1 10.0 all-reduce.3
  2194.9 231.6 %all-reduce.7.cloned.1.call-done = (bf16[256,8192]{1,0:T(8,128)(2,1)}, bf16[256,24576]{1,0:T(8,128)(2,1)}) async-done(((bf16[256,8192]{1,0:T(8,128)(2,1)}, bf16[256,24576]{1,0:T(8,128)(2,1)}), (bf16[256,8192]{1,0:T(8,128)(2,1)}, bf16[256,24576]{1,0:T(8,128)(2,1)})) %all-reduce.7.cloned.1.call-update) | async-done | bytes 16777232 | tf_op jit(solution)/shard_map/psum | solution.py:263
  2426.6 11.7 fusion.35
  2438.3 9.8 reshape.327
  2448.1 6.0 fusion.36
  (165 shorter events, 104.7 us)
Async XLA Ops:
  7.2 18.6 copy-start.4
  7.2 87.2 %all-gather.23.cloned.1.call-start = ((), (), s32[]{:S(2)}) async-start(), calls=%async_computation.7 | async-start | bytes 9437184 | tf_op jit(solution)/shard_map/all_gather | solution.py:83
  7.9 168.7 %all-gather.25.cloned.1.call-start = ((), (), s32[]{:S(2)}) async-start(), calls=%async_computation.8 | async-start | bytes 9437184 | tf_op jit(solution)/shard_map/all_gather | solution.py:84
  8.7 250.2 %all-gather.19.cloned.1.call-start = ((), (), s32[]{:S(2)}) async-start(), calls=%async_computation.5 | async-start | bytes 9437184 | tf_op jit(solution)/shard_map/all_gather | solution.py:85
  9.4 297.9 %all-gather.27.cloned.1.call-start = ((), (), s32[]{:S(2)}) async-start(), calls=%async_computation.9 | async-start | bytes 4718592 | tf_op jit(solution)/shard_map/all_gather | solution.py:110
  23.6 75.5 %copy-start.23 = (f32[8,1,256]{2,1,0:T(1,128)}, f32[8,1,256]{2,1,0:T(1,128)S(1)}, u32[]{:S(2)}) copy-start(f32[8,1,256]{2,1,0:T(1,128)S(1)} %convert_element_type.139) | copy-start | bytes 24580
  25.5 73.6 %copy-start.25 = (f32[128]{0:T(128)}, f32[128]{0:T(128)S(1)}, u32[]{:S(2)}) copy-start(f32[128]{0:T(128)S(1)} %add_rsqrt_fusion.1) | copy-start | bytes 1540
  183.5 123.8 %copy-start.16 = (bf16[128,16,64]{2,0,1:T(8,128)(2,1)}, bf16[128,16,64]{2,0,1:T(8,128)(2,1)S(1)}, u32[]{:S(2)}) copy-start(bf16[128,16,64]{2,0,1:T(8,128)(2,1)S(1)} %get-tuple-element.33) | copy-start | bytes 786436
  183.5 123.8 %copy-start.18 = (bf16[128,16,64]{2,0,1:T(8,128)(2,1)}, bf16[128,16,64]{2,0,1:T(8,128)(2,1)S(1)}, u32[]{:S(2)}) copy-start(bf16[128,16,64]{2,0,1:T(8,128)(2,1)S(1)} %get-tuple-element.34) | copy-start | bytes 786436
  184.9 169.9 %all-gather.21.cloned.1.call-start = ((), (), s32[]{:S(2)}) async-start(), calls=%async_computation.6 | async-start | bytes 4718592 | tf_op jit(solution)/shard_map/all_gather | solution.py:111
  264.3 172.7 %all-gather.29.cloned.1.call-start = ((), (), s32[]{:S(2)}) async-start(), calls=%async_computation.10 | async-start | bytes 9437184 | tf_op jit(solution)/shard_map/all_gather | solution.py:86
  264.9 460.9 %all-gather.31.cloned.1.call-start = ((), (), s32[]{:S(2)}) async-start(), calls=%async_computation.11 | async-start | bytes 37748736 | tf_op jit(solution)/shard_map/all_gather | solution.py:132
  265.7 10.7 copy-start.28
  265.7 748.6 %all-gather.33.cloned.1.call-start = ((), (), s32[]{:S(2)}) async-start(), calls=%async_computation.12 | async-start | bytes 37748736 | tf_op jit(solution)/shard_map/all_gather | solution.py:133
  266.4 1036.3 %all-gather.35.cloned.1.call-start = ((), (), s32[]{:S(2)}) async-start(), calls=%async_computation.13 | async-start | bytes 37748736 | tf_op jit(solution)/shard_map/all_gather | solution.py:144
  267.2 1224.4 %reduce-scatter.4.cloned.1.call-start = ((), (), s32[]{:S(2)}) async-start(), calls=%async_computation.21 | async-start | bytes 9437184
  361.3 80.5 %copy-start.9 = (bf16[16,128,128]{2,1,0:T(8,128)(2,1)}, bf16[16,128,128]{2,1,0:T(8,128)(2,1)S(1)}, u32[]{:S(2)}) copy-start(bf16[16,128,128]{2,1,0:T(8,128)(2,1)S(1)} %fusion.15) | copy-start | bytes 1572868
  745.4 557.3 %copy-start.12 = (bf16[128,2048]{1,0:T(8,128)(2,1)S(1)}, bf16[128,2048]{1,0:T(8,128)(2,1)}, u32[]{:S(2)}) copy-start(bf16[128,2048]{1,0:T(8,128)(2,1)} %param.25) | copy-start | bytes 1572868
  1368.5 6.8 copy-start.1
  1375.3 5.1 copy-start.17
  1375.3 5.1 copy-start.19
  1403.7 233.2 %all-gather.49.cloned.1.call-start = ((), (), s32[]{:S(2)}) async-start(), calls=%async_computation.20 | async-start | bytes 4718592 | tf_op jit(solution)/shard_map/all_gather | solution.py:162
  1404.4 249.8 %all-gather.43.cloned.1.call-start = ((), (), s32[]{:S(2)}) async-start(), calls=%async_computation.17 | async-start | bytes 4718592 | tf_op jit(solution)/shard_map/all_gather | solution.py:224
  1405.0 294.0 %all-gather.39.cloned.1.call-start = ((), (), s32[]{:S(2)}) async-start(), calls=%async_computation.15 | async-start | bytes 4718592 | tf_op jit(solution)/shard_map/all_gather | solution.py:222
  1507.1 240.2 %all-gather.37.cloned.1.call-start = ((), (), s32[]{:S(2)}) async-start(), calls=%async_computation.14 | async-start | bytes 4718592 | tf_op jit(solution)/shard_map/all_gather | solution.py:221
  1507.1 5.9 copy-start.10
  1509.8 285.0 %all-gather.41.cloned.1.call-start = ((), (), s32[]{:S(2)}) async-start(), calls=%async_computation.16 | async-start | bytes 4718592 | tf_op jit(solution)/shard_map/all_gather | solution.py:223
  1511.9 434.3 %all-gather.47.cloned.1.call-start = ((), (), s32[]{:S(2)}) async-start(), calls=%async_computation.19 | async-start | bytes 18874368 | tf_op jit(solution)/shard_map/all_gather | solution.py:161
  1512.5 585.1 %all-gather.45.cloned.1.call-start = ((), (), s32[]{:S(2)}) async-start(), calls=%async_computation.18 | async-start | bytes 18874368 | tf_op jit(solution)/shard_map/all_gather | solution.py:160
  1514.1 32.0 %all-to-all-start.1 = ((bf16[128,8,256]{2,0,1:T(8,128)(2,1)}), bf16[128,8,256]{2,0,1:T(8,128)(2,1)S(1)}, u32[]{:S(2)}, u32[]{:S(2)}) async-start(bf16[128,8,256]{2,0,1:T(8,128)(2,1)} %copy.72), calls=%async_computation.1 | async-start | bytes 1048576 | tf_op jit(solution)/shard_map/all_to_all | solution.py:228
  1546.1 100.2 %copy-start.22 = (bf16[128,8,256]{2,0,1:T(8,128)(2,1)}, bf16[128,8,256]{2,0,1:T(8,128)(2,1)S(1)}, u32[]{:S(2)}) copy-start(bf16[128,8,256]{2,0,1:T(8,128)(2,1)S(1)} %all-to-all-done.1) | copy-start | bytes 1572868
  1546.1 87.1 %all-to-all-start.3 = ((bf16[128,8,1024]{2,0,1:T(8,128)(2,1)}), bf16[128,8,1024]{2,0,1:T(8,128)(2,1)}, u32[]{:S(2)}, u32[]{:S(2)}) async-start(bf16[128,8,1024]{2,0,1:T(8,128)(2,1)} %bitcast.126), calls=%async_computation.3 | async-start | bytes 4194304 | tf_op jit(solution)/shard_map/all_to_all | solution.py:166
  1633.2 28.2 %all-to-all-start = ((bf16[128,8,256]{2,0,1:T(8,128)(2,1)}), bf16[128,8,256]{2,0,1:T(8,128)(2,1)S(1)}, u32[]{:S(2)}, u32[]{:S(2)}) async-start(bf16[128,8,256]{2,0,1:T(8,128)(2,1)} %bitcast.116), calls=%async_computation | async-start | bytes 1048576 | tf_op jit(solution)/shard_map/all_to_all | solution.py:227
  1661.4 139.5 %all-to-all-start.2 = ((bf16[128,8,256]{2,0,1:T(8,128)(2,1)}), bf16[128,8,256]{2,0,1:T(8,128)(2,1)S(1)}, u32[]{:S(2)}, u32[]{:S(2)}) async-start(bf16[128,8,256]{2,0,1:T(8,128)(2,1)} %bitcast.115), calls=%async_computation.2 | async-start | bytes 1048576 | tf_op jit(solution)/shard_map/all_to_all | solution.py:165
  1669.9 756.6 %all-reduce.7.cloned.1.call-start = ((), (), s32[]{:S(2)}) async-start(), calls=%async_computation.22 | async-start | bytes 33554432 | tf_op jit(solution)/shard_map/psum | solution.py:263
  1794.8 3.7 copy-start.21
  2097.6 10.9 copy-start.2
  2097.6 10.9 copy-start.3
  2121.6 15.6 copy-start.11
  2137.2 6.5 copy-start.14
  2137.2 13.5 slice-start
  2143.8 7.0 slice-start.1
  2143.8 7.0 copy-start.5
  2143.8 7.0 copy-start.15
  2143.8 7.0 copy-start.24
  2143.8 7.0 copy-start.26
  2150.8 41.4 %copy-start.8 = (f32[128,2048]{1,0:T(8,128)S(1)}, f32[128,2048]{1,0:T(8,128)}, u32[]{:S(2)}) copy-start(f32[128,2048]{1,0:T(8,128)} %copy-done.7) | copy-start | bytes 3145732
  2150.8 41.4 %copy-start.13 = (bf16[128,2048]{1,0:T(8,128)(2,1)S(1)}, bf16[128,2048]{1,0:T(8,128)(2,1)}, u32[]{:S(2)}) copy-start(bf16[128,2048]{1,0:T(8,128)(2,1)} %param.25) | copy-start | bytes 1572868
  (6 other events, 12.2 us)
Sparse Core Ops, SparseCore 0:
  9.6 84.7 all-gather.22
  96.0 80.5 all-gather.24
  178.2 80.5 all-gather.18
  260.9 46.3 all-gather.26
  309.3 45.3 all-gather.20
  356.2 80.7 all-gather.28
  438.6 287.1 all-gather.30
  727.4 286.8 all-gather.32
  1015.8 286.8 all-gather.34
  1403.8 87.7 reduce-scatter.3
  1493.2 56.5 all-gather.48
  1551.9 81.8 all-gather.42
  1635.3 63.5 all-gather.38
  1700.4 46.8 all-gather.36
  1748.7 46.0 all-gather.40
  1796.8 149.3 all-gather.46
  1948.2 149.3 all-gather.44
  2119.8 306.6 all-reduce.6
where the time goes:
time: 2470 us; the launch traced here: 2460 us
  waiting for transfers between devices  2020 us (82%)
  matrix products  238 us (10%)
  local copies, waits for them, and re-layouts  74.9 us (3%)
  blocking collectives  58.7 us (2%)
  other arithmetic  35.8 us (1%)
    all_gather x1, waiting for transfers between devices, local(): lax.all_gather(w_gate, 'inner', axis=0, tiled=True)  284 us
    all_gather x1, waiting for transfers between devices, local(): lax.all_gather(w_up, 'inner', axis=0, tiled=True)  269 us
    all_gather x1, waiting for transfers between devices, local(): lax.all_gather(w_down, 'inner', axis=0, tiled=True)  269 us
    psum x1, waiting for transfers between devices, local(): lax.psum(attn_share.astype(jnp.bfloat16), 'replica').astype(jnp.float32)  232 us
    all_gather x1, waiting for transfers between devices, local(): lax.all_gather(grad_up, 'inner', axis=0, tiled=True)  145 us
    all_gather x1, waiting for transfers between devices, local(): lax.all_gather(grad_gate, 'inner', axis=0, tiled=True)  139 us
    unnamed x19, waiting for transfers between devices  88.4 us
    all_to_all x1, waiting for transfers between devices, local(): lax.all_to_all(hidden, 'inner', split_axis=1, concat_axis=0, tiled=True)  81.1 us
  transfers between devices with their start and end apart: 22, of which 19 were waited for; matrix products, arithmetic and copies ran while one was open for 8% of the time, Pallas kernels for 0%

commit v1 on v0

v1 whole, which is shorter than its diff:
```python
import math

import jax
import jax.numpy as jnp
from jax import lax
from jax.sharding import PartitionSpec as P

HEAD_DIM = 128
PIECE = 256
epsilon = 1e-06
rope_base = 10000.0
dims_rows = (((1,), (1,)), ((), ()))
dims_cols = (((0,), (0,)), ((), ()))
f32 = jnp.float32
bf16 = jnp.bfloat16


def dot(a, b):
    return jnp.dot(a, b, preferred_element_type=f32)


def dot_t(a, b):
    return lax.dot_general(a, b, dims_rows, preferred_element_type=f32)


def t_dot(a, b):
    return lax.dot_general(a, b, dims_cols, preferred_element_type=f32)


def rope_tables(positions):
    half_dim = HEAD_DIM // 2
    frequency = rope_base ** (-jnp.arange(half_dim, dtype=f32) * 2.0 / HEAD_DIM)
    angle = positions.astype(f32)[:, None] * frequency[None, :]
    return jnp.cos(angle), jnp.sin(angle)


def rotate(flat, cosine, sine):
    half_dim = HEAD_DIM // 2
    heads = flat.reshape(flat.shape[0], -1, HEAD_DIM)
    a = heads[..., :half_dim]
    b = heads[..., half_dim:]
    cosine = cosine[:, None, :]
    sine = sine[:, None, :]
    return jnp.concatenate([a * cosine - b * sine, a * sine + b * cosine], axis=-1).reshape(flat.shape)


def rms_scale(values):
    return lax.rsqrt(jnp.mean(values * values, axis=1, keepdims=True) + epsilon)


def gather_tokens(block):
    return lax.all_gather(block, "inner", axis=0, tiled=True)


def scatter_tokens(partial):
    return lax.psum_scatter(partial.astype(bf16), "inner", scatter_dimension=0, tiled=True).astype(f32)


def column_shard(w):
    n = lax.axis_size("inner")
    nr = lax.axis_size("replica")
    rows, cols = w.shape
    part = rows // nr
    mine = lax.dynamic_slice_in_dim(w, lax.axis_index("replica") * part, part, 0)
    mine = mine.reshape(part, n, cols // n)
    got = lax.all_to_all(mine, "inner", split_axis=1, concat_axis=0, tiled=False)
    got = got.reshape(n, part, cols // n)
    full = lax.all_gather(got, "replica", axis=1, tiled=False)
    return full.reshape(n * rows, cols // n)


def owner_rows(g):
    n = lax.axis_size("inner")
    nr = lax.axis_size("replica")
    rows = g.shape[0] // n
    part = rows // nr
    cols = g.shape[1]
    g = g.astype(bf16).reshape(n, nr, part, cols).transpose(1, 0, 2, 3).reshape(nr * n * part, cols)
    mine = lax.psum_scatter(g, "replica", scatter_dimension=0, tiled=True).reshape(n, part, cols)
    got = lax.all_to_all(mine, "inner", split_axis=0, concat_axis=1, tiled=False)
    got = got.reshape(part, n * cols)
    return lax.all_gather(got, "replica", axis=0, tiled=True).astype(f32)


def sum_copies(g):
    mine = lax.psum_scatter(g.astype(bf16), "replica", scatter_dimension=0, tiled=True)
    return lax.all_gather(mine, "replica", axis=0, tiled=True).astype(f32)


def local(
    tokens,
    w_query,
    w_key,
    w_value,
    w_out,
    w_gate,
    w_up,
    w_down,
    gain_attn,
    gain_ffn,
    pieces,
    positions,
    cotangent,
):
    n = lax.axis_size("inner")
    place = lax.axis_index("inner")
    own = tokens.shape[0]
    length = own * n
    score_bias = -math.log(length)
    inv_root = 1.0 / math.sqrt(HEAD_DIM)
    heads = w_query.shape[1] // n // HEAD_DIM

    gains = lax.all_gather(jnp.stack([gain_attn, gain_ffn]), "inner", axis=1, tiled=True).astype(f32)
    attn_gain, ffn_gain = gains[0], gains[1]
    marks = lax.all_gather(jnp.stack([pieces, positions]), "inner", axis=1, tiled=True)
    pieces, positions = marks[0], marks[1]

    wq, wk, wv = column_shard(w_query), column_shard(w_key), column_shard(w_value)
    wg, wu = column_shard(w_gate), column_shard(w_up)

    x = gather_tokens(tokens).astype(f32)
    cot = gather_tokens(cotangent)
    cosine, sine = rope_tables(positions)
    r1 = rms_scale(x)
    u1 = x * r1
    n1 = (u1 * attn_gain).astype(bf16)
    q = rotate(dot(n1, wq), cosine, sine).astype(bf16).reshape(length, heads, HEAD_DIM)
    k = rotate(dot(n1, wk), cosine, sine).astype(bf16).reshape(length, heads, HEAD_DIM)
    v = dot(n1, wv).astype(bf16).reshape(length, heads, HEAD_DIM)

    index = jnp.arange(length)
    visible = (index[None, :] <= index[:, None]) | (
        (index[None, :] // PIECE == index[:, None] // PIECE) & (pieces[:, None] >= 0)
    )
    visible = visible.astype(f32)[None]

    def weights():
        score = jnp.einsum("qhd,khd->hqk", q, k, preferred_element_type=f32) * inv_root + score_bias
        sg = jax.nn.sigmoid(score)
        return sg, (sg * visible).astype(bf16)

    sg, p = weights()
    o = jnp.einsum("hqk,khd->qhd", p, v, preferred_element_type=f32).astype(bf16).reshape(length, -1)
    a = scatter_tokens(dot(o, w_out))
    mid = tokens.astype(f32) + a
    r2 = rms_scale(mid)
    u2 = mid * r2
    n2 = gather_tokens((u2 * ffn_gain).astype(bf16))

    gate = dot(n2, wg)
    up = dot(n2, wu)
    s = jax.nn.sigmoid(gate)
    silu = gate * s
    hid = (silu * up).astype(bf16)
    mlp = scatter_tokens(dot(hid, w_down))
    output = (mid + mlp).astype(bf16)

    ghid = dot_t(cot, w_down)
    ggate = (ghid * up * s * (1.0 + gate * (1.0 - s))).astype(bf16)
    gup = (ghid * silu).astype(bf16)
    gn2 = scatter_tokens(dot_t(ggate, wg) + dot_t(gup, wu))
    gu2 = gn2 * ffn_gain
    ffn_gain_part = jnp.sum(gn2 * u2, axis=0)
    gmid = cotangent.astype(f32) + r2 * (gu2 - u2 * jnp.mean(gu2 * u2, axis=1, keepdims=True))
    ga = gather_tokens(gmid.astype(bf16))

    grad_down = sum_copies(t_dot(hid, cot))
    grad_gate = owner_rows(t_dot(n2, ggate))
    grad_up = owner_rows(t_dot(n2, gup))

    go = dot_t(ga, w_out).astype(bf16).reshape(length, heads, HEAD_DIM)
    grad_out = sum_copies(t_dot(o, ga))
    gp = jnp.einsum("qhd,khd->hqk", go, v, preferred_element_type=f32)
    gs = (gp * sg * (1.0 - sg) * visible).astype(bf16)
    gq = jnp.einsum("hqk,khd->qhd", gs, k, preferred_element_type=f32).reshape(length, -1) * inv_root
    gk = jnp.einsum("hqk,qhd->khd", gs, q, preferred_element_type=f32).reshape(length, -1) * inv_root
    gv = jnp.einsum("hqk,qhd->khd", p, go, preferred_element_type=f32).reshape(length, -1)
    gql = rotate(gq, cosine, -sine).astype(bf16)
    gkl = rotate(gk, cosine, -sine).astype(bf16)
    gvl = gv.astype(bf16)
    gn1 = scatter_tokens(dot_t(gql, wq) + dot_t(gkl, wk) + dot_t(gvl, wv))
    grad_query = owner_rows(t_dot(n1, gql))
    grad_key = owner_rows(t_dot(n1, gkl))
    grad_value = owner_rows(t_dot(n1, gvl))

    own_x = tokens.astype(f32)
    r1 = rms_scale(own_x)
    u1 = own_x * r1
    gu1 = gn1 * attn_gain
    attn_gain_part = jnp.sum(gn1 * u1, axis=0)
    grad_tokens = gmid + r1 * (gu1 - u1 * jnp.mean(gu1 * u1, axis=1, keepdims=True))
    gain_sum = lax.psum(jnp.stack([attn_gain_part, ffn_gain_part]), ("replica", "inner"))
    rows = gain_attn.shape[0]
    gain_sum = lax.dynamic_slice_in_dim(gain_sum, place * rows, rows, 1)
    return (
        output,
        grad_tokens,
        grad_query,
        grad_key,
        grad_value,
        grad_out,
        grad_gate,
        grad_up,
        grad_down,
        gain_sum[0],
        gain_sum[1],
    )


def solution(mesh):
    tok = P(("replica", "inner"), None)
    row = P("inner", None)
    vec = P("inner")
    mark = P(("replica", "inner"))
    return jax.shard_map(
        local,
        mesh=mesh,
        in_specs=(tok, row, row, row, row, row, row, row, vec, vec, mark, mark, tok),
        out_specs=(tok, tok, row, row, row, row, row, row, row, vec, vec),
        check_vma=False,
    )
```

time: 2470 us -> 1300 us (0.53)
  waiting for transfers between devices: 2020 us -> 756 us
  blocking collectives: 58.7 us -> 289 us
  matrix products: 238 us -> 129 us
  local copies, waits for them, and re-layouts: 74.9 us -> 44.6 us
    all_gather x16, waiting for transfers between devices: 1590 us -> 487 us  [the longest x5 175 us: owner_rows(): return lax.all_gather(got, 'replica', axis=0, tiled=True).astype(f32)]
    reduce_scatter x0 -> x11, waiting for transfers between devices: none -> 267 us  [the longest x5 140 us: owner_rows(): lax.psum_scatter(g, 'replica', scatter_dimension=0, tiled=True)]
    psum x1 -> x0, waiting for transfers between devices: 232 us -> none  [local(): lax.psum(attn_share.astype(jnp.bfloat16), 'replica').astype(jnp.float32)]
    all_to_all x0 -> x10, blocking collectives: none -> 231 us  [the longest x5 125 us: column_shard(): lax.all_to_all(mine, 'inner', split_axis=1, concat_axis=0, tiled=False)]
    all_to_all x4 -> x0, waiting for transfers between devices: 110 us -> none  [the longest x1 81.1 us: local(): lax.all_to_all(hidden, 'inner', split_axis=1, concat_axis=0, tiled=True)]
    dot_general x27, matrix products: 238 us -> 129 us  [the longest x7 39.7 us: dot_t(): return lax.dot_general(a, b, dims_rows, preferred_element_type=f32)]
    unnamed x19 -> x27, waiting for transfers between devices: 88.4 us -> 2.27 us
    convert_element_type x9 -> x13, other arithmetic: 3.49 us -> 38 us  [the longest x5 21.5 us: owner_rows(): return lax.all_gather(got, 'replica', axis=0, tiled=True).astype(f32)]
  transfers between devices with their start and end apart: 22 -> 27, of which waited for: 19 -> 24; matrix products, arithmetic and copies ran while one was open for 8% -> 13% of each run, Pallas kernels for 0% -> 0%
where the time goes in v1:
time: 1300 us; the launch traced here: 1290 us
  waiting for transfers between devices  756 us (58%)
  blocking collectives  289 us (22%)
  matrix products  129 us (10%)
  other arithmetic  51.4 us (4%)
  local copies, waits for them, and re-layouts  44.6 us (3%)
  between operations  15.5 us (1%)
    all_gather x5, waiting for transfers between devices, owner_rows(): return lax.all_gather(got, 'replica', axis=0, tiled=True).astype(f32)  175 us
    reduce_scatter x5, waiting for transfers between devices, owner_rows(): lax.psum_scatter(g, 'replica', scatter_dimension=0, tiled=True)  140 us
    all_gather x4, waiting for transfers between devices, gather_tokens(): return lax.all_gather(block, 'inner', axis=0, tiled=True)  137 us
    all_gather x5, waiting for transfers between devices, column_shard(): full = lax.all_gather(got, 'replica', axis=1, tiled=False)  129 us
    all_to_all x5, blocking collectives, column_shard(): lax.all_to_all(mine, 'inner', split_axis=1, concat_axis=0, tiled=False)  125 us
    reduce_scatter x4, waiting for transfers between devices, scatter_tokens(): lax.psum_scatter(partial.astype(bf16), 'inner', scatter_dimension=0, tile...  108 us
    all_to_all x5, blocking collectives, owner_rows(): lax.all_to_all(mine, 'inner', split_axis=0, concat_axis=1, tiled=False)  105 us
    all_gather x2, waiting for transfers between devices, sum_copies(): return lax.all_gather(mine, 'replica', axis=0, tiled=True).astype(f32)  45 us
  transfers between devices with their start and end apart: 27, of which 24 were waited for; matrix products, arithmetic and copies ran while one was open for 13% of the time, Pallas kernels for 0%

profile of v1, /device:TPU:0, one launch (start us, length us, event | category | flops | bytes accessed | tf_op | source)
XLA Modules:
  0.0 1288.1 jit_solution(9325515200482436823)
XLA Ops:
  8.6 15.9 %all_to_all.150 = bf16[1,64,8,256]{3,1,0,2:T(8,128)(2,1)S(1)} all-to-all(bf16[1,64,8,256]{3,1,0,2:T(8,128)(2,1)S(1)} %copy.70), channel_id=1, replica_groups=mesh['replica'=4,'inner'=8] {'inner'}, dimensions={2} | all-to-all | bytes 524288 | tf_op jit(solution)/shard_map/all_to_all | solution.py:66
  25.5 12.1 all_to_all.151
  39.7 12.8 all_to_all.152
  53.3 9.6 all_gather.55
  62.9 9.2 all_gather.58
  82.8 25.8 %all-gather.44.cloned.1.call-done = bf16[8,4,64,1,256]{4,2,3,0,1:T(8,128)(2,1)} async-done(((bf16[8,1,64,1,256]{4,2,3,0,1:T(8,128)(2,1)}), bf16[8,4,64,1,256]{4,2,3,0,1:T(8,128)(2,1)}) %all-gather.44.cloned.1.call-update) | async-done | bytes 1048592 | tf_op jit(solution)/shard_map/all_gather | solution.py:68
  110.9 46.3 %all-gather.22.cloned.1.call-done = bf16[1024,2048]{1,0:T(8,128)(2,1)} async-done(((bf16[128,2048]{1,0:T(8,128)(2,1)}), bf16[1024,2048]{1,0:T(8,128)(2,1)}) %all-gather.22.cloned.1.call-update) | async-done | bytes 4194320 | tf_op jit(solution)/shard_map/all_gather | solution.py:52
  181.4 47.3 %all_to_all.153 = bf16[1,64,8,1024]{3,1,0,2:T(8,128)(2,1)} all-to-all(bf16[1,64,8,1024]{3,1,0,2:T(8,128)(2,1)S(1)} %copy.80), channel_id=1, replica_groups=mesh['replica'=4,'inner'=8] {'inner'}, dimensions={2} | all-to-all | bytes 2097152 | tf_op jit(solution)/shard_map/all_to_all | solution.py:66
  230.0 37.3 %all_to_all.154 = bf16[1,64,8,1024]{3,1,0,2:T(8,128)(2,1)} all-to-all(bf16[1,64,8,1024]{3,1,0,2:T(8,128)(2,1)S(1)} %copy.77), channel_id=1, replica_groups=mesh['replica'=4,'inner'=8] {'inner'}, dimensions={2} | all-to-all | bytes 2097152 | tf_op jit(solution)/shard_map/all_to_all | solution.py:66
  271.5 53.1 %all-gather.52.cloned.1.call-done = bf16[8,4,64,1,1024]{4,2,3,0,1:T(8,128)(2,1)} async-done(((bf16[8,1,64,1,1024]{4,2,3,0,1:T(8,128)(2,1)}), bf16[8,4,64,1,1024]{4,2,3,0,1:T(8,128)(2,1)}) %all-gather.52.cloned.1.call-update) | async-done | bytes 4194320 | tf_op jit(solution)/shard_map/all_gather | solution.py:68
  329.6 49.6 %all-gather.50.cloned.1.call-done = bf16[8,4,64,1,1024]{4,2,3,0,1:T(8,128)(2,1)} async-done(((bf16[8,1,64,1,1024]{4,2,3,0,1:T(8,128)(2,1)}), bf16[8,4,64,1,1024]{4,2,3,0,1:T(8,128)(2,1)}) %all-gather.50.cloned.1.call-update) | async-done | bytes 4194320 | tf_op jit(solution)/shard_map/all_gather | solution.py:68
  384.1 44.4 %all-gather.24.cloned.1.call-done = bf16[1024,2048]{1,0:T(8,128)(2,1)} async-done(((bf16[128,2048]{1,0:T(8,128)(2,1)}), bf16[1024,2048]{1,0:T(8,128)(2,1)}) %all-gather.24.cloned.1.call-update) | async-done | bytes 4194320 | tf_op jit(solution)/shard_map/all_gather | solution.py:52
  428.6 10.1 fusion.45
  438.7 6.5 fusion.44
  445.2 30.9 %all-gather.26.cloned.1.call-done = bf16[1024,2048]{1,0:T(8,128)(2,1)} async-done(((bf16[128,2048]{1,0:T(8,128)(2,1)}), bf16[1024,2048]{1,0:T(8,128)(2,1)}) %all-gather.26.cloned.1.call-update) | async-done | bytes 4194320 | tf_op jit(solution)/shard_map/all_gather | solution.py:52
  476.1 14.7 %multiply_convert_fusion.2 = (bf16[1024,1024]{1,0:T(8,128)(2,1)}, bf16[1024,1024]{1,0:T(8,128)(2,1)}, bf16[1024,1024]{1,0:T(8,128)(2,1)}) fusion(f32[1024,1024]{1,0:T(8,128)} %fusion.44, f32[1024,1024]{1,0:T(8,128)} %fusion.45, bf16[1024,2048]{1,0:T(8,128)(2,1)} %all-gather.26.cloned.1.call-done, bf16[1024,2048]{1,0:T(8,128)(2,1)} %param.20), kind=kOutput, calls=%fused_computation.14 | convolution fusion | flops 4310695936 | bytes 23068672 | tf_op jit(solution)/shard_map/dot_general | solution.py:23
  497.1 7.9 add_convert_fusion.1
  505.1 48.8 %reduce-scatter.16.cloned.1.call-done = bf16[128,2048]{1,0:T(8,128)(2,1)} async-done(((bf16[1024,2048]{1,0:T(8,128)(2,1)}), bf16[128,2048]{1,0:T(8,128)(2,1)}) %reduce-scatter.16.cloned.1.call-update) | async-done | bytes 524304 | tf_op jit(solution)/shard_map/reduce_scatter | solution.py:56
  557.9 9.4 convolution_convert_fusion.1
  567.6 7.5 convolution_convert_fusion.3
  577.6 7.5 convolution_convert_fusion.2
  587.7 15.6 %all-gather.28.cloned.1.call-done = bf16[1024,2048]{1,0:T(8,128)(2,1)} async-done(((bf16[128,2048]{1,0:T(8,128)(2,1)}), bf16[1024,2048]{1,0:T(8,128)(2,1)}) %all-gather.28.cloned.1.call-update) | async-done | bytes 4194320 | tf_op jit(solution)/shard_map/all_gather | solution.py:52
  619.9 6.6 multiply_convert_fusion
  638.9 18.6 %reduce-scatter.32.cloned.1.call-done = bf16[256,2048]{1,0:T(8,128)(2,1)} async-done(((bf16[1024,2048]{1,0:T(8,128)(2,1)}), bf16[256,2048]{1,0:T(8,128)(2,1)}) %reduce-scatter.32.cloned.1.call-update) | async-done | bytes 1048592 | tf_op jit(solution)/shard_map/reduce_scatter | solution.py:86
  657.6 56.4 %reduce-scatter.28.cloned.1.call-done = bf16[512,1024]{1,0:T(8,128)(2,1)} async-done(((bf16[2048,1024]{1,0:T(8,128)(2,1)}), bf16[512,1024]{1,0:T(8,128)(2,1)}) %reduce-scatter.28.cloned.1.call-update) | async-done | bytes 1048592 | tf_op jit(solution)/shard_map/reduce_scatter | solution.py:79
  714.1 31.2 %all_to_all.155 = bf16[8,64,1,1024]{3,1,2,0:T(8,128)(2,1)S(1)} all-to-all(bf16[8,64,1,1024]{3,1,2,0:T(8,128)(2,1)} %bitcast.242), channel_id=1, replica_groups=mesh['replica'=4,'inner'=8] {'inner'}, dimensions={0} | all-to-all | bytes 2097152 | tf_op jit(solution)/shard_map/all_to_all | solution.py:80
  746.4 23.2 %reduce-scatter.30.cloned.1.call-done = bf16[512,1024]{1,0:T(8,128)(2,1)} async-done(((bf16[2048,1024]{1,0:T(8,128)(2,1)}), bf16[512,1024]{1,0:T(8,128)(2,1)}) %reduce-scatter.30.cloned.1.call-update) | async-done | bytes 1048592 | tf_op jit(solution)/shard_map/reduce_scatter | solution.py:79
  769.6 31.2 %all_to_all.156 = bf16[8,64,1,1024]{3,1,2,0:T(8,128)(2,1)S(1)} all-to-all(bf16[8,64,1,1024]{3,1,2,0:T(8,128)(2,1)} %bitcast.241), channel_id=1, replica_groups=mesh['replica'=4,'inner'=8] {'inner'}, dimensions={0} | all-to-all | bytes 2097152 | tf_op jit(solution)/shard_map/all_to_all | solution.py:80
  802.8 28.7 %reduce-scatter.24.cloned.1.call-done = bf16[512,256]{1,0:T(8,128)(2,1)} async-done(((bf16[2048,256]{1,0:T(8,128)(2,1)}), bf16[512,256]{1,0:T(8,128)(2,1)}) %reduce-scatter.24.cloned.1.call-update) | async-done | bytes 262160 | tf_op jit(solution)/shard_map/reduce_scatter | solution.py:79
  831.4 14.3 %all_to_all.157 = bf16[8,64,1,256]{3,1,2,0:T(8,128)(2,1)S(1)} all-to-all(bf16[8,64,1,256]{3,1,2,0:T(8,128)(2,1)} %bitcast.262), channel_id=1, replica_groups=mesh['replica'=4,'inner'=8] {'inner'}, dimensions={0} | all-to-all | bytes 524288 | tf_op jit(solution)/shard_map/all_to_all | solution.py:80
  846.6 16.2 %reduce-scatter.22.cloned.1.call-done = bf16[512,256]{1,0:T(8,128)(2,1)} async-done(((bf16[2048,256]{1,0:T(8,128)(2,1)}), bf16[512,256]{1,0:T(8,128)(2,1)}) %reduce-scatter.22.cloned.1.call-update) | async-done | bytes 262160 | tf_op jit(solution)/shard_map/reduce_scatter | solution.py:79
  862.8 14.3 %all_to_all.158 = bf16[8,64,1,256]{3,1,2,0:T(8,128)(2,1)S(1)} all-to-all(bf16[8,64,1,256]{3,1,2,0:T(8,128)(2,1)} %bitcast.263), channel_id=1, replica_groups=mesh['replica'=4,'inner'=8] {'inner'}, dimensions={0} | all-to-all | bytes 524288 | tf_op jit(solution)/shard_map/all_to_all | solution.py:80
  877.9 15.9 %reduce-scatter.20.cloned.1.call-done = bf16[512,256]{1,0:T(8,128)(2,1)} async-done(((bf16[2048,256]{1,0:T(8,128)(2,1)}), bf16[512,256]{1,0:T(8,128)(2,1)}) %reduce-scatter.20.cloned.1.call-update) | async-done | bytes 262160 | tf_op jit(solution)/shard_map/reduce_scatter | solution.py:79
  893.8 14.3 %all_to_all.159 = bf16[8,64,1,256]{3,1,2,0:T(8,128)(2,1)S(1)} all-to-all(bf16[8,64,1,256]{3,1,2,0:T(8,128)(2,1)} %bitcast.264), channel_id=1, replica_groups=mesh['replica'=4,'inner'=8] {'inner'}, dimensions={0} | all-to-all | bytes 524288 | tf_op jit(solution)/shard_map/all_to_all | solution.py:80
  916.3 9.3 convolution_convert_fusion.4
  925.6 23.0 %all-gather.42.cloned.1.call-done = bf16[1024,2048]{1,0:T(8,128)(2,1)} async-done(((bf16[256,2048]{1,0:T(8,128)(2,1)}), bf16[1024,2048]{1,0:T(8,128)(2,1)}) %all-gather.42.cloned.1.call-update) | async-done | bytes 4194320 | tf_op jit(solution)/shard_map/all_gather | solution.py:87
  948.6 6.7 convert_element_type.224
  955.2 48.5 %all-gather.38.cloned.1.call-done = bf16[256,8192]{1,0:T(8,128)(2,1)} async-done(((bf16[64,8192]{1,0:T(8,128)(2,1)}), bf16[256,8192]{1,0:T(8,128)(2,1)}) %all-gather.38.cloned.1.call-update) | async-done | bytes 4194320 | tf_op jit(solution)/shard_map/all_gather | solution.py:82
  1003.7 6.6 convert_element_type.220
  1010.3 48.2 %all-gather.40.cloned.1.call-done = bf16[256,8192]{1,0:T(8,128)(2,1)} async-done(((bf16[64,8192]{1,0:T(8,128)(2,1)}), bf16[256,8192]{1,0:T(8,128)(2,1)}) %all-gather.40.cloned.1.call-update) | async-done | bytes 4194320 | tf_op jit(solution)/shard_map/all_gather | solution.py:82
  1058.5 6.6 convert_element_type.222
  1065.0 22.1 %all-gather.36.cloned.1.call-done = bf16[256,2048]{1,0:T(8,128)(2,1)} async-done(((bf16[64,2048]{1,0:T(8,128)(2,1)}), bf16[256,2048]{1,0:T(8,128)(2,1)}) %all-gather.36.cloned.1.call-update) | async-done | bytes 1048592 | tf_op jit(solution)/shard_map/all_gather | solution.py:87
  1089.9 26.4 %all-gather.34.cloned.1.call-done = bf16[256,2048]{1,0:T(8,128)(2,1)} async-done(((bf16[64,2048]{1,0:T(8,128)(2,1)}), bf16[256,2048]{1,0:T(8,128)(2,1)}) %all-gather.34.cloned.1.call-update) | async-done | bytes 1048592 | tf_op jit(solution)/shard_map/all_gather | solution.py:82
  1119.1 25.7 %all-gather.32.cloned.1.call-done = bf16[256,2048]{1,0:T(8,128)(2,1)} async-done(((bf16[64,2048]{1,0:T(8,128)(2,1)}), bf16[256,2048]{1,0:T(8,128)(2,1)}) %all-gather.32.cloned.1.call-update) | async-done | bytes 1048592 | tf_op jit(solution)/shard_map/all_gather | solution.py:82
  1147.6 26.4 %all-gather.30.cloned.1.call-done = bf16[256,2048]{1,0:T(8,128)(2,1)} async-done(((bf16[64,2048]{1,0:T(8,128)(2,1)}), bf16[256,2048]{1,0:T(8,128)(2,1)}) %all-gather.30.cloned.1.call-update) | async-done | bytes 1048592 | tf_op jit(solution)/shard_map/all_gather | solution.py:82
  1176.9 49.5 %reduce-scatter.18.cloned.1.call-done = bf16[128,2048]{1,0:T(8,128)(2,1)} async-done(((bf16[1024,2048]{1,0:T(8,128)(2,1)}), bf16[128,2048]{1,0:T(8,128)(2,1)}) %reduce-scatter.18.cloned.1.call-update) | async-done | bytes 524304 | tf_op jit(solution)/shard_map/reduce_scatter | solution.py:56
  1227.9 39.7 %psum.7 = f32[2,2048]{1,0:T(2,128)S(1)} all-reduce(f32[2,2048]{1,0:T(2,128)S(1)} %pad_maximum_fusion.6), channel_id=1, replica_groups=mesh['replica'=4,'inner'=8] {'replica','inner'}, use_global_device_ids=true, to_apply=%region_18.19 | all-reduce | flops 4096 | bytes 32768 | tf_op jit(solution)/shard_map/psum | solution.py:192
  1268.2 9.7 reduce-scatter.14.cloned.1.call-done
  (233 shorter events, 130.7 us)
Async XLA Ops:
  7.2 167.7 %copy-start = (bf16[256,2048]{1,0:T(8,128)(2,1)S(1)}, bf16[256,2048]{1,0:T(8,128)(2,1)}, u32[]{:S(2)}) copy-start(bf16[256,2048]{1,0:T(8,128)(2,1)} %param.17) | copy-start | bytes 3145732
  7.2 69.5 %all-gather.48.cloned.1.call-start = ((), (), s32[]{:S(2)}) async-start(), calls=%async_computation.45 | async-start | bytes 1310720 | tf_op jit(solution)/shard_map/all_gather | solution.py:68
  8.5 44.7 %copy-start.43 = (bf16[256]{0:T(256)(128)(2,1)S(1)}, bf16[256]{0:T(256)(128)(2,1)}, u32[]{:S(2)}) copy-start(bf16[256]{0:T(256)(128)(2,1)} %param.21) | copy-start | bytes 1540
  8.5 44.8 %copy-start.44 = (bf16[256]{0:T(256)(128)(2,1)S(1)}, bf16[256]{0:T(256)(128)(2,1)}, u32[]{:S(2)}) copy-start(bf16[256]{0:T(256)(128)(2,1)} %param.22) | copy-start | bytes 1540
  8.5 54.4 %copy-start.40 = (s32[128]{0:T(128)S(1)}, s32[128]{0:T(128)}, u32[]{:S(2)}) copy-start(s32[128]{0:T(128)} %param.24) | copy-start | bytes 1540
  8.5 54.4 %copy-start.41 = (s32[128]{0:T(128)S(1)}, s32[128]{0:T(128)}, u32[]{:S(2)}) copy-start(s32[128]{0:T(128)} %param.23) | copy-start | bytes 1540
  25.4 54.8 %all-gather.46.cloned.1.call-start = ((), (), s32[]{:S(2)}) async-start(), calls=%async_computation.44 | async-start | bytes 1310720 | tf_op jit(solution)/shard_map/all_gather | solution.py:68
  38.6 70.0 %all-gather.44.cloned.1.call-start = ((), (), s32[]{:S(2)}) async-start(), calls=%async_computation.43 | async-start | bytes 1310720 | tf_op jit(solution)/shard_map/all_gather | solution.py:68
  52.6 104.7 %all-gather.22.cloned.1.call-start = ((), (), s32[]{:S(2)}) async-start(), calls=%async_computation.21 | async-start | bytes 4718592 | tf_op jit(solution)/shard_map/all_gather | solution.py:52
  53.2 214.2 %reduce-scatter.12.cloned.1.call-start = ((), (), s32[]{:S(2)}) async-start(), calls=%async_computation.22 | async-start | bytes 4718592 | tf_op jit(solution)/shard_map/reduce_scatter | solution.py:56
  78.0 33.0 %copy-start.6 = (bf16[8,4,64,1,256]{4,2,1,0,3:T(8,128)(2,1)}, bf16[8,4,64,1,256]{4,2,1,0,3:T(8,128)(2,1)S(1)}, u32[]{:S(2)}) copy-start(bf16[8,4,64,1,256]{4,2,1,0,3:T(8,128)(2,1)S(1)} %copy.73) | copy-start | bytes 3145732
  81.4 79.1 %copy-start.8 = (bf16[8,4,64,1,256]{4,2,1,0,3:T(8,128)(2,1)}, bf16[8,4,64,1,256]{4,2,1,0,3:T(8,128)(2,1)S(1)}, u32[]{:S(2)}) copy-start(bf16[8,4,64,1,256]{4,2,1,0,3:T(8,128)(2,1)S(1)} %copy.68) | copy-start | bytes 3145732
  168.0 5.4 copy-start.1
  169.5 5.4 copy-start.24
  178.2 146.4 %all-gather.52.cloned.1.call-start = ((), (), s32[]{:S(2)}) async-start(), calls=%async_computation.47 | async-start | bytes 5242880 | tf_op jit(solution)/shard_map/all_gather | solution.py:68
  228.7 38.6 %copy-start.4 = (bf16[128,2048]{1,0:T(8,128)(2,1)S(1)}, bf16[128,2048]{1,0:T(8,128)(2,1)}, u32[]{:S(2)}) copy-start(bf16[128,2048]{1,0:T(8,128)(2,1)} %param.13) | copy-start | bytes 1572868
  228.7 150.5 %all-gather.50.cloned.1.call-start = ((), (), s32[]{:S(2)}) async-start(), calls=%async_computation.46 | async-start | bytes 5242880 | tf_op jit(solution)/shard_map/all_gather | solution.py:68
  267.3 161.3 %all-gather.24.cloned.1.call-start = ((), (), s32[]{:S(2)}) async-start(), calls=%async_computation.23 | async-start | bytes 4718592 | tf_op jit(solution)/shard_map/all_gather | solution.py:52
  270.7 205.4 %all-gather.26.cloned.1.call-start = ((), (), s32[]{:S(2)}) async-start(), calls=%async_computation.25 | async-start | bytes 4718592 | tf_op jit(solution)/shard_map/all_gather | solution.py:52
  271.5 282.5 %reduce-scatter.16.cloned.1.call-start = ((), (), s32[]{:S(2)}) async-start(), calls=%async_computation.26 | async-start | bytes 4718592 | tf_op jit(solution)/shard_map/reduce_scatter | solution.py:56
  428.6 10.1 copy-start.19
  428.6 10.1 copy-start.42
  476.1 14.7 %copy-start.20 = (bf16[8,4,64,1,1024]{4,2,1,0,3:T(8,128)(2,1)S(1)}, bf16[8,4,64,1,1024]{4,2,1,0,3:T(8,128)(2,1)}, u32[]{:S(2)}) copy-start(bf16[8,4,64,1,1024]{4,2,1,0,3:T(8,128)(2,1)} %copy.79) | copy-start | bytes 12582916
  490.8 6.3 copy-start.18
  505.0 48.9 %copy-start.5 = (bf16[128,2048]{1,0:T(8,128)(2,1)S(1)}, bf16[128,2048]{1,0:T(8,128)(2,1)}, u32[]{:S(2)}) copy-start(bf16[128,2048]{1,0:T(8,128)(2,1)} %reduce-scatter.12.cloned.1.call-done) | copy-start | bytes 1572868
  505.0 50.5 %copy-start.11 = (bf16[128,2048]{1,0:T(8,128)(2,1)S(1)}, bf16[128,2048]{1,0:T(8,128)(2,1)}, u32[]{:S(2)}) copy-start(bf16[128,2048]{1,0:T(8,128)(2,1)} %param.25) | copy-start | bytes 1572868
  505.1 98.2 %all-gather.28.cloned.1.call-start = ((), (), s32[]{:S(2)}) async-start(), calls=%async_computation.27 | async-start | bytes 4718592 | tf_op jit(solution)/shard_map/all_gather | solution.py:52
  557.8 99.7 %reduce-scatter.32.cloned.1.call-start = ((), (), s32[]{:S(2)}) async-start(), calls=%async_computation.41 | async-start | bytes 5242880 | tf_op jit(solution)/shard_map/reduce_scatter | solution.py:86
  567.3 146.7 %reduce-scatter.28.cloned.1.call-start = ((), (), s32[]{:S(2)}) async-start(), calls=%async_computation.37 | async-start | bytes 5242880 | tf_op jit(solution)/shard_map/reduce_scatter | solution.py:79
  577.5 192.1 %reduce-scatter.30.cloned.1.call-start = ((), (), s32[]{:S(2)}) async-start(), calls=%async_computation.39 | async-start | bytes 5242880 | tf_op jit(solution)/shard_map/reduce_scatter | solution.py:79
  587.6 214.4 %reduce-scatter.26.cloned.1.call-start = ((), (), s32[]{:S(2)}) async-start(), calls=%async_computation.35 | async-start | bytes 1310720 | tf_op jit(solution)/shard_map/reduce_scatter | solution.py:86
  607.7 223.7 %reduce-scatter.24.cloned.1.call-start = ((), (), s32[]{:S(2)}) async-start(), calls=%async_computation.33 | async-start | bytes 1310720 | tf_op jit(solution)/shard_map/reduce_scatter | solution.py:79
  619.8 6.7 copy-start.34
  619.8 6.7 copy-start.36
  619.8 243.0 %reduce-scatter.22.cloned.1.call-start = ((), (), s32[]{:S(2)}) async-start(), calls=%async_computation.31 | async-start | bytes 1310720 | tf_op jit(solution)/shard_map/reduce_scatter | solution.py:79
  633.6 260.3 %reduce-scatter.20.cloned.1.call-start = ((), (), s32[]{:S(2)}) async-start(), calls=%async_computation.29 | async-start | bytes 1310720 | tf_op jit(solution)/shard_map/reduce_scatter | solution.py:79
  638.9 309.7 %all-gather.42.cloned.1.call-start = ((), (), s32[]{:S(2)}) async-start(), calls=%async_computation.42 | async-start | bytes 5242880 | tf_op jit(solution)/shard_map/all_gather | solution.py:87
  657.6 346.2 %all-gather.38.cloned.1.call-start = ((), (), s32[]{:S(2)}) async-start(), calls=%async_computation.38 | async-start | bytes 5242880 | tf_op jit(solution)/shard_map/all_gather | solution.py:82
  746.4 312.1 %all-gather.40.cloned.1.call-start = ((), (), s32[]{:S(2)}) async-start(), calls=%async_computation.40 | async-start | bytes 5242880 | tf_op jit(solution)/shard_map/all_gather | solution.py:82
  800.8 108.2 %copy-start.7 = (bf16[8,4,64,1,256]{4,2,1,0,3:T(8,128)(2,1)S(1)}, bf16[8,4,64,1,256]{4,2,1,0,3:T(8,128)(2,1)}, u32[]{:S(2)}) copy-start(bf16[8,4,64,1,256]{4,2,1,0,3:T(8,128)(2,1)} %copy-done.6) | copy-start | bytes 3145732
  802.0 285.2 %all-gather.36.cloned.1.call-start = ((), (), s32[]{:S(2)}) async-start(), calls=%async_computation.36 | async-start | bytes 1310720 | tf_op jit(solution)/shard_map/all_gather | solution.py:87
  802.7 313.6 %all-gather.34.cloned.1.call-start = ((), (), s32[]{:S(2)}) async-start(), calls=%async_computation.34 | async-start | bytes 1310720 | tf_op jit(solution)/shard_map/all_gather | solution.py:82
  846.5 298.3 %all-gather.32.cloned.1.call-start = ((), (), s32[]{:S(2)}) async-start(), calls=%async_computation.32 | async-start | bytes 1310720 | tf_op jit(solution)/shard_map/all_gather | solution.py:82
  877.9 296.2 %all-gather.30.cloned.1.call-start = ((), (), s32[]{:S(2)}) async-start(), calls=%async_computation.30 | async-start | bytes 1310720 | tf_op jit(solution)/shard_map/all_gather | solution.py:82
  908.9 317.4 %reduce-scatter.18.cloned.1.call-start = ((), (), s32[]{:S(2)}) async-start(), calls=%async_computation.28 | async-start | bytes 4718592 | tf_op jit(solution)/shard_map/reduce_scatter | solution.py:56
  916.2 361.6 %reduce-scatter.14.cloned.1.call-start = ((), (), s32[]{:S(2)}) async-start(), calls=%async_computation.24 | async-start | bytes 4718592 | tf_op jit(solution)/shard_map/reduce_scatter | solution.py:56
  1119.1 158.7 %copy-start.10 = (bf16[128,2048]{1,0:T(8,128)(2,1)S(1)}, bf16[128,2048]{1,0:T(8,128)(2,1)}, u32[]{:S(2)}) copy-start(bf16[128,2048]{1,0:T(8,128)(2,1)} %reduce-scatter.16.cloned.1.call-done) | copy-start | bytes 1572868
  1119.1 158.7 %copy-start.12 = (bf16[128,2048]{1,0:T(8,128)(2,1)S(1)}, bf16[128,2048]{1,0:T(8,128)(2,1)}, u32[]{:S(2)}) copy-start(bf16[128,2048]{1,0:T(8,128)(2,1)} %param.25) | copy-start | bytes 1572868
  (24 other events, 65.3 us)
Sparse Core Ops, SparseCore 0:
  25.5 25.5 all-gather.47
  53.5 26.6 all-gather.45
  82.0 26.6 all-gather.43
  110.1 47.1 all-gather.21
  178.3 78.1 reduce-scatter.11
  258.2 66.3 all-gather.51
  326.5 52.6 all-gather.49
  381.4 47.1 all-gather.23
  430.2 45.8 all-gather.25
  505.2 48.7 reduce-scatter.15
  557.9 45.2 all-gather.27
  606.1 51.4 reduce-scatter.31
  661.4 52.6 reduce-scatter.27
  716.9 52.6 reduce-scatter.29
  772.6 27.6 reduce-scatter.25
  803.7 27.7 reduce-scatter.23
  835.0 27.7 reduce-scatter.21
  866.1 27.7 reduce-scatter.19
  895.8 52.7 all-gather.41
  951.0 52.6 all-gather.37
  1005.7 52.6 all-gather.39
  1060.5 26.6 all-gather.35
  1089.7 26.6 all-gather.33
  1118.2 26.6 all-gather.31
  1147.4 26.6 all-gather.29
  1176.3 49.9 reduce-scatter.17
  1228.6 49.2 reduce-scatter.13

commit v2 on v1

v2 whole, which is shorter than its diff:
```python
import functools
import math

import jax
import jax.numpy as jnp
from jax import lax
from jax.experimental import pallas as pl
from jax.experimental.pallas import tpu as pltpu
from jax.sharding import PartitionSpec as P

HEAD_DIM = 128
PIECE = 256
epsilon = 1e-06
rope_base = 10000.0
dims_rows = (((1,), (1,)), ((), ()))
dims_cols = (((0,), (0,)), ((), ()))
f32 = jnp.float32
bf16 = jnp.bfloat16


def dot(a, b):
    return jnp.dot(a, b, preferred_element_type=f32)


def dot_t(a, b):
    return lax.dot_general(a, b, dims_rows, preferred_element_type=f32)


def t_dot(a, b):
    return lax.dot_general(a, b, dims_cols, preferred_element_type=f32)


def rope_tables(positions):
    half_dim = HEAD_DIM // 2
    frequency = rope_base ** (-jnp.arange(half_dim, dtype=f32) * 2.0 / HEAD_DIM)
    angle = positions.astype(f32)[:, None] * frequency[None, :]
    cosine, sine = jnp.cos(angle), jnp.sin(angle)
    return jnp.concatenate([cosine, cosine], axis=1), jnp.concatenate([-sine, sine], axis=1)


def rms_scale(values):
    return lax.rsqrt(jnp.mean(values * values, axis=1, keepdims=True) + epsilon)


def rcopy(src, dst, ssem, rsem, to):
    return pltpu.make_async_remote_copy(
        src_ref=src,
        dst_ref=dst,
        send_sem=ssem,
        recv_sem=rsem,
        device_id={"inner": to},
        device_id_type=pl.DeviceIdType.MESH,
    )


def signal(sem, to):
    pl.semaphore_signal(sem, inc=1, device_id={"inner": to}, device_id_type=pl.DeviceIdType.MESH)


def line_body(n, n_ag, n_rs, a2a_blocks, parts, *refs):
    refs = list(refs)
    nz = n // 2
    n_a2a = len(a2a_blocks)
    take = lambda count: [refs.pop(0) for _ in range(count)]
    ag_in, rs_in, a2a_in = take(n_ag), take(n_rs), [take(t[0]) for t in a2a_blocks]
    ag_out, rs_out, a2a_out = take(n_ag), take(n_rs), take(n_a2a)
    ag_sem = [take(7) for _ in range(n_ag)]
    rs_scr = [take(9) for _ in range(n_rs)]
    a2a_sem = [take(3) for _ in range(n_a2a)]
    me = lax.axis_index("inner")
    z, c = me // 2, lax.rem(me, 2)
    sib = me + 1 - 2 * c
    barrier = pltpu.get_barrier_semaphore()
    if n_a2a:
        for k in range(1, n):
            signal(barrier, lax.rem(me + k, n))
        pl.semaphore_wait(barrier, n - 1)
    else:
        signal(barrier, sib)

        @pl.when(z + 1 < nz)
        def _():
            signal(barrier, me + 2)

        @pl.when(z > 0)
        def _():
            signal(barrier, me - 2)

        pl.semaphore_wait(barrier, 1 + (z + nz - 1) // nz + (2 * nz - 2 - z) // nz)

    def rows_of(ref, j):
        count = ref.shape[0] // parts
        return pl.ds(pl.multiple_of(j * count, count), count)

    class Gather:
        def __init__(self, x, out, sems):
            self.x, self.out = x, out
            self.own_sem, self.rs, self.rr, self.ls, self.lr, self.ss, self.sr = sems

        def own(self):
            return pltpu.make_async_copy(self.x, self.out.at[me], self.own_sem)

        def piece(self, block, s, j):
            rows = rows_of(self.x, j)
            return self.x.at[rows] if s == 0 else self.out.at[block, rows]

        def right(self, s, j):
            b = me - 2 * s
            dst = self.out.at[b, rows_of(self.x, j)]
            return rcopy(self.piece(b, s, j), dst, self.rs.at[s, j], self.rr.at[s + 1, j], me + 2)

        def left(self, s, j):
            b = me + 2 * s
            dst = self.out.at[b, rows_of(self.x, j)]
            return rcopy(self.piece(b, s, j), dst, self.ls.at[s, j], self.lr.at[s + 1, j], me - 2)

        def side(self, s, k, j):
            b = me - 2 * s if k == 0 else me + 2 * s
            dst = self.out.at[b, rows_of(self.x, j)]
            return rcopy(self.piece(b, s, j), dst, self.ss.at[k, s, j], self.sr.at[k, s, j], sib)

        def from_left(self, s, j):
            dst = self.out.at[me - 2 * s, rows_of(self.x, j)]
            return rcopy(dst, dst, self.rs.at[s, j], self.rr.at[s, j], me - 2)

        def from_right(self, s, j):
            dst = self.out.at[me + 2 * s, rows_of(self.x, j)]
            return rcopy(dst, dst, self.ls.at[s, j], self.lr.at[s, j], me + 2)

        def from_side(self, s, k, j):
            b = sib - 2 * s if k == 0 else sib + 2 * s
            dst = self.out.at[b, rows_of(self.x, j)]
            return rcopy(dst, dst, self.ss.at[k, s, j], self.sr.at[k, s, j], sib)

        def begin(self):
            @pl.loop(0, parts)
            def _(j):
                @pl.when(z + 1 < nz)
                def _():
                    self.right(0, j).start()

                @pl.when(z > 0)
                def _():
                    self.left(0, j).start()

            self.own().start()

            @pl.loop(0, parts)
            def _(j):
                self.side(0, 0, j).start()

        def step(self, s, j):
            @pl.when(z >= s)
            def _():
                self.from_left(s, j).wait_recv()

                @pl.when(z + 1 < nz)
                def _():
                    self.right(s, j).start()

                self.side(s, 0, j).start()

            @pl.when(z + s < nz)
            def _():
                self.from_right(s, j).wait_recv()

                @pl.when(z > 0)
                def _():
                    self.left(s, j).start()

                self.side(s, 1, j).start()

        def end(self):
            self.own().wait()
            for s in range(nz):
                @pl.loop(0, parts)
                def _(j):
                    @pl.when(z >= s)
                    def _():
                        @pl.when(z + 1 < nz)
                        def _():
                            self.right(s, j).wait_send()

                        self.side(s, 0, j).wait_send()
                        self.from_side(s, 0, j).wait_recv()

                    @pl.when(z + s < nz)
                    def _():
                        @pl.when(z > 0)
                        def _():
                            self.left(s, j).wait_send()

                        if s > 0:
                            self.side(s, 1, j).wait_send()
                            self.from_side(s, 1, j).wait_recv()

    class Scatter:
        def __init__(self, p, out, scratch):
            self.p, self.out = p, out
            self.sib_buf, self.l_buf, self.r_buf, self.ss, self.sr, self.rs, self.rr, self.ls, self.lr = scratch
            self.count = out.shape[0] // parts

        def side(self, d, j):
            rows = rows_of(self.out, j)
            return rcopy(self.p.at[2 * d + 1 - c, rows], self.sib_buf.at[d, rows], self.ss.at[d, j], self.sr.at[d, j], sib)

        def right(self, d, j, to=2):
            rows = rows_of(self.out, j)
            return rcopy(self.l_buf.at[d, rows], self.l_buf.at[d, rows], self.rs.at[d, j], self.rr.at[d, j], me + to)

        def left(self, d, j, to=-2):
            rows = rows_of(self.out, j)
            return rcopy(self.r_buf.at[d, rows], self.r_buf.at[d, rows], self.ls.at[d, j], self.lr.at[d, j], me + to)

        def begin(self):
            for s in range(nz // 2):
                for d in (nz - 1 - s, s):
                    @pl.loop(0, parts)
                    def _(j):
                        self.side(d, j).start()

        def pair(self, d, rows):
            return self.p[2 * d + c, rows, :].astype(f32) + self.sib_buf[d, rows, :].astype(f32)

        def step(self, s, j):
            rows = rows_of(self.out, j)
            d = nz - s

            @pl.when(d > z)
            def _():
                self.side(d, j).wait_recv()

                @pl.when(z > 0)
                def _():
                    self.right(d, j, -2).wait_recv()
                    self.l_buf[d, rows, :] = (self.pair(d, rows) + self.l_buf[d, rows, :].astype(f32)).astype(bf16)

                @pl.when(z == 0)
                def _():
                    self.l_buf[d, rows, :] = self.pair(d, rows).astype(bf16)

                self.right(d, j).start()

            e = s - 1

            @pl.when(e < z)
            def _():
                self.side(e, j).wait_recv()

                @pl.when(z + 1 < nz)
                def _():
                    self.left(e, j, 2).wait_recv()
                    self.r_buf[e, rows, :] = (self.pair(e, rows) + self.r_buf[e, rows, :].astype(f32)).astype(bf16)

                @pl.when(z + 1 == nz)
                def _():
                    self.r_buf[e, rows, :] = self.pair(e, rows).astype(bf16)

                self.left(e, j).start()

        def end(self):
            @pl.loop(0, parts)
            def _(j):
                rows = rows_of(self.out, j)
                self.side(z, j).wait_recv()
                self.out[rows, :] = self.pair(z, rows)

                @pl.when(z > 0)
                def _():
                    self.right(z, j, -2).wait_recv()
                    self.out[rows, :] = self.out[rows, :] + self.l_buf[z, rows, :].astype(f32)

                @pl.when(z + 1 < nz)
                def _():
                    self.left(z, j, 2).wait_recv()
                    self.out[rows, :] = self.out[rows, :] + self.r_buf[z, rows, :].astype(f32)

            for d in range(nz):
                @pl.loop(0, parts)
                def _(j):
                    self.side(d, j).wait_send()

                    @pl.when(d > z)
                    def _():
                        self.right(d, j).wait_send()

                    @pl.when(d < z)
                    def _():
                        self.left(d, j).wait_send()

    class Exchange:
        def __init__(self, src, dst, sems, blocks):
            self.src, self.dst = src, dst
            self.own_sem, self.send, self.recv = sems
            _, self.src_of, self.dst_of, self.count = blocks

        def to(self, k, m):
            other = lax.rem(me + k, n)
            return rcopy(
                self.src_of(self.src, other, m), self.dst_of(self.dst, me, m), self.send.at[k, m], self.recv.at[k, m], other
            )

        def came(self, k, m):
            other = lax.rem(me - k + n, n)
            return rcopy(
                self.src_of(self.src, other, m), self.dst_of(self.dst, other, m), self.send.at[k, m], self.recv.at[k, m], other
            )

        def own(self, m):
            return pltpu.make_async_copy(
                self.src_of(self.src, me, m), self.dst_of(self.dst, me, m), self.own_sem.at[m]
            )

        def begin(self):
            for k in range(1, n):
                for m in range(self.count):
                    self.to(k, m).start()
            for m in range(self.count):
                self.own(m).start()

        def step(self, s, j):
            pass

        def end(self):
            for m in range(self.count):
                self.own(m).wait()
            for k in range(1, n):
                for m in range(self.count):
                    self.came(k, m).wait_recv()
                    self.to(k, m).wait_send()

    parts_of = [Gather(*t) for t in zip(ag_in, ag_out, ag_sem)]
    parts_of += [Scatter(*t) for t in zip(rs_in, rs_out, rs_scr)]
    parts_of += [Exchange(*t) for t in zip(a2a_in, a2a_out, a2a_sem, a2a_blocks)]
    for part in parts_of:
        part.begin()
    if n_ag + n_rs:
        for s in range(1, nz):
            @pl.loop(0, parts)
            def _(j):
                for part in parts_of:
                    part.step(s, j)
    for part in parts_of:
        part.end()


def line_comm(cid, name, ag=(), rs=(), a2a=(), parts=2):
    n = lax.axis_size("inner")
    nz = n // 2
    dma = pltpu.SemaphoreType.DMA
    hbm = pl.BlockSpec(memory_space=pl.ANY)
    vmem = pl.BlockSpec(memory_space=pltpu.VMEM)
    rs = [p.reshape((n, p.shape[0] // n) + p.shape[1:]) for p in rs]
    out_shape = [jax.ShapeDtypeStruct((n,) + x.shape, x.dtype) for x in ag]
    out_shape += [jax.ShapeDtypeStruct(p.shape[1:], f32) for p in rs]
    out_shape += [jax.ShapeDtypeStruct(t[1], t[0][0].dtype) for t in a2a]
    scratch = []
    for _ in ag:
        scratch += [dma, dma((nz, parts)), dma((nz + 1, parts)), dma((nz, parts)), dma((nz + 1, parts))]
        scratch += [dma((2, nz, parts)), dma((2, nz, parts))]
    for p in rs:
        scratch += [pltpu.VMEM((nz,) + p.shape[1:], bf16)] * 3 + [dma((nz, parts))] * 6
    for t in a2a:
        scratch += [dma((t[4],)), dma((n, t[4])), dma((n, t[4]))]
    outs = pl.pallas_call(
        functools.partial(line_body, n, len(ag), len(rs), [(len(t[0]),) + t[2:5] for t in a2a], parts),
        out_shape=out_shape,
        in_specs=[hbm] * len(ag) + [vmem] * len(rs) + [hbm] * sum(len(t[0]) for t in a2a),
        out_specs=[hbm] * len(ag) + [vmem] * len(rs) + [hbm] * len(a2a),
        scratch_shapes=scratch,
        compiler_params=pltpu.CompilerParams(
            collective_id=cid, has_side_effects=True, vmem_limit_bytes=48 * 2**20
        ),
        name=name,
    )(*ag, *rs, *[w for t in a2a for w in t[0]])
    outs = [o.reshape((-1,) + o.shape[2:]) if i < len(ag) else o for i, o in enumerate(outs)]
    return outs


def rotate(flat, cosine, sine):
    return flat * cosine + pltpu.roll(flat, HEAD_DIM // 2, 1) * sine


def squash(q, k, piece, keys, length):
    scale = -math.log2(math.e) / math.sqrt(HEAD_DIM)
    sg = 1.0 / (1.0 + jnp.exp2(dot_t(q, k) * scale + math.log2(length)))
    row = lax.broadcasted_iota(jnp.int32, (PIECE, PIECE), 0)
    col = lax.broadcasted_iota(jnp.int32, (PIECE, PIECE), 1)
    return sg, (col <= row) | (piece >= 0)


def masked(value, visible, keys):
    last = jnp.where(visible, value[:, keys - PIECE :], 0.0)
    return last if keys == PIECE else jnp.concatenate([value[:, : keys - PIECE], last], axis=1)


def attn_body(heads, length, lin, cosine, sine, piece, out, rot):
    h, b = pl.program_id(0), pl.program_id(1)
    at = lambda part: pl.ds(pl.multiple_of((part * heads + h) * HEAD_DIM, HEAD_DIM), HEAD_DIM)
    blocks = length // PIECE

    @pl.when(b == 0)
    def _():
        @pl.loop(0, blocks)
        def _(i):
            rows = pl.ds(pl.multiple_of(i * PIECE, PIECE), PIECE)
            for part in (0, 1):
                rot[rows, at(part)] = rotate(lin[rows, at(part)], cosine[rows, :], sine[rows, :]).astype(bf16)
            rot[rows, at(2)] = lin[rows, at(2)].astype(bf16)

    for i in range(blocks):
        @pl.when(b == i)
        def _():
            keys = (i + 1) * PIECE
            own = pl.ds(i * PIECE, PIECE)
            sg, visible = squash(rot[own, at(0)], rot[0:keys, at(1)], piece[...], keys, length)
            out[...] = dot(masked(sg, visible, keys).astype(bf16), rot[0:keys, at(2)]).astype(bf16)


def attention(lin, cosine, sine, piece):
    length, width = lin.shape
    heads = width // 3 // HEAD_DIM
    whole = lambda x: pl.BlockSpec(x.shape, lambda h, b: (0, 0))
    return pl.pallas_call(
        functools.partial(attn_body, heads, length),
        grid=(heads, length // PIECE),
        out_shape=[
            jax.ShapeDtypeStruct((length, width // 3), bf16),
            jax.ShapeDtypeStruct((length, width), bf16),
        ],
        in_specs=[whole(lin), whole(cosine), whole(sine), pl.BlockSpec((PIECE, 1), lambda h, b: (b, 0))],
        out_specs=[
            pl.BlockSpec((PIECE, HEAD_DIM), lambda h, b: (b, h)),
            pl.BlockSpec((length, width), lambda h, b: (0, 0)),
        ],
        compiler_params=pltpu.CompilerParams(vmem_limit_bytes=48 * 2**20),
        cost_estimate=pl.CostEstimate(
            flops=4 * heads * length * length * HEAD_DIM // 2, bytes_accessed=8 * length * width, transcendentals=heads * length * length
        ),
        name="attention",
    )(lin, cosine, sine, piece)


def attn_back_body(heads, length, rot, go, cosine, sine, piece, out, gk, gv):
    h, b = pl.program_id(0), pl.program_id(1)
    at = lambda part: pl.ds(pl.multiple_of((part * heads + h) * HEAD_DIM, HEAD_DIM), HEAD_DIM)
    blocks = length // PIECE
    inv_root = 1.0 / math.sqrt(HEAD_DIM)

    @pl.when(b == 0)
    def _():
        gk[...] = jnp.zeros_like(gk)
        gv[...] = jnp.zeros_like(gv)

    for i in range(blocks):
        @pl.when(b == i)
        def _():
            keys = (i + 1) * PIECE
            own = pl.ds(i * PIECE, PIECE)
            q, g = rot[own, at(0)], go[...]
            sg, visible = squash(q, rot[0:keys, at(1)], piece[...], keys, length)
            p = masked(sg, visible, keys).astype(bf16)
            gs = masked(dot_t(g, rot[0:keys, at(2)]) * sg * (1.0 - sg), visible, keys).astype(bf16)
            gq = dot(gs, rot[0:keys, at(1)]) * inv_root
            out[own, at(0)] = rotate(gq, cosine[own, :], -sine[own, :]).astype(bf16)
            gk[0:keys, :] += t_dot(gs, q)
            gv[0:keys, :] += t_dot(p, g)

    @pl.when(b == blocks - 1)
    def _():
        @pl.loop(0, blocks)
        def _(i):
            rows = pl.ds(pl.multiple_of(i * PIECE, PIECE), PIECE)
            out[rows, at(1)] = rotate(gk[rows, :] * inv_root, cosine[rows, :], -sine[rows, :]).astype(bf16)
            out[rows, at(2)] = gv[rows, :].astype(bf16)


def attention_back(rot, go, cosine, sine, piece):
    length, width = rot.shape
    heads = width // 3 // HEAD_DIM
    whole = lambda x: pl.BlockSpec(x.shape, lambda h, b: (0, 0))
    return pl.pallas_call(
        functools.partial(attn_back_body, heads, length),
        grid=(heads, length // PIECE),
        out_shape=jax.ShapeDtypeStruct((length, width), bf16),
        in_specs=[
            whole(rot),
            pl.BlockSpec((PIECE, HEAD_DIM), lambda h, b: (b, h)),
            whole(cosine),
            whole(sine),
            pl.BlockSpec((PIECE, 1), lambda h, b: (b, 0)),
        ],
        out_specs=pl.BlockSpec((length, width), lambda h, b: (0, 0)),
        scratch_shapes=[pltpu.VMEM((length, HEAD_DIM), f32)] * 2,
        compiler_params=pltpu.CompilerParams(vmem_limit_bytes=48 * 2**20),
        cost_estimate=pl.CostEstimate(
            flops=10 * heads * length * length * HEAD_DIM // 2, bytes_accessed=8 * length * width, transcendentals=heads * length * length
        ),
        name="attention_back",
    )(rot, go, cosine, sine, piece)


def gain_body(n, nr, g, out, group, copies, ss, sr, cs, cr):
    me, r = lax.axis_index("inner"), lax.axis_index("replica")
    mesh_id = pl.DeviceIdType.MESH
    barrier = pltpu.get_barrier_semaphore()
    for k in range(1, n):
        signal(barrier, lax.rem(me + k, n))
    for k in range(1, nr):
        pl.semaphore_signal(barrier, inc=1, device_id={"replica": lax.rem(r + k, nr)}, device_id_type=mesh_id)
    pl.semaphore_wait(barrier, n + nr - 2)

    def inside(k):
        to = lax.rem(me + k, n)
        return rcopy(g.at[to], group.at[k], ss.at[k], sr.at[k], to)

    def across(k):
        return pltpu.make_async_remote_copy(
            src_ref=copies.at[0],
            dst_ref=copies.at[k],
            send_sem=cs.at[k],
            recv_sem=cr.at[k],
            device_id={"replica": lax.rem(r + k, nr)},
            device_id_type=mesh_id,
        )

    for k in range(1, n):
        inside(k).start()
    total = g[me]
    for k in range(1, n):
        inside(k).wait_recv()
        total = total + group[k]
    copies[0] = total
    for k in range(1, nr):
        across(k).start()
    for k in range(1, nr):
        across(k).wait_recv()
        total = total + copies[k]
    out[...] = total
    for k in range(1, n):
        inside(k).wait_send()
    for k in range(1, nr):
        across(k).wait_send()


def gain_sum(cid, parts):
    n, nr = lax.axis_size("inner"), lax.axis_size("replica")
    cols = parts.shape[1] // n
    g = jnp.zeros((n, 8, cols), f32).at[:, :2].set(parts.reshape(2, n, cols).transpose(1, 0, 2))
    dma = pltpu.SemaphoreType.DMA
    vmem = pl.BlockSpec(memory_space=pltpu.VMEM)
    return pl.pallas_call(
        functools.partial(gain_body, n, nr),
        out_shape=jax.ShapeDtypeStruct((8, cols), f32),
        in_specs=[vmem],
        out_specs=vmem,
        scratch_shapes=[
            pltpu.VMEM((n, 8, cols), f32),
            pltpu.VMEM((nr, 8, cols), f32),
            dma((n,)),
            dma((n,)),
            dma((nr,)),
            dma((nr,)),
        ],
        compiler_params=pltpu.CompilerParams(collective_id=cid, has_side_effects=True),
        name="gain_sum",
    )(g)[:2]


def columns_out(weights):
    n, nr = lax.axis_size("inner"), lax.axis_size("replica")
    part = weights[0].shape[0] // nr
    cols = weights[0].shape[1] // n

    def source(refs, other, m):
        rows = pl.ds(pl.multiple_of(lax.axis_index("replica") * part, part), part)
        return refs[m].at[rows, pl.ds(pl.multiple_of(other * cols, cols), cols)]

    def target(ref, other, m):
        return ref.at[other, :, pl.ds(m * cols, cols)]

    return (tuple(weights), (n, part, cols * len(weights)), source, target, len(weights))


def to_all(block):
    n = lax.axis_size("inner")
    return ((block,), (n,) + block.shape, lambda refs, other, m: refs[0], lambda ref, other, m: ref.at[other], 1)


def rows_back(share, count):
    n, part, width = share.shape
    cols = width // count

    def source(refs, other, m):
        return refs[0].at[other, :, pl.ds(m * cols, cols)]

    def target(ref, other, m):
        return ref.at[m, :, pl.ds(pl.multiple_of(other * cols, cols), cols)]

    return ((share,), (count, part, n * cols), source, target, count)


def all_copies(block):
    n, part, cols = block.shape
    full = lax.all_gather(block, "replica", axis=0, tiled=False)
    return full.transpose(1, 0, 2, 3).reshape(-1, cols)


def sum_parts(products):
    n, nr = lax.axis_size("inner"), lax.axis_size("replica")
    g = jnp.concatenate([p.astype(bf16) for p in products], axis=1)
    part = g.shape[0] // n // nr
    g = g.reshape(n, nr, part, -1).transpose(1, 0, 2, 3).reshape(nr * n * part, -1)
    return lax.psum_scatter(g, "replica", scatter_dimension=0, tiled=True).reshape(n, part, -1)


def join(block, axis):
    return lax.all_gather(block, "replica", axis=axis, tiled=False)


def local(
    tokens,
    w_query,
    w_key,
    w_value,
    w_out,
    w_gate,
    w_up,
    w_down,
    gain_attn,
    gain_ffn,
    pieces,
    positions,
    cotangent,
):
    n = lax.axis_size("inner")
    nr = lax.axis_size("replica")
    own, width = tokens.shape
    length = own * n
    rows = gain_attn.shape[0]

    marks = jnp.zeros((8, own), jnp.int32).at[0].set(pieces).at[1].set(positions)
    gains = jnp.zeros((8, rows), f32).at[0].set(gain_attn.astype(f32)).at[1].set(gain_ffn.astype(f32))
    qkv_share, marks, gains = line_comm(
        0, "load_attn", a2a=[columns_out([w_query, w_key, w_value]), to_all(marks), to_all(gains)]
    )
    w_qkv = all_copies(qkv_share)
    x, gu_share = line_comm(1, "load_ffn", ag=[tokens], a2a=[columns_out([w_gate, w_up])])
    w_gu = all_copies(gu_share)
    w_g, w_u = w_gu[:, : w_gu.shape[1] // 2], w_gu[:, w_gu.shape[1] // 2 :]
    pieces, positions = marks[:, 0].reshape(length, 1), marks[:, 1].reshape(length)
    attn_gain, ffn_gain = gains[:, 0].reshape(-1), gains[:, 1].reshape(-1)

    x = x.astype(f32)
    cosine, sine = rope_tables(positions)
    u1 = x * rms_scale(x)
    n1 = (u1 * attn_gain).astype(bf16)
    o, rot = attention(dot(n1, w_qkv), cosine, sine, pieces)
    cot, a = line_comm(2, "attn_out", ag=[cotangent], rs=[dot(o, w_out).astype(bf16)])
    mid = tokens.astype(f32) + a
    r2 = rms_scale(mid)
    u2 = mid * r2
    (n2,) = line_comm(3, "gather_n2", ag=[(u2 * ffn_gain).astype(bf16)])

    gate = dot(n2, w_g)
    up = dot(n2, w_u)
    s = jax.nn.sigmoid(gate)
    silu = gate * s
    hid = (silu * up).astype(bf16)
    down_share = lax.psum_scatter(t_dot(hid, cot).astype(bf16), "replica", scatter_dimension=0, tiled=True)
    ghid = dot_t(cot, w_down)
    ggate = (ghid * up * s * (1.0 + gate * (1.0 - s))).astype(bf16)
    gup = (ghid * silu).astype(bf16)
    gu_share = sum_parts([t_dot(n2, ggate), t_dot(n2, gup)])
    (gn2,) = line_comm(4, "scatter_gn2", rs=[(dot_t(ggate, w_g) + dot_t(gup, w_u)).astype(bf16)])
    gu2 = gn2 * ffn_gain
    ffn_gain_part = jnp.sum(gn2 * u2, axis=0)
    gmid = cotangent.astype(f32) + r2 * (gu2 - u2 * jnp.mean(gu2 * u2, axis=1, keepdims=True))
    ga, mlp = line_comm(5, "gather_ga", ag=[gmid.astype(bf16)], rs=[dot(hid, w_down).astype(bf16)])
    output = (mid + mlp).astype(bf16)

    go = dot_t(ga, w_out).astype(bf16)
    out_share = lax.psum_scatter(t_dot(o, ga).astype(bf16), "replica", scatter_dimension=0, tiled=True)
    gqkv = attention_back(rot, go, cosine, sine, pieces)
    qkv_share = sum_parts([t_dot(n1, gqkv)])
    gn1_part = dot_t(gqkv, w_qkv)
    attn_gain_part = jnp.sum(gn1_part * u1, axis=0)
    (gn1,) = line_comm(6, "scatter_gn1", rs=[gn1_part.astype(bf16)])
    (gu_rows,) = line_comm(7, "rows_ffn", a2a=[rows_back(gu_share, 2)])
    (qkv_rows,) = line_comm(8, "rows_attn", a2a=[rows_back(qkv_share, 3)])
    gain_rows = gain_sum(9, jnp.stack([attn_gain_part, ffn_gain_part]))

    grad_down = join(down_share, 0).reshape(w_down.shape).astype(f32)
    grad_out = join(out_share, 0).reshape(w_out.shape).astype(f32)
    grad_gu = join(gu_rows, 0).astype(f32)
    grad_qkv = join(qkv_rows, 0).astype(f32)

    own_x = tokens.astype(f32)
    r1 = rms_scale(own_x)
    u1 = own_x * r1
    gu1 = gn1 * attn_gain
    grad_tokens = gmid + r1 * (gu1 - u1 * jnp.mean(gu1 * u1, axis=1, keepdims=True))
    return (
        output,
        grad_tokens,
        grad_qkv[:, 0].reshape(w_query.shape),
        grad_qkv[:, 1].reshape(w_key.shape),
        grad_qkv[:, 2].reshape(w_value.shape),
        grad_out,
        grad_gu[:, 0].reshape(w_gate.shape),
        grad_gu[:, 1].reshape(w_up.shape),
        grad_down,
        gain_rows[0],
        gain_rows[1],
    )


def solution(mesh):
    tok = P(("replica", "inner"), None)
    row = P("inner", None)
    vec = P("inner")
    mark = P(("replica", "inner"))
    return jax.shard_map(
        local,
        mesh=mesh,
        in_specs=(tok, row, row, row, row, row, row, row, vec, vec, mark, mark, tok),
        out_specs=(tok, tok, row, row, row, row, row, row, row, vec, vec),
        check_vma=False,
    )
```

time: 1300 us -> 911 us (0.70)
  waiting for transfers between devices: 756 us -> 216 us
  Pallas kernels: 0 us -> 468 us
  blocking collectives: 289 us -> 0 us
  matrix products: 129 us -> 96.5 us
  local copies, waits for them, and re-layouts: 44.6 us -> 75.4 us
  other arithmetic: 51.4 us -> 29.7 us
    pallas_call x0 -> x12, Pallas kernels: none -> 468 us  [the longest x9 441 us: line_comm(): pl.pallas_call(functools.partial(line_body, n, len(ag), len(rs), [(len(t[...]
    all_gather x16 -> x6, waiting for transfers between devices: 487 us -> 90.2 us  [the longest x4 90.2 us: join(): return lax.all_gather(block, 'replica', axis=axis, tiled=False)]
    all_to_all x10 -> x0, blocking collectives: 231 us -> none  [the longest x5 125 us: column_shard(): lax.all_to_all(mine, 'inner', split_axis=1, concat_axis=0, tiled=False)]
    reduce_scatter x11 -> x4, waiting for transfers between devices: 267 us -> 125 us  [the longest x2 89.9 us: sum_parts(): lax.psum_scatter(g, 'replica', scatter_dimension=0, tiled=True)]
    psum x1 -> x0, blocking collectives: 39.7 us -> none  [local(): lax.psum(jnp.stack([attn_gain_part, ffn_gain_part]), ('replica', 'inner'))]
    convert_element_type x13 -> x5, other arithmetic: 38 us -> 13 us  [the longest x1 6.65 us: local(): grad_down = join(down_share, 0).reshape(w_down.shape).astype(f32)]
    transpose x0 -> x4, local copies, waits for them, and re-layouts: none -> 21.9 us  [the longest x2 11.4 us: all_copies(): return full.transpose(1, 0, 2, 3).reshape(-1, cols)]
    all_gather x2 -> x0, blocking collectives: 18.8 us -> none  [the longest x1 9.64 us: local(): lax.all_gather(jnp.stack([gain_attn, gain_ffn]), 'inner', axis=1, tiled=T...]
  transfers between devices with their start and end apart: 27 -> 10, of which waited for: 24 -> 4; matrix products, arithmetic and copies ran while one was open for 13% -> 13% of each run, Pallas kernels for 0% -> 37%
where the time goes in v2:
time: 911 us; the launch traced here: 901 us
  Pallas kernels  468 us (51%)
  waiting for transfers between devices  216 us (24%)
  matrix products  96.5 us (11%)
  local copies, waits for them, and re-layouts  75.4 us (8%)
  other arithmetic  29.7 us (3%)
  between operations  15.2 us (2%)
    pallas_call x9, Pallas kernels, line_comm(): pl.pallas_call(functools.partial(line_body, n, len(ag), len(rs), [(len(t[...  441 us
    all_gather x4, waiting for transfers between devices, join(): return lax.all_gather(block, 'replica', axis=axis, tiled=False)  90.2 us
    reduce_scatter x2, waiting for transfers between devices, sum_parts(): lax.psum_scatter(g, 'replica', scatter_dimension=0, tiled=True)  89.9 us
    reduce_scatter x1, waiting for transfers between devices, local(): lax.psum_scatter(t_dot(hid, cot).astype(bf16), 'replica', scatter_dimensi...  34.8 us
    dot_general x5, matrix products, dot(): return jnp.dot(a, b, preferred_element_type=f32)  33.9 us
    dot_general x5, matrix products, t_dot(): return lax.dot_general(a, b, dims_cols, preferred_element_type=f32)  31.3 us
    dot_general x5, matrix products, dot_t(): return lax.dot_general(a, b, dims_rows, preferred_element_type=f32)  31.3 us
    unnamed x84, local copies, waits for them, and re-layouts  20.4 us
  transfers between devices with their start and end apart: 10, of which 4 were waited for; matrix products, arithmetic and copies ran while one was open for 13% of the time, Pallas kernels for 37%

profile of v2, /device:TPU:0, one launch (start us, length us, event | category | flops | bytes accessed | tf_op | source)
XLA Modules:
  0.0 901.2 jit_solution(6582681978745764936)
XLA Ops:
  13.7 25.8 %load_attn.1 = (bf16[8,64,768]{2,1,0:T(8,128)(2,1)}, s32[8,8,128]{2,1,0:T(8,128)S(1)}, f32[8,8,256]{2,1,0:T(8,128)S(1)}) custom-call(bf16[256,2048]{1,0:T(8,128)(2,1)S(1)} %copy-done.22, bf16[256,2048]{1,0:T(8,128)(2,1)S(1)} %copy-done.23, bf16[256,2048]{1,0:T(8,128)(2,1)S(1)} %copy-done.24, s32[8,128]{1,0:T(8,128)S(1)} %scatter.21.refs_3_, ...), custom_call_target="tpu_custom_call" | custom-call | tf_op jit(solution)/shard_map/load_attn/pallas_call | solution.py:365
  39.7 81.5 %load_ffn.1 = (bf16[8,128,2048]{2,1,0:T(8,128)(2,1)}, bf16[8,64,2048]{2,1,0:T(8,128)(2,1)S(1)}) custom-call(bf16[128,2048]{1,0:T(8,128)(2,1)S(1)} %copy-done.2, bf16[256,8192]{1,0:T(8,128)(2,1)} %refs_1_.2, bf16[256,8192]{1,0:T(8,128)(2,1)} %refs_2_.2), custom_call_target="tpu_custom_call" | custom-call | tf_op jit(solution)/shard_map/load_ffn/pallas_call | solution.py:365
  122.8 1.9 fusion.15
  126.1 3.0 multiply_convert_fusion.1
  129.1 3.0 copy.44
  132.1 1.9 copy-done.33
  134.0 5.1 fusion.22.lin
  139.1 7.2 attention.1
  148.4 3.3 convolution_convert_fusion
  151.6 72.0 %attn_out.1 = (bf16[8,128,2048]{2,1,0:T(8,128)(2,1)S(1)}, f32[128,2048]{1,0:T(8,128)S(1)}) custom-call(bf16[128,2048]{1,0:T(8,128)(2,1)S(1)} %copy-done.8, bf16[8,128,2048]{2,1,0:T(8,128)(2,1)} %bitcast.98), custom_call_target="tpu_custom_call" | custom-call | tf_op jit(solution)/shard_map/attn_out/pallas_call | solution.py:365
  224.2 39.5 %gather_n2.1 = bf16[8,128,2048]{2,1,0:T(8,128)(2,1)S(1)} custom-call(bf16[128,2048]{1,0:T(8,128)(2,1)S(1)} %multiply_convert_fusion.5.refs_0_), custom_call_target="tpu_custom_call" | custom-call | tf_op jit(solution)/shard_map/gather_n2/pallas_call | solution.py:365
  263.7 2.0 copy-done.12
  265.7 8.3 fusion.23
  274.0 8.4 copy.46
  282.5 10.1 %fusion.3 = f32[1024,1024]{1,0:T(8,128)} fusion(bf16[1024,2048]{1,0:T(8,128)(2,1)} %bitcast.85, bf16[2048,2048]{1,0:T(8,128)(2,1)} %bitcast.102), kind=kOutput, calls=%fused_computation.19 | convolution fusion | flops 4294967296 | bytes 12582912 | tf_op jit(solution)/shard_map/dot_general | solution.py:22
  292.6 9.5 %multiply_convert_fusion.2 = (bf16[1024,1024]{1,0:T(8,128)(2,1)}, bf16[1024,1024]{1,0:T(8,128)(2,1)S(1)}, bf16[1024,1024]{1,0:T(8,128)(2,1)}) fusion(f32[1024,1024]{1,0:T(8,128)} %fusion.3, f32[1024,1024]{1,0:T(8,128)S(1)} %copy-done.38, bf16[1024,2048]{1,0:T(8,128)(2,1)S(1)} %bitcast.87, bf16[2048,2048]{1,0:T(8,128)(2,1)S(1)} %bitcast.103), kind=kOutput, calls=%fused_computation.7 | convolution fusion | flops 4310695936 | bytes 23068672 | tf_op jit(solution)/shard_map/dot_general | solution.py:22
  302.0 6.8 fusion.1
  308.8 7.4 add_convert_fusion
  316.3 43.8 %scatter_gn2.1 = f32[128,2048]{1,0:T(8,128)S(1)} custom-call(bf16[8,128,2048]{2,1,0:T(8,128)(2,1)S(1)} %bitcast.84), custom_call_target="tpu_custom_call" | custom-call | tf_op jit(solution)/shard_map/scatter_gn2/pallas_call | solution.py:365
  360.8 6.0 convolution_convert_fusion.4
  366.8 69.0 %gather_ga.1 = (bf16[8,128,2048]{2,1,0:T(8,128)(2,1)S(1)}, f32[128,2048]{1,0:T(8,128)S(1)}) custom-call(bf16[128,2048]{1,0:T(8,128)(2,1)S(1)} %fusion.17.refs_0_, bf16[8,128,2048]{2,1,0:T(8,128)(2,1)} %bitcast.108), custom_call_target="tpu_custom_call" | custom-call | tf_op jit(solution)/shard_map/gather_ga/pallas_call | solution.py:365
  436.8 2.0 copy-done.27
  438.8 2.3 convolution_convert_fusion.6
  441.2 3.6 convolution_convert_fusion.7.go
  444.9 7.6 attention_back.1
  452.5 5.2 multiply_reduce_fusion
  457.7 3.8 convolution_convert_fusion.5
  461.5 1.9 copy.48
  463.5 9.4 %convolution_convert_fusion.1 = bf16[1024,2048]{1,0:T(8,128)(2,1)} fusion(bf16[1024,1024]{1,0:T(8,128)(2,1)} %get-tuple-element.101, bf16[1024,2048]{1,0:T(8,128)(2,1)} %bitcast.92), kind=kOutput, calls=%fused_computation.13 | convolution fusion | flops 4297064448 | bytes 10485760 | tf_op jit(solution)/shard_map/dot_general | solution.py:30
  473.2 9.6 %convolution_convert_fusion.2 = bf16[2048,1024]{0,1:T(8,128)(2,1)} fusion(bf16[1024,2048]{1,0:T(8,128)(2,1)} %bitcast.86, bf16[1024,1024]{1,0:T(8,128)(2,1)} %get-tuple-element.103), kind=kOutput, calls=%fused_computation.14 | convolution fusion | flops 4297064448 | bytes 10485760 | tf_op jit(solution)/shard_map/dot_general | solution.py:30
  482.8 6.3 convolution_convert_fusion.3
  489.1 8.7 pad_maximum_fusion
  497.9 12.0 %copy.49 = bf16[2048,2048]{1,0:T(8,128)(2,1)} copy(bf16[2048,2048]{0,1:T(8,128)(2,1)} %pad_maximum_fusion) | data formatting | bytes 16777216 | tf_op jit(solution)/shard_map/concatenate | solution.py:611
  509.9 8.5 copy.50
  520.4 17.0 %rows_attn.1 = bf16[3,64,2048]{2,1,0:T(8,128)(2,1)} custom-call(bf16[8,64,768]{2,1,0:T(8,128)(2,1)S(1)} %bitcast.90), custom_call_target="tpu_custom_call" | custom-call | tf_op jit(solution)/shard_map/rows_attn/pallas_call | solution.py:365
  537.5 34.8 %reduce-scatter.11.cloned.1.call-done = bf16[256,2048]{1,0:T(8,128)(2,1)} async-done(((bf16[1024,2048]{1,0:T(8,128)(2,1)}), bf16[256,2048]{1,0:T(8,128)(2,1)}) %reduce-scatter.11.cloned.1.call-update) | async-done | bytes 1048592 | tf_op jit(solution)/shard_map/reduce_scatter | solution.py:670
  572.4 89.8 %reduce-scatter.9.cloned.1.call-done = bf16[512,2048]{1,0:T(8,128)(2,1)} async-done(((bf16[2048,2048]{1,0:T(8,128)(2,1)}), bf16[512,2048]{1,0:T(8,128)(2,1)}) %reduce-scatter.9.cloned.1.call-update) | async-done | bytes 2097168 | tf_op jit(solution)/shard_map/reduce_scatter | solution.py:614
  663.8 37.9 %rows_ffn.1 = bf16[2,64,8192]{2,1,0:T(8,128)(2,1)S(1)} custom-call(bf16[8,64,2048]{2,1,0:T(8,128)(2,1)S(1)} %bitcast.89), custom_call_target="tpu_custom_call" | custom-call | tf_op jit(solution)/shard_map/rows_ffn/pallas_call | solution.py:365
  703.1 2.2 copy-done.11
  705.4 53.9 %scatter_gn1.1 = f32[128,2048]{1,0:T(8,128)S(1)} custom-call(bf16[8,128,2048]{2,1,0:T(8,128)(2,1)S(1)} %bitcast.83), custom_call_target="tpu_custom_call" | custom-call | tf_op jit(solution)/shard_map/scatter_gn1/pallas_call | solution.py:365
  760.0 12.8 %gain_sum.1 = f32[8,256]{1,0:T(8,128)} custom-call(f32[8,8,256]{2,1,0:T(8,128)} %scatter.32.g), custom_call_target="tpu_custom_call" | custom-call | tf_op jit(solution)/shard_map/gain_sum/pallas_call | solution.py:552
  774.4 3.2 fusion.13
  777.5 2.8 convert_element_type.140
  780.3 4.8 fusion.19
  785.1 6.8 all-gather.23.cloned.1.call-done
  791.9 6.7 convert_element_type.141
  798.6 83.4 %all-gather.21.cloned.1.call-done = bf16[8,64,8192]{2,1,0:T(8,128)(2,1)} async-done(((bf16[2,64,8192]{2,1,0:T(8,128)(2,1)}), bf16[8,64,8192]{2,1,0:T(8,128)(2,1)}) %all-gather.21.cloned.1.call-update) | async-done | bytes 8388624 | tf_op jit(solution)/shard_map/all_gather | solution.py:618
  882.0 11.9 %fusion.18 = (f32[4,1,64,8192]{3,2,1,0:T(8,128)}, f32[4,1,64,8192]{3,2,1,0:T(8,128)}) fusion(bf16[4,2,64,8192]{3,2,1,0:T(8,128)(2,1)} %bitcast.95), kind=kLoop, calls=%fused_computation.60 | loop fusion | bytes 33554432 | tf_op jit(solution)/shard_map/slice | solution.py:711
  (131 shorter events, 21.5 us)
Async XLA Ops:
  7.2 141.2 %copy-start = (bf16[256,2048]{1,0:T(8,128)(2,1)S(1)}, bf16[256,2048]{1,0:T(8,128)(2,1)}, u32[]{:S(2)}) copy-start(bf16[256,2048]{1,0:T(8,128)(2,1)} %param.27) | copy-start | bytes 3145732
  7.2 32.5 %copy-start.2 = (bf16[128,2048]{1,0:T(8,128)(2,1)S(1)}, bf16[128,2048]{1,0:T(8,128)(2,1)}, u32[]{:S(2)}) copy-start(bf16[128,2048]{1,0:T(8,128)(2,1)} %refs_0_.3) | copy-start | bytes 1572868
  7.2 121.9 %all-gather.13.cloned.1.call-start = ((), (), s32[]{:S(2)}) async-start(), calls=%async_computation.8 | async-start | bytes 3932160 | tf_op jit(solution)/shard_map/all_gather | solution.py:605
  10.1 1.2 copy-start.22
  11.3 1.2 copy-start.23
  12.5 1.2 copy-start.24
  39.6 234.4 %all-gather.15.cloned.1.call-start = ((), (), s32[]{:S(2)}) async-start(), calls=%async_computation.9 | async-start | bytes 10485760 | tf_op jit(solution)/shard_map/all_gather | solution.py:605
  121.1 1.3 copy-start.15
  122.5 396.1 %reduce-scatter.7.cloned.1.call-start = ((), (), s32[]{:S(2)}) async-start(), calls=%async_computation.5 | async-start | bytes 1310720 | tf_op jit(solution)/shard_map/reduce_scatter | solution.py:683
  122.8 16.3 %copy-start.6 = (s32[1024,1]{1,0:T(8,128)}, s32[1024,1]{1,0:T(8,128)S(1)}, u32[]{:S(2)}) copy-start(s32[1024,1]{1,0:T(8,128)S(1)} %copy.45.piece) | copy-start | bytes 12292
  122.8 2.4 copy-start.30
  125.1 14.1 %copy-start.4 = (f32[1024,128]{1,0:T(8,128)}, f32[1024,128]{1,0:T(8,128)S(1)}, u32[]{:S(2)}) copy-start(f32[1024,128]{1,0:T(8,128)S(1)} %get-tuple-element.124.sine) | copy-start | bytes 1572868
  129.1 4.9 copy-start.33
  132.1 7.0 copy-start.34
  147.5 4.1 copy-start.8
  223.7 42.0 %copy-start.26 = (bf16[8,128,2048]{2,1,0:T(8,128)(2,1)}, bf16[8,128,2048]{2,1,0:T(8,128)(2,1)S(1)}, u32[]{:S(2)}) copy-start(bf16[8,128,2048]{2,1,0:T(8,128)(2,1)S(1)} %get-tuple-element.88) | copy-start | bytes 12582916
  224.0 39.7 %copy-start.28 = (f32[128,2048]{1,0:T(8,128)}, f32[128,2048]{1,0:T(8,128)S(1)}, u32[]{:S(2)}) copy-start(f32[128,2048]{1,0:T(8,128)S(1)} %get-tuple-element.96) | copy-start | bytes 3145732
  263.7 2.0 copy-start.12
  282.5 10.1 %copy-start.13 = (bf16[8,128,2048]{2,1,0:T(8,128)(2,1)S(1)}, bf16[8,128,2048]{2,1,0:T(8,128)(2,1)}, u32[]{:S(2)}) copy-start(bf16[8,128,2048]{2,1,0:T(8,128)(2,1)} %copy-done.12) | copy-start | bytes 12582916
  282.5 10.1 %copy-start.32 = (bf16[8,4,64,2048]{3,2,1,0:T(8,128)(2,1)S(1)}, bf16[8,4,64,2048]{3,2,1,0:T(8,128)(2,1)}, u32[]{:S(2)}) copy-start(bf16[8,4,64,2048]{3,2,1,0:T(8,128)(2,1)} %copy.46) | copy-start | bytes 25165828
  282.5 10.1 %copy-start.38 = (f32[1024,1024]{1,0:T(8,128)S(1)}, f32[1024,1024]{1,0:T(8,128)}, u32[]{:S(2)}) copy-start(f32[1024,1024]{1,0:T(8,128)} %fusion.23) | copy-start | bytes 12582916
  302.0 6.8 copy-start.39
  302.0 6.8 copy-start.41
  316.2 43.9 %copy-start.29 = (f32[128,2048]{1,0:T(8,128)S(1)}, f32[128,2048]{1,0:T(8,128)}, u32[]{:S(2)}) copy-start(f32[128,2048]{1,0:T(8,128)} %copy-done.28) | copy-start | bytes 3145732
  316.2 44.2 %copy-start.9 = (bf16[128,2048]{1,0:T(8,128)(2,1)S(1)}, bf16[128,2048]{1,0:T(8,128)(2,1)}, u32[]{:S(2)}) copy-start(bf16[128,2048]{1,0:T(8,128)(2,1)} %refs_0_.5) | copy-start | bytes 1572868
  316.2 44.5 %copy-start.36 = (bf16[1024,2048]{1,0:T(8,128)(2,1)S(1)}, bf16[1024,2048]{1,0:T(8,128)(2,1)}, u32[]{:S(2)}) copy-start(bf16[1024,2048]{1,0:T(8,128)(2,1)} %param.30) | copy-start | bytes 12582916
  316.2 44.5 %copy-start.37 = (bf16[1024,1024]{1,0:T(8,128)(2,1)S(1)}, bf16[1024,1024]{1,0:T(8,128)(2,1)}, u32[]{:S(2)}) copy-start(bf16[1024,1024]{1,0:T(8,128)(2,1)} %get-tuple-element.101) | copy-start | bytes 6291460
  366.8 72.0 %copy-start.20 = (bf16[1024,256]{1,0:T(8,128)(2,1)S(1)}, bf16[1024,256]{1,0:T(8,128)(2,1)}, u32[]{:S(2)}) copy-start(bf16[1024,256]{1,0:T(8,128)(2,1)} %copy-done.19) | copy-start | bytes 1572868
  436.8 2.0 copy-start.27
  441.1 78.2 %reduce-scatter.5.cloned.1.call-start = ((), (), s32[]{:S(2)}) async-start(), calls=%async_computation.4 | async-start | bytes 3932160 | tf_op jit(solution)/shard_map/reduce_scatter | solution.py:614
  441.2 3.7 copy-start.5
  441.2 3.7 copy-start.7
  441.2 3.7 copy-start.18
  441.2 11.3 %copy-start.35 = (bf16[8,4,64,768]{3,2,1,0:T(8,128)(2,1)S(1)}, bf16[8,4,64,768]{3,2,1,0:T(8,128)(2,1)}, u32[]{:S(2)}) copy-start(bf16[8,4,64,768]{3,2,1,0:T(8,128)(2,1)} %copy-done.34) | copy-start | bytes 9437188
  444.8 7.6 copy-start.31
  463.5 108.8 %reduce-scatter.11.cloned.1.call-start = ((), (), s32[]{:S(2)}) async-start(), calls=%async_computation.7 | async-start | bytes 5242880 | tf_op jit(solution)/shard_map/reduce_scatter | solution.py:670
  473.0 189.3 %reduce-scatter.9.cloned.1.call-start = ((), (), s32[]{:S(2)}) async-start(), calls=%async_computation.6 | async-start | bytes 10485760 | tf_op jit(solution)/shard_map/reduce_scatter | solution.py:614
  473.2 9.6 %copy-start.14 = (bf16[8,128,2048]{2,1,0:T(8,128)(2,1)S(1)}, bf16[8,128,2048]{2,1,0:T(8,128)(2,1)}, u32[]{:S(2)}) copy-start(bf16[8,128,2048]{2,1,0:T(8,128)(2,1)} %copy-done.12) | copy-start | bytes 12582916
  473.2 9.6 %copy-start.40 = (bf16[1024,1024]{1,0:T(8,128)(2,1)S(1)}, bf16[1024,1024]{1,0:T(8,128)(2,1)}, u32[]{:S(2)}) copy-start(bf16[1024,1024]{1,0:T(8,128)(2,1)} %copy-done.39) | copy-start | bytes 6291460
  518.5 259.1 %all-gather.19.cloned.1.call-start = ((), (), s32[]{:S(2)}) async-start(), calls=%async_computation.11 | async-start | bytes 1310720 | tf_op jit(solution)/shard_map/all_gather | solution.py:618
  519.2 261.1 %all-gather.17.cloned.1.call-start = ((), (), s32[]{:S(2)}) async-start(), calls=%async_computation.10 | async-start | bytes 3932160 | tf_op jit(solution)/shard_map/all_gather | solution.py:618
  537.5 254.5 %all-gather.23.cloned.1.call-start = ((), (), s32[]{:S(2)}) async-start(), calls=%async_computation.13 | async-start | bytes 5242880 | tf_op jit(solution)/shard_map/all_gather | solution.py:618
  572.3 309.7 %all-gather.21.cloned.1.call-start = ((), (), s32[]{:S(2)}) async-start(), calls=%async_computation.12 | async-start | bytes 10485760 | tf_op jit(solution)/shard_map/all_gather | solution.py:618
  662.2 1.6 copy-start.16
  701.7 1.3 copy-start.3
  703.1 71.3 %copy-start.10 = (bf16[128,2048]{1,0:T(8,128)(2,1)S(1)}, bf16[128,2048]{1,0:T(8,128)(2,1)}, u32[]{:S(2)}) copy-start(bf16[128,2048]{1,0:T(8,128)(2,1)} %refs_0_.5) | copy-start | bytes 1572868
  703.1 2.2 copy-start.11
  882.0 11.9 %copy-start.1 = (bf16[256,2048]{1,0:T(8,128)(2,1)S(1)}, bf16[256,2048]{1,0:T(8,128)(2,1)}, u32[]{:S(2)}) copy-start(bf16[256,2048]{1,0:T(8,128)(2,1)} %param.27) | copy-start | bytes 3145732
  (4 other events, 4.2 us)
Sparse Core Ops, SparseCore 0:
  39.7 44.4 all-gather.12
  122.6 87.5 all-gather.14
  441.2 28.0 reduce-scatter.6
  472.5 43.9 reduce-scatter.4
  519.6 52.6 reduce-scatter.10
  575.8 86.3 reduce-scatter.8
  664.2 26.6 all-gather.18
  692.8 43.9 all-gather.16
  738.9 53.0 all-gather.22
  794.4 87.5 all-gather.20

commit v3 on v2

--- a/solution.py
+++ b/solution.py
@@ -42,39 +42,50 @@
     return lax.rsqrt(jnp.mean(values * values, axis=1, keepdims=True) + epsilon)
 
 
-def rcopy(src, dst, ssem, rsem, to):
+def rcopy(src, dst, ssem, rsem, to, axis="inner"):
     return pltpu.make_async_remote_copy(
         src_ref=src,
         dst_ref=dst,
         send_sem=ssem,
         recv_sem=rsem,
-        device_id={"inner": to},
+        device_id={axis: to},
         device_id_type=pl.DeviceIdType.MESH,
     )
 
 
-def signal(sem, to):
-    pl.semaphore_signal(sem, inc=1, device_id={"inner": to}, device_id_type=pl.DeviceIdType.MESH)
-
-
-def line_body(n, n_ag, n_rs, a2a_blocks, parts, *refs):
+def signal(sem, to, axis="inner"):
+    pl.semaphore_signal(sem, inc=1, device_id={axis: to}, device_id_type=pl.DeviceIdType.MESH)
+
+
+def line_body(n, n_ag, n_rs, a2a_blocks, spreads, n_sum, parts, *refs):
     refs = list(refs)
     nz = n // 2
     n_a2a = len(a2a_blocks)
     take = lambda count: [refs.pop(0) for _ in range(count)]
+    n_sp = len(spreads)
     ag_in, rs_in, a2a_in = take(n_ag), take(n_rs), [take(t[0]) for t in a2a_blocks]
-    ag_out, rs_out, a2a_out = take(n_ag), take(n_rs), take(n_a2a)
+    sp_in, sum_in = take(n_sp), take(n_sum)
+    ag_out, rs_out, a2a_out, sp_out, sum_out = take(n_ag), take(n_rs), take(n_a2a), take(n_sp), take(n_sum)
     ag_sem = [take(7) for _ in range(n_ag)]
     rs_scr = [take(9) for _ in range(n_rs)]
     a2a_sem = [take(3) for _ in range(n_a2a)]
+    sp_sem = [take(5) for _ in range(n_sp)]
+    sum_scr = [take(6) for _ in range(n_sum)]
     me = lax.axis_index("inner")
     z, c = me // 2, lax.rem(me, 2)
     sib = me + 1 - 2 * c
+    r = lax.axis_index("replica")
+    across_x, across_y = r + 1 - 2 * lax.rem(r, 2), r + 2 - 4 * (r // 2)
     barrier = pltpu.get_barrier_semaphore()
+    more = 0
+    if n_sp + n_sum:
+        signal(barrier, across_x, "replica")
+        signal(barrier, across_y, "replica")
+        more = 2
     if n_a2a:
         for k in range(1, n):
             signal(barrier, lax.rem(me + k, n))
-        pl.semaphore_wait(barrier, n - 1)
+        pl.semaphore_wait(barrier, n - 1 + more)
     else:
         signal(barrier, sib)
 
@@ -86,7 +97,7 @@
         def _():
             signal(barrier, me - 2)
 
-        pl.semaphore_wait(barrier, 1 + (z + nz - 1) // nz + (2 * nz - 2 - z) // nz)
+        pl.semaphore_wait(barrier, 1 + more + (z + nz - 1) // nz + (2 * nz - 2 - z) // nz)
 
     def rows_of(ref, j):
         count = ref.shape[0] // parts
@@ -329,9 +340,145 @@
                     self.came(k, m).wait_recv()
                     self.to(k, m).wait_send()
 
+    class Spread:
+        def __init__(self, src, out, sems, phases):
+            self.src, self.out, self.phases = src, out, phases
+            self.own_sem, self.send, self.recv, self.send_half, self.recv_half = sems
+            self.half = out.shape[1] // 2
+
+        def own(self):
+            return pltpu.make_async_copy(self.src, self.out.at[r], self.own_sem)
+
+        def first(self, axis):
+            to = across_y if axis else across_x
+            return rcopy(self.src, self.out.at[r], self.send.at[axis], self.recv.at[axis], to, "replica")
+
+        def first_came(self, axis):
+            who = across_y if axis else across_x
+            return rcopy(self.out.at[who], self.out.at[who], self.send.at[axis], self.recv.at[axis], who, "replica")
+
+        def half_of(self, block, axis):
+            return self.out.at[block, pl.ds(axis * self.half, self.half)]
+
+        def second(self, axis):
+            block, to = (across_x, across_y) if axis else (across_y, across_x)
+            piece = self.half_of(block, axis)
+            return rcopy(piece, piece, self.send_half.at[axis], self.recv_half.at[axis], to, "replica")
+
+        def second_came(self, axis):
+            piece = self.half_of(3 - r, axis)
+            who = across_y if axis else across_x
+            return rcopy(piece, piece, self.send_half.at[axis], self.recv_half.at[axis], who, "replica")
+
+        def begin(self):
+            if 1 in self.phases:
+                self.first(0).start()
+                self.first(1).start()
+                self.own().start()
+            else:
+                self.second(0).start()
+                self.second(1).start()
+
+        def step(self, s, j):
+            pass
+
+        def mid(self):
+            if self.phases == (1, 2):
+                self.first_came(0).wait_recv()
+                self.second(1).start()
+                self.first_came(1).wait_recv()
+                self.second(0).start()
+
+        def end(self):
+            if 1 in self.phases:
+                self.own().wait()
+                for axis in (0, 1):
+                    self.first(axis).wait_send()
+                    if 2 not in self.phases:
+                        self.first_came(axis).wait_recv()
+            if 2 in self.phases:
+                for axis in (0, 1):
+                    self.second(axis).wait_send()
+                    self.second_came(axis).wait_recv()
+
     parts_of = [Gather(*t) for t in zip(ag_in, ag_out, ag_sem)]
     parts_of += [Scatter(*t) for t in zip(rs_in, rs_out, rs_scr)]
     parts_of += [Exchange(*t) for t in zip(a2a_in, a2a_out, a2a_sem, a2a_blocks)]
+    class Sum:
+        def __init__(self, p, out, scratch):
+            self.p, self.out = p, out
+            self.a, self.b, self.send_a, self.recv_a, self.send_b, self.recv_b = scratch
+            self.half = out.shape[0] // 2
+            self.bits = (lax.rem(r, 2), r // 2)
+
+        def rows(self, h):
+            return pl.ds(h * self.half, self.half)
+
+        def who(self, h):
+            return across_y if h else across_x
+
+        def first(self, h, k):
+            other = 1 - self.bits[h]
+            q = 2 * other + k if h else other + 2 * k
+            return rcopy(
+                self.p.at[q, self.rows(h)], self.a.at[h, k], self.send_a.at[h, k], self.recv_a.at[h, k], self.who(h), "replica"
+            )
+
+        def second(self, h):
+            piece = self.a.at[h, 1 - self.bits[1 - h]]
+            return rcopy(piece, self.b.at[h], self.send_b.at[h], self.recv_b.at[h], self.who(1 - h), "replica")
+
+        def each(self, h, put):
+            step = 16
+
+            @pl.loop(0, self.half // step)
+            def _(i):
+                put(pl.multiple_of(i * step, step), step)
+
+        def mine(self, h, k, at, step):
+            q = 2 * self.bits[1] + k if h else self.bits[0] + 2 * k
+            rows = pl.ds(h * self.half + at, step)
+            return self.p[q, rows, :].astype(f32) + self.a[h, k, pl.ds(at, step), :].astype(f32)
+
+        def begin(self):
+            for h in (0, 1):
+                self.first(h, 1 - self.bits[1 - h]).start()
+            for h in (0, 1):
+                self.first(h, self.bits[1 - h]).start()
+
+        def step(self, s, j):
+            pass
+
+        def mid(self):
+            for h in (0, 1):
+                k = 1 - self.bits[1 - h]
+                self.first(h, k).wait_recv()
+
+                def put(at, step):
+                    self.a[h, k, pl.ds(at, step), :] = self.mine(h, k, at, step).astype(bf16)
+
+                self.each(h, put)
+                self.second(h).start()
+
+        def end(self):
+            for h in (0, 1):
+                k = self.bits[1 - h]
+                self.first(h, k).wait_recv()
+                self.second(h).wait_recv()
+
+                def put(at, step):
+                    total = self.mine(h, k, at, step) + self.b[h, pl.ds(at, step), :].astype(f32)
+                    self.out[pl.ds(h * self.half + at, step), :] = total.astype(bf16)
+
+                self.each(h, put)
+            for h in (0, 1):
+                for k in (0, 1):
+                    self.first(h, k).wait_send()
+                self.second(h).wait_send()
+
+    square_parts = [Spread(*t) for t in zip(sp_in, sp_out, sp_sem, spreads)]
+    square_parts += [Sum(*t) for t in zip(sum_in, sum_out, sum_scr)]
+    parts_of += square_parts
     for part in parts_of:
         part.begin()
     if n_ag + n_rs:
@@ -340,11 +487,18 @@
             def _(j):
                 for part in parts_of:
                     part.step(s, j)
+
+            if s == nz - 2:
+                for part in square_parts:
+                    part.mid()
+    else:
+        for part in square_parts:
+            part.mid()
     for part in parts_of:
         part.end()
 
 
-def line_comm(cid, name, ag=(), rs=(), a2a=(), parts=2):
+def line_comm(cid, name, us, ag=(), rs=(), a2a=(), spread=(), sums=(), parts=2):
     n = lax.axis_size("inner")
     nz = n // 2
     dma = pltpu.SemaphoreType.DMA
@@ -354,6 +508,12 @@
     out_shape = [jax.ShapeDtypeStruct((n,) + x.shape, x.dtype) for x in ag]
     out_shape += [jax.ShapeDtypeStruct(p.shape[1:], f32) for p in rs]
     out_shape += [jax.ShapeDtypeStruct(t[1], t[0][0].dtype) for t in a2a]
+    out_shape += [jax.ShapeDtypeStruct(b.shape if 1 not in ph else (4,) + b.shape, b.dtype) for b, ph in spread]
+    out_shape += [jax.ShapeDtypeStruct((p.shape[0] // 4, p.shape[1]), bf16) for p in sums]
+    sums = [p.reshape((4, p.shape[0] // 4) + p.shape[1:]) for p in sums]
+    first_in = len(ag) + len(rs) + sum(len(t[0]) for t in a2a)
+    first_out = len(ag) + len(rs) + len(a2a)
+    aliases = {first_in + i: first_out + i for i, (b, ph) in enumerate(spread) if 1 not in ph}
     scratch = []
     for _ in ag:
         scratch += [dma, dma((nz, parts)), dma((nz + 1, parts)), dma((nz, parts)), dma((nz + 1, parts))]
@@ -362,17 +522,25 @@
         scratch += [pltpu.VMEM((nz,) + p.shape[1:], bf16)] * 3 + [dma((nz, parts))] * 6
     for t in a2a:
         scratch += [dma((t[4],)), dma((n, t[4])), dma((n, t[4]))]
+    for _ in spread:
+        scratch += [dma, dma((2,)), dma((2,)), dma((2,)), dma((2,))]
+    for p in sums:
+        half = (p.shape[1] // 2, p.shape[2])
+        scratch += [pltpu.VMEM((2, 2) + half, bf16), pltpu.VMEM((2,) + half, bf16)]
+        scratch += [dma((2, 2)), dma((2, 2)), dma((2,)), dma((2,))]
     outs = pl.pallas_call(
-        functools.partial(line_body, n, len(ag), len(rs), [(len(t[0]),) + t[2:5] for t in a2a], parts),
+        functools.partial(line_body, n, len(ag), len(rs), [(len(t[0]),) + t[2:5] for t in a2a], [ph for _, ph in spread], len(sums), parts),
         out_shape=out_shape,
-        in_specs=[hbm] * len(ag) + [vmem] * len(rs) + [hbm] * sum(len(t[0]) for t in a2a),
-        out_specs=[hbm] * len(ag) + [vmem] * len(rs) + [hbm] * len(a2a),
+        in_specs=[hbm] * len(ag) + [vmem] * len(rs) + [hbm] * (sum(len(t[0]) for t in a2a) + len(spread)) + [vmem] * len(sums),
+        out_specs=[hbm] * len(ag) + [vmem] * len(rs) + [hbm] * (len(a2a) + len(spread)) + [vmem] * len(sums),
+        input_output_aliases=aliases,
         scratch_shapes=scratch,
         compiler_params=pltpu.CompilerParams(
             collective_id=cid, has_side_effects=True, vmem_limit_bytes=48 * 2**20
         ),
+        cost_estimate=pl.CostEstimate(flops=us * 1150000000, bytes_accessed=us * 3600000, transcendentals=0),
         name=name,
-    )(*ag, *rs, *[w for t in a2a for w in t[0]])
+    )(*ag, *rs, *[w for t in a2a for w in t[0]], *[b for b, _ in spread], *sums)
     outs = [o.reshape((-1,) + o.shape[2:]) if i < len(ag) else o for i, o in enumerate(outs)]
     return outs
 
@@ -567,19 +735,16 @@
     )(g)[:2]
 
 
-def columns_out(weights):
+def columns_out(w):
     n, nr = lax.axis_size("inner"), lax.axis_size("replica")
-    part = weights[0].shape[0] // nr
-    cols = weights[0].shape[1] // n
+    part = w.shape[0] // nr
+    cols = w.shape[1] // n
 
     def source(refs, other, m):
         rows = pl.ds(pl.multiple_of(lax.axis_index("replica") * part, part), part)
-        return refs[m].at[rows, pl.ds(pl.multiple_of(other * cols, cols), cols)]
-
-    def target(ref, other, m):
-        return ref.at[other, :, pl.ds(m * cols, cols)]
-
-    return (tuple(weights), (n, part, cols * len(weights)), source, target, len(weights))
+        return refs[0].at[rows, pl.ds(pl.multiple_of(other * cols, cols), cols)]
+
+    return ((w,), (n, part, cols), source, lambda ref, other, m: ref.at[other], 1)
 
 
 def to_all(block):
@@ -600,22 +765,28 @@
     return ((share,), (count, part, n * cols), source, target, count)
 
 
-def all_copies(block):
-    n, part, cols = block.shape
-    full = lax.all_gather(block, "replica", axis=0, tiled=False)
-    return full.transpose(1, 0, 2, 3).reshape(-1, cols)
-
-
-def sum_parts(products):
+def shares_first(x):
     n, nr = lax.axis_size("inner"), lax.axis_size("replica")
-    g = jnp.concatenate([p.astype(bf16) for p in products], axis=1)
-    part = g.shape[0] // n // nr
-    g = g.reshape(n, nr, part, -1).transpose(1, 0, 2, 3).reshape(nr * n * part, -1)
-    return lax.psum_scatter(g, "replica", scatter_dimension=0, tiled=True).reshape(n, part, -1)
-
-
-def join(block, axis):
-    return lax.all_gather(block, "replica", axis=axis, tiled=False)
+    part = x.shape[1] // n // nr
+    return x.reshape(x.shape[0], n, nr, part).transpose(0, 2, 1, 3).reshape(x.shape)
+
+
+def owners_first(x):
+    n, nr = lax.axis_size("inner"), lax.axis_size("replica")
+    part = x.shape[1] // n // nr
+    return x.reshape(x.shape[0], nr, n, part).transpose(0, 2, 1, 3).reshape(x.shape)
+
+
+def sum_share(product):
+    return lax.psum_scatter(product.astype(bf16), "replica", scatter_dimension=0, tiled=True)
+
+
+def join(block):
+    return lax.all_gather(block, "replica", axis=0, tiled=False)
+
+
+def flat(w):
+    return w.reshape(-1, w.shape[-1])
 
 
 def local(
@@ -635,66 +806,110 @@
 ):
     n = lax.axis_size("inner")
     nr = lax.axis_size("replica")
+    square = nr == 4
     own, width = tokens.shape
     length = own * n
     rows = gain_attn.shape[0]
+    after = lax.optimization_barrier
 
     marks = jnp.zeros((8, own), jnp.int32).at[0].set(pieces).at[1].set(positions)
     gains = jnp.zeros((8, rows), f32).at[0].set(gain_attn.astype(f32)).at[1].set(gain_ffn.astype(f32))
-    qkv_share, marks, gains = line_comm(
-        0, "load_attn", a2a=[columns_out([w_query, w_key, w_value]), to_all(marks), to_all(gains)]
+    q_share, k_share, v_share, marks, gains = line_comm(
+        0,
+        "load_attn", 25,
+        a2a=[columns_out(w_query), columns_out(w_key), columns_out(w_value), to_all(marks), to_all(gains)],
     )
-    w_qkv = all_copies(qkv_share)
-    x, gu_share = line_comm(1, "load_ffn", ag=[tokens], a2a=[columns_out([w_gate, w_up])])
-    w_gu = all_copies(gu_share)
-    w_g, w_u = w_gu[:, : w_gu.shape[1] // 2], w_gu[:, w_gu.shape[1] // 2 :]
+    qkv_share = jnp.concatenate([q_share, k_share, v_share], axis=2)
+    loads = [columns_out(w_gate), columns_out(w_up)]
+    if square:
+        x, g_share, u_share, w_qkv = line_comm(
+            1, "load_ffn", 80, ag=[shares_first(tokens)], a2a=loads, spread=[(qkv_share, (1, 2))]
+        )
+    else:
+        w_qkv = join(qkv_share)
+        x, g_share, u_share = line_comm(1, "load_ffn", 80, ag=[shares_first(tokens)], a2a=loads)
+    w_qkv = flat(w_qkv)
+    cot, x = after((cotangent, x))
+    cot = lax.all_gather(cot, "inner", axis=0, tiled=True)
     pieces, positions = marks[:, 0].reshape(length, 1), marks[:, 1].reshape(length)
-    attn_gain, ffn_gain = gains[:, 0].reshape(-1), gains[:, 1].reshape(-1)
+    attn_gain, ffn_gain = gains[:, 0].reshape(1, -1), gains[:, 1].reshape(1, -1)
 
     x = x.astype(f32)
     cosine, sine = rope_tables(positions)
     u1 = x * rms_scale(x)
-    n1 = (u1 * attn_gain).astype(bf16)
+    n1 = (u1 * shares_first(attn_gain)).astype(bf16)
     o, rot = attention(dot(n1, w_qkv), cosine, sine, pieces)
-    cot, a = line_comm(2, "attn_out", ag=[cotangent], rs=[dot(o, w_out).astype(bf16)])
+    a_part = dot(o, w_out).astype(bf16)
+    if square:
+        a, w_g, w_u = line_comm(2, "attn_out", 50, rs=[a_part], spread=[(g_share, (1,)), (u_share, (1,))])
+    else:
+        w_g, w_u = join(g_share), join(u_share)
+        (a,) = line_comm(2, "attn_out", 50, rs=[a_part])
     mid = tokens.astype(f32) + a
     r2 = rms_scale(mid)
     u2 = mid * r2
-    (n2,) = line_comm(3, "gather_n2", ag=[(u2 * ffn_gain).astype(bf16)])
+    n2 = shares_first((u2 * ffn_gain).astype(bf16))
+    if square:
+        n2, w_g, w_u = line_comm(3, "gather_n2", 40, ag=[n2], spread=[(w_g, (2,)), (w_u, (2,))])
+    else:
+        (n2,) = line_comm(3, "gather_n2", 40, ag=[n2])
+    w_g, w_u = flat(w_g), flat(w_u)
 
     gate = dot(n2, w_g)
     up = dot(n2, w_u)
     s = jax.nn.sigmoid(gate)
     silu = gate * s
     hid = (silu * up).astype(bf16)
-    down_share = lax.psum_scatter(t_dot(hid, cot).astype(bf16), "replica", scatter_dimension=0, tiled=True)
+    g_down = t_dot(hid, cot).astype(bf16)
     ghid = dot_t(cot, w_down)
     ggate = (ghid * up * s * (1.0 + gate * (1.0 - s))).astype(bf16)
     gup = (ghid * silu).astype(bf16)
-    gu_share = sum_parts([t_dot(n2, ggate), t_dot(n2, gup)])
-    (gn2,) = line_comm(4, "scatter_gn2", rs=[(dot_t(ggate, w_g) + dot_t(gup, w_u)).astype(bf16)])
+    gu = t_dot(n2, jnp.concatenate([ggate, gup], axis=1)).astype(bf16)
+    gn2_part = (dot_t(ggate, w_g) + dot_t(gup, w_u)).astype(bf16)
+    gu, gn2_part = after((gu, gn2_part))
+    gu_share = sum_share(gu)
+    (gn2,) = line_comm(4, "scatter_gn2", 44, rs=[gn2_part])
+    gn2 = owners_first(gn2)
     gu2 = gn2 * ffn_gain
     ffn_gain_part = jnp.sum(gn2 * u2, axis=0)
     gmid = cotangent.astype(f32) + r2 * (gu2 - u2 * jnp.mean(gu2 * u2, axis=1, keepdims=True))
-    ga, mlp = line_comm(5, "gather_ga", ag=[gmid.astype(bf16)], rs=[dot(hid, w_down).astype(bf16)])
+    if square:
+        ga, down_share = line_comm(5, "gather_ga", 40, ag=[gmid.astype(bf16)], sums=[g_down])
+    else:
+        (ga,) = line_comm(5, "gather_ga", 40, ag=[gmid.astype(bf16)])
+        down_share = sum_share(g_down)
+
+    go = dot_t(ga, w_out).astype(bf16)
+    gqkv = attention_back(rot, go, cosine, sine, pieces)
+    g_out = t_dot(o, ga).astype(bf16)
+    g_qkv = t_dot(n1, gqkv).astype(bf16)
+    gn1_part = dot_t(gqkv, w_qkv)
+    attn_gain_part = jnp.sum(gn1_part * u1, axis=0, keepdims=True)
+    gn1_part = gn1_part.astype(bf16)
+    gu_back = rows_back(gu_share.reshape(n, -1, gu.shape[1]), 2)
+    mlp_part = dot(hid, w_down).astype(bf16)
+    if square:
+        gn1, gu_rows, grad_down, out_share, qkv_share = line_comm(
+            6, "scatter_gn1", 80, rs=[gn1_part], a2a=[gu_back], spread=[(down_share, (1, 2))], sums=[g_out, g_qkv]
+        )
+        qkv_back = rows_back(qkv_share.reshape(n, -1, gqkv.shape[1]), 3)
+        mlp, qkv_rows, grad_gu, grad_out = line_comm(
+            7, "rows_ffn", 75, rs=[mlp_part], a2a=[qkv_back], spread=[(gu_rows, (1, 2)), (out_share, (1, 2))]
+        )
+        (grad_qkv,) = line_comm(8, "rows_attn", 28, spread=[(flat(qkv_rows), (1, 2))])
+    else:
+        gn1, gu_rows = line_comm(6, "scatter_gn1", 80, rs=[gn1_part], a2a=[gu_back])
+        qkv_back = rows_back(sum_share(g_qkv).reshape(n, -1, gqkv.shape[1]), 3)
+        mlp, qkv_rows = line_comm(7, "rows_ffn", 75, rs=[mlp_part], a2a=[qkv_back])
+        grad_gu, grad_out, grad_down, grad_qkv = join(gu_rows), join(sum_share(g_out)), join(down_share), join(qkv_rows)
     output = (mid + mlp).astype(bf16)
-
-    go = dot_t(ga, w_out).astype(bf16)
-    out_share = lax.psum_scatter(t_dot(o, ga).astype(bf16), "replica", scatter_dimension=0, tiled=True)
-    gqkv = attention_back(rot, go, cosine, sine, pieces)
-    qkv_share = sum_parts([t_dot(n1, gqkv)])
-    gn1_part = dot_t(gqkv, w_qkv)
-    attn_gain_part = jnp.sum(gn1_part * u1, axis=0)
-    (gn1,) = line_comm(6, "scatter_gn1", rs=[gn1_part.astype(bf16)])
-    (gu_rows,) = line_comm(7, "rows_ffn", a2a=[rows_back(gu_share, 2)])
-    (qkv_rows,) = line_comm(8, "rows_attn", a2a=[rows_back(qkv_share, 3)])
-    gain_rows = gain_sum(9, jnp.stack([attn_gain_part, ffn_gain_part]))
-
-    grad_down = join(down_share, 0).reshape(w_down.shape).astype(f32)
-    grad_out = join(out_share, 0).reshape(w_out.shape).astype(f32)
-    grad_gu = join(gu_rows, 0).astype(f32)
-    grad_qkv = join(qkv_rows, 0).astype(f32)
-
+    gain_rows = gain_sum(9, jnp.stack([owners_first(attn_gain_part)[0], ffn_gain_part]))
+    grad_down = grad_down.reshape(w_down.shape).astype(f32)
+    grad_out = grad_out.reshape(w_out.shape).astype(f32)
+    grad_gu = grad_gu.astype(f32)
+    grad_qkv = grad_qkv.reshape(nr, 3, -1, width).astype(f32)
+
+    gn1 = owners_first(gn1)
     own_x = tokens.astype(f32)
     r1 = rms_scale(own_x)
     u1 = own_x * r1

time: 911 us -> 768 us (0.84)
  waiting for transfers between devices: 216 us -> 0.04 us
  Pallas kernels: 468 us -> 546 us
  matrix products: 96.5 us -> 117 us
  local copies, waits for them, and re-layouts: 75.4 us -> 57.9 us
    reduce_scatter x4 -> x1, waiting for transfers between devices: 125 us -> 0.01 us  [sum_share(): lax.psum_scatter(product.astype(bf16), 'replica', scatter_dimension=0, ti...]
    all_gather x6 -> x1, waiting for transfers between devices: 90.2 us -> 0.01 us  [local(): cot = lax.all_gather(cot, 'inner', axis=0, tiled=True)]
    pallas_call x9, Pallas kernels: 441 us -> 520 us  [line_comm(): pl.pallas_call(functools.partial(line_body, n, len(ag), len(rs), [(len(t[...]
    transpose x4 -> x5, local copies, waits for them, and re-layouts: 21.9 us -> 6.53 us  [the longest x3 4.62 us: owners_first(): x.reshape(x.shape[0], nr, n, part).transpose(0, 2, 1, 3).reshape(x.shape)]
    concatenate x1 -> x0, local copies, waits for them, and re-layouts: 12 us -> none  [sum_parts(): g = jnp.concatenate([p.astype(bf16) for p in products], axis=1)]
    dot_general x5 -> x4, matrix products: 31.3 us -> 40.1 us  [t_dot(): return lax.dot_general(a, b, dims_cols, preferred_element_type=f32)]
    unnamed x84 -> x113, local copies, waits for them, and re-layouts: 20.4 us -> 18.9 us
  transfers between devices with their start and end apart: 10 -> 2, of which waited for: 4 -> 0; matrix products, arithmetic and copies ran while one was open for 13% -> 11% of each run, Pallas kernels for 37% -> 30%
where the time goes in v3:
time: 768 us; the launch traced here: 759 us
  Pallas kernels  546 us (71%)
  matrix products  117 us (15%)
  local copies, waits for them, and re-layouts  57.9 us (8%)
  other arithmetic  23.4 us (3%)
  between operations  15.1 us (2%)
    pallas_call x9, Pallas kernels, line_comm(): pl.pallas_call(functools.partial(line_body, n, len(ag), len(rs), [(len(t[...  520 us
    dot_general x4, matrix products, t_dot(): return lax.dot_general(a, b, dims_cols, preferred_element_type=f32)  40.1 us
    dot_general x5, matrix products, dot_t(): return lax.dot_general(a, b, dims_rows, preferred_element_type=f32)  39.3 us
    dot_general x5, matrix products, dot(): return jnp.dot(a, b, preferred_element_type=f32)  37.1 us
    unnamed x113, local copies, waits for them, and re-layouts  18.9 us
  transfers between devices with their start and end apart: 2, of which 0 were waited for; matrix products, arithmetic and copies ran while one was open for 11% of the time, Pallas kernels for 30%

profile of v3, /device:TPU:0, one launch (start us, length us, event | category | flops | bytes accessed | tf_op | source)
XLA Modules:
  0.0 758.9 jit_solution(12480046515552114609)
XLA Ops:
  8.6 1.3 copy.30
  15.3 25.8 %load_attn.1 = (bf16[8,64,256]{2,1,0:T(8,128)(2,1)S(1)}, bf16[8,64,256]{2,1,0:T(8,128)(2,1)S(1)}, bf16[8,64,256]{2,1,0:T(8,128)(2,1)S(1)}, s32[8,8,128]{2,1,0:T(8,128)S(1)}, f32[8,8,256]{2,1,0:T(8,128)S(1)}) custom-call(bf16[256,2048]{1,0:T(8,128)(2,1)S(1)} %copy-done.11, bf16[256,2048]{1,0:T(8,128)(2,1)S(1)} %copy-done.12, ...), custom_call_target="tpu_custom_call" | custom-call | flops 28750000128 | bytes 90000000 | tf_op jit(solution)/shard_map/load_attn/pallas_call | solution.py:531
  41.1 81.7 %load_ffn.1 = (bf16[8,128,2048]{2,1,0:T(8,128)(2,1)}, bf16[8,64,1024]{2,1,0:T(8,128)(2,1)S(1)}, bf16[8,64,1024]{2,1,0:T(8,128)(2,1)S(1)}, bf16[4,8,64,768]{3,2,1,0:T(8,128)(2,1)}) custom-call(bf16[128,2048]{1,0:T(8,128)(2,1)S(1)} %copy.32.refs_0_, bf16[256,8192]{1,0:T(8,128)(2,1)} %refs_1_.3, bf16[256,8192]{1,0:T(8,128)(2,1)} %refs_2_.3, ...), custom_call_target="tpu_custom_call" | custom-call | flops 92000002048 | bytes 288000000 | tf_op jit(solution)/shard_map/load_ffn/pallas_call | solution.py:531
  124.8 3.1 fusion.4
  128.9 1.9 fusion.19
  130.9 8.9 %fusion.12.lin = f32[1024,768]{1,0:T(8,128)} fusion(bf16[2048,768]{1,0:T(8,128)(2,1)} %bitcast.140, bf16[1024,2048]{1,0:T(8,128)(2,1)} %bitcast.103, f32[2048]{0:T(1024)S(1)} %mul.149, f32[1024]{0:T(1024)S(1)} %add_rsqrt_fusion), kind=kOutput, calls=%fused_computation.29 | convolution fusion | flops 3229614080 | bytes 10498048 | tf_op jit(solution)/shard_map/dot_general | solution.py:22
  140.1 7.6 %attention.1 = (bf16[1024,256]{1,0:T(8,128)(2,1)S(1)}, bf16[1024,768]{1,0:T(8,128)(2,1)S(1)}) custom-call(f32[1024,768]{1,0:T(8,128)} %fusion.12.lin, f32[1024,128]{1,0:T(8,128)S(1)} %get-tuple-element.163.cosine, f32[1024,128]{1,0:T(8,128)S(1)} %get-tuple-element.164.sine, s32[1024,1]{1,0:T(8,128)S(1)} %copy.34.piece), custom_call_target="tpu_custom_call" | custom-call | flops 536870912 | bytes 6291456 | tf_op jit(solution)/shard_map/attention/pallas_call | solution.py:592
  147.8 3.3 convolution_convert_fusion.1
  151.2 59.5 %attn_out.1 = (f32[128,2048]{1,0:T(8,128)S(1)}, bf16[4,8,64,1024]{3,2,1,0:T(8,128)(2,1)}, bf16[4,8,64,1024]{3,2,1,0:T(8,128)(2,1)}) custom-call(bf16[8,128,2048]{2,1,0:T(8,128)(2,1)} %bitcast.99, bf16[8,64,1024]{2,1,0:T(8,128)(2,1)S(1)} %copy-done.24, bf16[8,64,1024]{2,1,0:T(8,128)(2,1)S(1)} %copy-done.26), custom_call_target="tpu_custom_call" | custom-call | flops 57500000256 | bytes 180000000 | tf_op jit(solution)/shard_map/attn_out/pallas_call | solution.py:531
  212.9 2.0 copy.35
  214.9 1.9 copy.36
  216.8 2.0 copy.37.refs_0_
  219.9 42.3 %gather_n2.1 = (bf16[8,128,2048]{2,1,0:T(8,128)(2,1)S(1)}, bf16[4,8,64,1024]{3,2,1,0:T(8,128)(2,1)}, bf16[4,8,64,1024]{3,2,1,0:T(8,128)(2,1)}) custom-call(bf16[128,2048]{1,0:T(8,128)(2,1)S(1)} %copy-done.10, bf16[4,8,64,1024]{3,2,1,0:T(8,128)(2,1)} %get-tuple-element.115.refs_1_, ...), custom_call_target="tpu_custom_call", output_to_operand_aliasing={{1}: (1, {}), {2}: (2, {})} | custom-call | flops 46000001024 | bytes 144000000 | tf_op jit(solution)/shard_map/gather_n2/pallas_call | solution.py:531
  262.2 2.0 copy-done.15
  264.2 8.3 %fusion.26 = f32[1024,1024]{0,1:T(8,128)} fusion(bf16[1024,2048]{1,0:T(8,128)(2,1)S(1)} %bitcast.92, bf16[2048,1024]{1,0:T(8,128)(2,1)} %bitcast.136), kind=kOutput, calls=%fused_computation.66 | convolution fusion | flops 4294967296 | bytes 12582912 | tf_op jit(solution)/shard_map/dot_general | solution.py:22
  272.5 10.1 %fusion.27 = f32[1024,1024]{0,1:T(8,128)} fusion(bf16[1024,2048]{1,0:T(8,128)(2,1)} %all-gather.2.cloned.1.call-done, bf16[1024,2048]{1,0:T(8,128)(2,1)} %param.30), kind=kOutput, calls=%fused_computation.67 | convolution fusion | flops 4294967296 | bytes 12582912 | tf_op jit(solution)/shard_map/dot_general | solution.py:26
  282.6 10.4 %multiply_convert_fusion.1 = (bf16[1024,1024]{0,1:T(8,128)(2,1)}, bf16[1024,1024]{0,1:T(8,128)(2,1)}, bf16[1024,1024]{0,1:T(8,128)(2,1)}) fusion(f32[1024,1024]{0,1:T(8,128)} %fusion.27, f32[1024,1024]{0,1:T(8,128)} %fusion.26, bf16[1024,2048]{1,0:T(8,128)(2,1)S(1)} %bitcast.93, bf16[2048,1024]{1,0:T(8,128)(2,1)S(1)} %bitcast.134), kind=kOutput, calls=%fused_computation.14 | convolution fusion | flops 4310695936 | bytes 23068672 | tf_op jit(solution)/shard_map/dot_general | solution.py:22
  293.0 8.6 %fusion.28 = f32[1024,2048]{1,0:T(8,128)} fusion(bf16[1024,1024]{0,1:T(8,128)(2,1)} %get-tuple-element.143, bf16[2048,1024]{1,0:T(8,128)(2,1)S(1)} %bitcast.135), kind=kOutput, calls=%fused_computation.68 | convolution fusion | flops 4294967296 | bytes 14680064 | tf_op jit(solution)/shard_map/dot_general | solution.py:26
  301.6 22.1 %convolution_convert_fusion = bf16[2048,2048]{1,0:T(8,128)(2,1)} fusion(bf16[1024,2048]{1,0:T(8,128)(2,1)S(1)} %bitcast.94, bf16[1024,1024]{0,1:T(8,128)(2,1)S(1)} %copy-done.55, bf16[1024,1024]{0,1:T(8,128)(2,1)S(1)} %copy-done.54), kind=kOutput, calls=%fused_computation.8 | convolution fusion | flops 8602517504 | bytes 16777216 | tf_op jit(solution)/shard_map/dot_general | solution.py:30
  323.7 11.8 %add_convert_fusion = bf16[1024,2048]{1,0:T(8,128)(2,1)} fusion(f32[1024,2048]{1,0:T(8,128)} %fusion.28, bf16[1024,1024]{0,1:T(8,128)(2,1)} %get-tuple-element.144, bf16[2048,1024]{1,0:T(8,128)(2,1)} %bitcast.137), kind=kOutput, calls=%fused_computation.7 | convolution fusion | flops 4299161600 | bytes 18874368 | tf_op jit(solution)/shard_map/dot_general | solution.py:26
  336.2 2.2 copy-done.17
  338.3 44.4 %scatter_gn2.1 = f32[128,2048]{1,0:T(8,128)S(1)} custom-call(bf16[8,128,2048]{2,1,0:T(8,128)(2,1)S(1)} %bitcast.95), custom_call_target="tpu_custom_call" | custom-call | flops 50600001536 | bytes 158400000 | tf_op jit(solution)/shard_map/scatter_gn2/pallas_call | solution.py:531
  383.7 2.5 copy.38
  386.2 2.3 copy.39
  388.6 2.6 copy.40
  391.1 2.0 multiply_reduce_fusion
  393.2 2.0 fusion.21.refs_0_
  395.2 8.1 %convolution_convert_fusion.2 = bf16[1024,2048]{1,0:T(8,128)(2,1)} fusion(bf16[1024,1024]{0,1:T(8,128)(2,1)} %get-tuple-element.145, bf16[1024,2048]{1,0:T(8,128)(2,1)S(1)} %copy-done.51), kind=kOutput, calls=%fused_computation.19 | convolution fusion | flops 4297064448 | bytes 10485760 | tf_op jit(solution)/shard_map/dot_general | solution.py:30
  403.3 52.5 %gather_ga.1 = (bf16[8,128,2048]{2,1,0:T(8,128)(2,1)S(1)}, bf16[256,2048]{1,0:T(8,128)(2,1)S(1)}) custom-call(bf16[128,2048]{1,0:T(8,128)(2,1)S(1)} %fusion.21.refs_0_, bf16[4,256,2048]{2,1,0:T(8,128)(2,1)} %bitcast.139), custom_call_target="tpu_custom_call" | custom-call | flops 46000001024 | bytes 144000000 | tf_op jit(solution)/shard_map/gather_ga/pallas_call | solution.py:531
  458.1 7.4 attention_back.1
  465.6 7.5 fusion.3
  473.9 11.3 %gain_sum.1 = f32[8,256]{1,0:T(8,128)} custom-call(f32[8,8,256]{2,1,0:T(8,128)} %scatter.32.g), custom_call_target="tpu_custom_call" | custom-call | tf_op jit(solution)/shard_map/gain_sum/pallas_call | solution.py:720
  485.2 1.4 fusion.25
  486.6 4.4 convolution_convert_fusion.5
  491.1 5.4 convolution_convert_fusion.4
  496.6 6.2 convolution_convert_fusion.3
  504.0 88.1 %scatter_gn1.1 = (f32[128,2048]{1,0:T(8,128)S(1)}, bf16[2,64,8192]{2,1,0:T(8,128)(2,1)}, bf16[4,256,2048]{2,1,0:T(8,128)(2,1)}, bf16[64,2048]{1,0:T(8,128)(2,1)S(1)}, bf16[512,768]{1,0:T(8,128)(2,1)S(1)}) custom-call(bf16[8,128,2048]{2,1,0:T(8,128)(2,1)} %bitcast.133, bf16[8,64,2048]{2,1,0:T(8,128)(2,1)} %bitcast.132, bf16[256,2048]{1,0:T(8,128)(2,1)S(1)} %copy-done.22, ...), custom_call_target="tpu_custom_call" | custom-call | flops 92000002048 | bytes 288000000 | tf_op jit(solution)/shard_map/scatter_gn1/pallas_call | solution.py:531
  592.2 1.6 copy-done.27
  593.8 96.8 %rows_ffn.1 = (f32[128,2048]{1,0:T(8,128)S(1)}, bf16[3,64,2048]{2,1,0:T(8,128)(2,1)S(1)}, bf16[4,2,64,8192]{3,2,1,0:T(8,128)(2,1)}, bf16[4,64,2048]{2,1,0:T(8,128)(2,1)S(1)}) custom-call(bf16[8,128,2048]{2,1,0:T(8,128)(2,1)} %bitcast.138, bf16[8,64,768]{2,1,0:T(8,128)(2,1)S(1)} %bitcast.97, bf16[2,64,8192]{2,1,0:T(8,128)(2,1)S(1)} %copy-done.27, ...), custom_call_target="tpu_custom_call" | custom-call | flops 86249996288 | bytes 270000000 | tf_op jit(solution)/shard_map/rows_ffn/pallas_call | solution.py:531
  691.4 11.9 %fusion.22 = (f32[4,1,64,8192]{3,2,1,0:T(8,128)}, f32[4,1,64,8192]{3,2,1,0:T(8,128)}) fusion(bf16[4,2,64,8192]{3,2,1,0:T(8,128)(2,1)} %get-tuple-element.133), kind=kLoop, calls=%fused_computation.62 | loop fusion | bytes 33554432 | tf_op jit(solution)/shard_map/slice | solution.py:926
  703.3 28.6 %rows_attn.1 = bf16[4,192,2048]{2,1,0:T(8,128)(2,1)S(1)} custom-call(bf16[192,2048]{1,0:T(8,128)(2,1)S(1)} %bitcast.98), custom_call_target="tpu_custom_call" | custom-call | flops 32199999488 | bytes 100800000 | tf_op jit(solution)/shard_map/rows_attn/pallas_call | solution.py:531
  731.9 2.9 fusion.23
  734.8 1.6 bitcast_convert_fusion.1
  737.8 2.3 copy.43
  740.1 1.6 copy.44
  741.7 1.3 fusion.14
  743.1 6.8 bitcast_convert_fusion
  750.0 1.7 fusion.17
  (146 shorter events, 21.7 us)
Async XLA Ops:
  7.2 140.7 %copy-start = (bf16[256,2048]{1,0:T(8,128)(2,1)S(1)}, bf16[256,2048]{1,0:T(8,128)(2,1)}, u32[]{:S(2)}) copy-start(bf16[256,2048]{1,0:T(8,128)(2,1)} %param.27) | copy-start | bytes 3145732
  7.2 265.3 %all-gather.2.cloned.1.call-start = ((), (), s32[]{:S(2)}) async-start(), calls=%async_computation.1 | async-start | bytes 4718592 | tf_op jit(solution)/shard_map/all_gather | solution.py:833
  124.8 378.0 %reduce-scatter.2.cloned.1.call-start = ((), (), s32[]{:S(2)}) async-start(), calls=%async_computation.2 | async-start | bytes 10485760 | tf_op jit(solution)/shard_map/reduce_scatter | solution.py:781
  127.9 11.9 %copy-start.45 = (f32[1024]{0:T(1024)}, f32[1024]{0:T(1024)S(1)}, u32[]{:S(2)}) copy-start(f32[1024]{0:T(1024)S(1)} %add_rsqrt_fusion) | copy-start | bytes 12292
  128.5 82.4 %copy-start.36 = (f32[8,1,256]{2,1,0:T(1,128)}, f32[8,1,256]{2,1,0:T(1,128)S(1)}, u32[]{:S(2)}) copy-start(f32[8,1,256]{2,1,0:T(1,128)S(1)} %get-tuple-element.154) | copy-start | bytes 24580
  128.7 11.1 %copy-start.40 = (f32[2048]{0:T(1024)}, f32[2048]{0:T(1024)S(1)}, u32[]{:S(2)}) copy-start(f32[2048]{0:T(1024)S(1)} %mul.149) | copy-start | bytes 24580
  140.1 11.0 %copy-start.1 = (f32[1024,128]{1,0:T(8,128)}, f32[1024,128]{1,0:T(8,128)S(1)}, u32[]{:S(2)}) copy-start(f32[1024,128]{1,0:T(8,128)S(1)} %get-tuple-element.163.cosine) | copy-start | bytes 1572868
  140.1 11.0 %copy-start.3 = (f32[1024,128]{1,0:T(8,128)}, f32[1024,128]{1,0:T(8,128)S(1)}, u32[]{:S(2)}) copy-start(f32[1024,128]{1,0:T(8,128)S(1)} %get-tuple-element.164.sine) | copy-start | bytes 1572868
  147.8 3.3 copy-start.7
  147.8 3.3 copy-start.24
  147.8 3.3 copy-start.26
  151.1 59.5 %copy-start.31 = (bf16[128,2048]{1,0:T(8,128)(2,1)S(1)}, bf16[128,2048]{1,0:T(8,128)(2,1)}, u32[]{:S(2)}) copy-start(bf16[128,2048]{1,0:T(8,128)(2,1)} %param.23) | copy-start | bytes 1572868
  262.2 2.0 copy-start.15
  272.5 10.1 %copy-start.16 = (bf16[8,128,2048]{2,1,0:T(8,128)(2,1)S(1)}, bf16[8,128,2048]{2,1,0:T(8,128)(2,1)}, u32[]{:S(2)}) copy-start(bf16[8,128,2048]{2,1,0:T(8,128)(2,1)} %copy-done.15) | copy-start | bytes 12582916
  272.5 10.1 %copy-start.52 = (bf16[4,8,64,1024]{3,2,1,0:T(8,128)(2,1)S(1)}, bf16[4,8,64,1024]{3,2,1,0:T(8,128)(2,1)}, u32[]{:S(2)}) copy-start(bf16[4,8,64,1024]{3,2,1,0:T(8,128)(2,1)} %get-tuple-element.118) | copy-start | bytes 12582916
  293.0 8.6 %copy-start.54 = (bf16[1024,1024]{0,1:T(8,128)(2,1)S(1)}, bf16[1024,1024]{0,1:T(8,128)(2,1)}, u32[]{:S(2)}) copy-start(bf16[1024,1024]{0,1:T(8,128)(2,1)} %get-tuple-element.143) | copy-start | bytes 6291460
  293.0 8.6 %copy-start.55 = (bf16[1024,1024]{0,1:T(8,128)(2,1)S(1)}, bf16[1024,1024]{0,1:T(8,128)(2,1)}, u32[]{:S(2)}) copy-start(bf16[1024,1024]{0,1:T(8,128)(2,1)} %get-tuple-element.144) | copy-start | bytes 6291460
  336.1 2.2 copy-start.17
  383.7 7.4 copy-start.37
  383.7 7.4 copy-start.43
  391.1 4.1 copy-start.51
  393.2 10.1 %copy-start.48 = (f32[128]{0:T(128)}, f32[128]{0:T(128)S(1)}, u32[]{:S(2)}) copy-start(f32[128]{0:T(128)S(1)} %broadcast_multiply_fusion.1) | copy-start | bytes 1540
  455.7 2.0 copy-start.14
  455.7 2.3 copy-start.21
  455.8 2.3 copy-start.2
  455.8 2.3 copy-start.4
  458.1 7.4 copy-start.34
  458.1 7.4 copy-start.46
  465.5 7.5 copy-start.5
  465.6 21.1 %copy-start.8 = (bf16[1024,256]{1,0:T(8,128)(2,1)S(1)}, bf16[1024,256]{1,0:T(8,128)(2,1)}, u32[]{:S(2)}) copy-start(bf16[1024,256]{1,0:T(8,128)(2,1)} %copy-done.7) | copy-start | bytes 1572868
  473.1 18.0 %copy-start.41 = (f32[2048]{0:T(1024)S(1)}, f32[2048]{0:T(1024)}, u32[]{:S(2)}) copy-start(f32[2048]{0:T(1024)} %copy-done.40) | copy-start | bytes 24580
  473.1 18.0 %copy-start.6 = (bf16[1024,768]{1,0:T(8,128)(2,1)S(1)}, bf16[1024,768]{1,0:T(8,128)(2,1)}, u32[]{:S(2)}) copy-start(bf16[1024,768]{1,0:T(8,128)(2,1)} %copy-done.5) | copy-start | bytes 4718596
  485.2 5.9 copy-start.35
  491.1 5.5 copy-start.50
  491.1 5.5 copy-start.53
  496.6 6.2 copy-start.18
  502.8 1.2 copy-start.22
  592.2 1.6 copy-start.27
  691.4 11.9 %copy-start.20 = (bf16[3,64,2048]{2,1,0:T(8,128)(2,1)S(1)}, bf16[3,64,2048]{2,1,0:T(8,128)(2,1)}, u32[]{:S(2)}) copy-start(bf16[3,64,2048]{2,1,0:T(8,128)(2,1)} %copy-done.19) | copy-start | bytes 2359300
  734.8 6.8 copy-start.39
  734.8 6.8 copy-start.47
  743.0 6.9 copy-start.29
  743.0 6.9 copy-start.30
  743.0 6.9 copy-start.32
  743.1 6.9 copy-start.33
  743.1 6.9 copy-start.38
  743.1 6.9 copy-start.44
  743.1 6.9 copy-start.49
  (10 other events, 10.5 us)
Sparse Core Ops, SparseCore 0:
  124.9 52.7 all-gather.1
  335.7 97.4 reduce-scatter.1

commit v4 on v3

--- a/solution.py
+++ b/solution.py
@@ -57,7 +57,7 @@
     pl.semaphore_signal(sem, inc=1, device_id={axis: to}, device_id_type=pl.DeviceIdType.MESH)
 
 
-def line_body(n, n_ag, n_rs, a2a_blocks, spreads, n_sum, parts, *refs):
+def line_body(n, n_ag, n_rs, a2a_blocks, spreads, n_sum, chain, chain_at, parts, *refs):
     refs = list(refs)
     nz = n // 2
     n_a2a = len(a2a_blocks)
@@ -66,11 +66,13 @@
     ag_in, rs_in, a2a_in = take(n_ag), take(n_rs), [take(t[0]) for t in a2a_blocks]
     sp_in, sum_in = take(n_sp), take(n_sum)
     ag_out, rs_out, a2a_out, sp_out, sum_out = take(n_ag), take(n_rs), take(n_a2a), take(n_sp), take(n_sum)
+    chain_out = take(len(chain))
     ag_sem = [take(7) for _ in range(n_ag)]
     rs_scr = [take(9) for _ in range(n_rs)]
     a2a_sem = [take(3) for _ in range(n_a2a)]
     sp_sem = [take(5) for _ in range(n_sp)]
     sum_scr = [take(6) for _ in range(n_sum)]
+    chain_sem = [take(5) for _ in chain]
     me = lax.axis_index("inner")
     z, c = me // 2, lax.rem(me, 2)
     sib = me + 1 - 2 * c
@@ -78,7 +80,7 @@
     across_x, across_y = r + 1 - 2 * lax.rem(r, 2), r + 2 - 4 * (r // 2)
     barrier = pltpu.get_barrier_semaphore()
     more = 0
-    if n_sp + n_sum:
+    if n_sp + n_sum + len(chain):
         signal(barrier, across_x, "replica")
         signal(barrier, across_y, "replica")
         more = 2
@@ -302,19 +304,20 @@
     class Exchange:
         def __init__(self, src, dst, sems, blocks):
             self.src, self.dst = src, dst
-            self.own_sem, self.send, self.recv = sems
-            _, self.src_of, self.dst_of, self.count = blocks
+            self.own_sem, self.sent, self.recv = sems
+            _, self.src_of, self.dst_of, self.count, self.late = blocks
+            self.arrived = False
 
         def to(self, k, m):
             other = lax.rem(me + k, n)
             return rcopy(
-                self.src_of(self.src, other, m), self.dst_of(self.dst, me, m), self.send.at[k, m], self.recv.at[k, m], other
+                self.src_of(self.src, other, m), self.dst_of(self.dst, me, m), self.sent.at[k, m], self.recv.at[k, m], other
             )
 
         def came(self, k, m):
             other = lax.rem(me - k + n, n)
             return rcopy(
-                self.src_of(self.src, other, m), self.dst_of(self.dst, other, m), self.send.at[k, m], self.recv.at[k, m], other
+                self.src_of(self.src, other, m), self.dst_of(self.dst, other, m), self.sent.at[k, m], self.recv.at[k, m], other
             )
 
         def own(self, m):
@@ -322,22 +325,37 @@
                 self.src_of(self.src, me, m), self.dst_of(self.dst, me, m), self.own_sem.at[m]
             )
 
+        def send(self, first, last):
+            for k in range(first, last):
+                for m in range(self.count):
+                    self.to(k, m).start()
+
         def begin(self):
+            if not self.late:
+                self.send(1, n)
+            for m in range(self.count):
+                self.own(m).start()
+
+        def step(self, s, j):
+            pass
+
+        def after_step(self, s):
+            if self.late:
+                self.send(1 + (n - 1) * (s - 1) // (nz - 1), 1 + (n - 1) * s // (nz - 1))
+
+        def arrive(self):
+            if not self.arrived:
+                self.arrived = True
+                for m in range(self.count):
+                    self.own(m).wait()
+                for k in range(1, n):
+                    for m in range(self.count):
+                        self.came(k, m).wait_recv()
+
+        def end(self):
+            self.arrive()
             for k in range(1, n):
                 for m in range(self.count):
-                    self.to(k, m).start()
-            for m in range(self.count):
-                self.own(m).start()
-
-        def step(self, s, j):
-            pass
-
-        def end(self):
-            for m in range(self.count):
-                self.own(m).wait()
-            for k in range(1, n):
-                for m in range(self.count):
-                    self.came(k, m).wait_recv()
                     self.to(k, m).wait_send()
 
     class Spread:
@@ -478,29 +496,51 @@
 
     square_parts = [Spread(*t) for t in zip(sp_in, sp_out, sp_sem, spreads)]
     square_parts += [Sum(*t) for t in zip(sum_in, sum_out, sum_scr)]
+    exchanges = parts_of[n_ag + n_rs :]
+    chained = [Spread(a2a_out[i], out, sems, (1, 2)) for i, out, sems in zip(chain, chain_out, chain_sem)]
+
+    def begin_chain():
+        for i, part in zip(chain, chained):
+            exchanges[i].arrive()
+            part.begin()
+
     parts_of += square_parts
     for part in parts_of:
         part.begin()
     if n_ag + n_rs:
+        if chain_at == 0:
+            begin_chain()
         for s in range(1, nz):
             @pl.loop(0, parts)
             def _(j):
                 for part in parts_of:
                     part.step(s, j)
 
-            if s == nz - 2:
+            for part in exchanges:
+                part.after_step(s)
+            if s == chain_at:
+                begin_chain()
+            if s == max(1, chain_at):
                 for part in square_parts:
                     part.mid()
     else:
+        begin_chain()
         for part in square_parts:
             part.mid()
+    if chained:
+        for part in parts_of[: n_ag + n_rs]:
+            part.end()
+        for part in chained:
+            part.mid()
+        parts_of = parts_of[n_ag + n_rs :] + chained
     for part in parts_of:
         part.end()
 
 
-def line_comm(cid, name, us, ag=(), rs=(), a2a=(), spread=(), sums=(), parts=2):
+def line_comm(cid, name, us, ag=(), rs=(), a2a=(), spread=(), sums=(), chain=(), chain_at=None, parts=2):
     n = lax.axis_size("inner")
     nz = n // 2
+    chain_at = nz - 2 if chain_at is None else chain_at
     dma = pltpu.SemaphoreType.DMA
     hbm = pl.BlockSpec(memory_space=pl.ANY)
     vmem = pl.BlockSpec(memory_space=pltpu.VMEM)
@@ -510,6 +550,7 @@
     out_shape += [jax.ShapeDtypeStruct(t[1], t[0][0].dtype) for t in a2a]
     out_shape += [jax.ShapeDtypeStruct(b.shape if 1 not in ph else (4,) + b.shape, b.dtype) for b, ph in spread]
     out_shape += [jax.ShapeDtypeStruct((p.shape[0] // 4, p.shape[1]), bf16) for p in sums]
+    out_shape += [jax.ShapeDtypeStruct((4,) + a2a[i][1], a2a[i][0][0].dtype) for i in chain]
     sums = [p.reshape((4, p.shape[0] // 4) + p.shape[1:]) for p in sums]
     first_in = len(ag) + len(rs) + sum(len(t[0]) for t in a2a)
     first_out = len(ag) + len(rs) + len(a2a)
@@ -528,11 +569,13 @@
         half = (p.shape[1] // 2, p.shape[2])
         scratch += [pltpu.VMEM((2, 2) + half, bf16), pltpu.VMEM((2,) + half, bf16)]
         scratch += [dma((2, 2)), dma((2, 2)), dma((2,)), dma((2,))]
+    for _ in chain:
+        scratch += [dma, dma((2,)), dma((2,)), dma((2,)), dma((2,))]
     outs = pl.pallas_call(
-        functools.partial(line_body, n, len(ag), len(rs), [(len(t[0]),) + t[2:5] for t in a2a], [ph for _, ph in spread], len(sums), parts),
+        functools.partial(line_body, n, len(ag), len(rs), [(len(t[0]),) + t[2:6] for t in a2a], [ph for _, ph in spread], len(sums), chain, chain_at, parts),
         out_shape=out_shape,
         in_specs=[hbm] * len(ag) + [vmem] * len(rs) + [hbm] * (sum(len(t[0]) for t in a2a) + len(spread)) + [vmem] * len(sums),
-        out_specs=[hbm] * len(ag) + [vmem] * len(rs) + [hbm] * (len(a2a) + len(spread)) + [vmem] * len(sums),
+        out_specs=[hbm] * len(ag) + [vmem] * len(rs) + [hbm] * (len(a2a) + len(spread)) + [vmem] * len(sums) + [hbm] * len(chain),
         input_output_aliases=aliases,
         scratch_shapes=scratch,
         compiler_params=pltpu.CompilerParams(
@@ -668,73 +711,6 @@
     )(rot, go, cosine, sine, piece)
 
 
-def gain_body(n, nr, g, out, group, copies, ss, sr, cs, cr):
-    me, r = lax.axis_index("inner"), lax.axis_index("replica")
-    mesh_id = pl.DeviceIdType.MESH
-    barrier = pltpu.get_barrier_semaphore()
-    for k in range(1, n):
-        signal(barrier, lax.rem(me + k, n))
-    for k in range(1, nr):
-        pl.semaphore_signal(barrier, inc=1, device_id={"replica": lax.rem(r + k, nr)}, device_id_type=mesh_id)
-    pl.semaphore_wait(barrier, n + nr - 2)
-
-    def inside(k):
-        to = lax.rem(me + k, n)
-        return rcopy(g.at[to], group.at[k], ss.at[k], sr.at[k], to)
-
-    def across(k):
-        return pltpu.make_async_remote_copy(
-            src_ref=copies.at[0],
-            dst_ref=copies.at[k],
-            send_sem=cs.at[k],
-            recv_sem=cr.at[k],
-            device_id={"replica": lax.rem(r + k, nr)},
-            device_id_type=mesh_id,
-        )
-
-    for k in range(1, n):
-        inside(k).start()
-    total = g[me]
-    for k in range(1, n):
-        inside(k).wait_recv()
-        total = total + group[k]
-    copies[0] = total
-    for k in range(1, nr):
-        across(k).start()
-    for k in range(1, nr):
-        across(k).wait_recv()
-        total = total + copies[k]
-    out[...] = total
-    for k in range(1, n):
-        inside(k).wait_send()
-    for k in range(1, nr):
-        across(k).wait_send()
-
-
-def gain_sum(cid, parts):
-    n, nr = lax.axis_size("inner"), lax.axis_size("replica")
-    cols = parts.shape[1] // n
-    g = jnp.zeros((n, 8, cols), f32).at[:, :2].set(parts.reshape(2, n, cols).transpose(1, 0, 2))
-    dma = pltpu.SemaphoreType.DMA
-    vmem = pl.BlockSpec(memory_space=pltpu.VMEM)
-    return pl.pallas_call(
-        functools.partial(gain_body, n, nr),
-        out_shape=jax.ShapeDtypeStruct((8, cols), f32),
-        in_specs=[vmem],
-        out_specs=vmem,
-        scratch_shapes=[
-            pltpu.VMEM((n, 8, cols), f32),
-            pltpu.VMEM((nr, 8, cols), f32),
-            dma((n,)),
-            dma((n,)),
-            dma((nr,)),
-            dma((nr,)),
-        ],
-        compiler_params=pltpu.CompilerParams(collective_id=cid, has_side_effects=True),
-        name="gain_sum",
-    )(g)[:2]
-
-
 def columns_out(w):
     n, nr = lax.axis_size("inner"), lax.axis_size("replica")
     part = w.shape[0] // nr
@@ -744,25 +720,31 @@
         rows = pl.ds(pl.multiple_of(lax.axis_index("replica") * part, part), part)
         return refs[0].at[rows, pl.ds(pl.multiple_of(other * cols, cols), cols)]
 
-    return ((w,), (n, part, cols), source, lambda ref, other, m: ref.at[other], 1)
+    return ((w,), (n, part, cols), source, lambda ref, other, m: ref.at[other], 1, False)
 
 
 def to_all(block):
     n = lax.axis_size("inner")
-    return ((block,), (n,) + block.shape, lambda refs, other, m: refs[0], lambda ref, other, m: ref.at[other], 1)
-
-
-def rows_back(share, count):
-    n, part, width = share.shape
-    cols = width // count
+    return ((block,), (n,) + block.shape, lambda refs, other, m: refs[0], lambda ref, other, m: ref.at[other], 1, False)
+
+
+def rows_back(share, first, count, late=False):
+    n, part, _ = share.shape
+    cols = first[1]
 
     def source(refs, other, m):
-        return refs[0].at[other, :, pl.ds(m * cols, cols)]
+        return refs[0].at[other, :, pl.ds((first[0] + m) * cols, cols)]
 
     def target(ref, other, m):
-        return ref.at[m, :, pl.ds(pl.multiple_of(other * cols, cols), cols)]
-
-    return ((share,), (count, part, n * cols), source, target, count)
+        return ref.at[pl.ds(m * part, part), pl.ds(pl.multiple_of(other * cols, cols), cols)]
+
+    return ((share,), (count * part, n * cols), source, target, count, late)
+
+
+def sum_blocks(g):
+    n = lax.axis_size("inner")
+    cols = g.shape[1]
+    return ((g,), (n,) + (g.shape[0] // n, cols), lambda refs, other, m: refs[0].at[pl.ds(pl.multiple_of(other * 16, 16), 16)], lambda ref, other, m: ref.at[other], 1, False)
 
 
 def shares_first(x):
@@ -874,10 +856,12 @@
     ffn_gain_part = jnp.sum(gn2 * u2, axis=0)
     gmid = cotangent.astype(f32) + r2 * (gu2 - u2 * jnp.mean(gu2 * u2, axis=1, keepdims=True))
     if square:
-        ga, down_share = line_comm(5, "gather_ga", 40, ag=[gmid.astype(bf16)], sums=[g_down])
+        ga, down_share = line_comm(5, "gather_ga", 50, ag=[gmid.astype(bf16)], sums=[g_down])
     else:
         (ga,) = line_comm(5, "gather_ga", 40, ag=[gmid.astype(bf16)])
         down_share = sum_share(g_down)
+    ga, down_share, gu_share = after((ga, down_share, gu_share))
+    grad_down = join(down_share)
 
     go = dot_t(ga, w_out).astype(bf16)
     gqkv = attention_back(rot, go, cosine, sine, pieces)
@@ -886,27 +870,46 @@
     gn1_part = dot_t(gqkv, w_qkv)
     attn_gain_part = jnp.sum(gn1_part * u1, axis=0, keepdims=True)
     gn1_part = gn1_part.astype(bf16)
-    gu_back = rows_back(gu_share.reshape(n, -1, gu.shape[1]), 2)
-    mlp_part = dot(hid, w_down).astype(bf16)
+    gains = jnp.stack([owners_first(attn_gain_part)[0].reshape(n, rows), ffn_gain_part.reshape(n, rows)], axis=1)
+    gains = jnp.pad(gains, ((0, 0), (0, 14), (0, 0))).reshape(n * 16, rows)
+    cols = w_gate.shape[1] // n
+    head_cols = gqkv.shape[1] // 3
+    gu_share = gu_share.reshape(n, -1, 2 * cols)
     if square:
-        gn1, gu_rows, grad_down, out_share, qkv_share = line_comm(
-            6, "scatter_gn1", 80, rs=[gn1_part], a2a=[gu_back], spread=[(down_share, (1, 2))], sums=[g_out, g_qkv]
+        gn1, gate_rows, up_rows, gains, out_share, qkv_share, grad_gate = line_comm(
+            6,
+            "scatter_gn1",
+            1,
+            rs=[gn1_part],
+            a2a=[rows_back(gu_share, (0, cols), 1), rows_back(gu_share, (1, cols), 1, True), sum_blocks(gains)],
+            sums=[g_out, g_qkv],
+            chain=(0,),
+            chain_at=0,
         )
-        qkv_back = rows_back(qkv_share.reshape(n, -1, gqkv.shape[1]), 3)
-        mlp, qkv_rows, grad_gu, grad_out = line_comm(
-            7, "rows_ffn", 75, rs=[mlp_part], a2a=[qkv_back], spread=[(gu_rows, (1, 2)), (out_share, (1, 2))]
+        mlp_part, gains = dot(hid, w_down).astype(bf16), jnp.sum(gains, axis=0)
+        qkv_back = rows_back(qkv_share.reshape(n, -1, 3 * head_cols), (0, head_cols), 3)
+        mlp_part, grad_down = after((mlp_part, grad_down))
+        mlp, qkv_rows, grad_up, grad_out, gains, grad_qkv = line_comm(
+            7,
+            "rows_attn",
+            70,
+            rs=[mlp_part],
+            a2a=[qkv_back],
+            spread=[(up_rows, (1, 2)), (out_share, (1, 2)), (gains, (1, 2))],
+            chain=(0,),
+            chain_at=0,
         )
-        (grad_qkv,) = line_comm(8, "rows_attn", 28, spread=[(flat(qkv_rows), (1, 2))])
+        gains = jnp.sum(gains, axis=0)
     else:
-        gn1, gu_rows = line_comm(6, "scatter_gn1", 80, rs=[gn1_part], a2a=[gu_back])
-        qkv_back = rows_back(sum_share(g_qkv).reshape(n, -1, gqkv.shape[1]), 3)
-        mlp, qkv_rows = line_comm(7, "rows_ffn", 75, rs=[mlp_part], a2a=[qkv_back])
-        grad_gu, grad_out, grad_down, grad_qkv = join(gu_rows), join(sum_share(g_out)), join(down_share), join(qkv_rows)
+        gu_back = rows_back(gu_share, (0, cols), 2)
+        gn1, gu_rows, gains = line_comm(6, "scatter_gn1", 80, rs=[gn1_part], a2a=[gu_back, sum_blocks(gains)])
+        gains = lax.psum(jnp.sum(gains, axis=0), "replica")
+        qkv_back = rows_back(sum_share(g_qkv).reshape(n, -1, 3 * head_cols), (0, head_cols), 3)
+        mlp_part = dot(hid, w_down).astype(bf16)
+        mlp, qkv_rows = line_comm(7, "rows_attn", 75, rs=[mlp_part], a2a=[qkv_back])
+        grad_gu = join(gu_rows).reshape(nr, 2, -1, n * cols)
+        grad_gate, grad_up, grad_out, grad_qkv = grad_gu[:, 0], grad_gu[:, 1], join(sum_share(g_out)), join(qkv_rows)
     output = (mid + mlp).astype(bf16)
-    gain_rows = gain_sum(9, jnp.stack([owners_first(attn_gain_part)[0], ffn_gain_part]))
-    grad_down = grad_down.reshape(w_down.shape).astype(f32)
-    grad_out = grad_out.reshape(w_out.shape).astype(f32)
-    grad_gu = grad_gu.astype(f32)
     grad_qkv = grad_qkv.reshape(nr, 3, -1, width).astype(f32)
 
     gn1 = owners_first(gn1)
@@ -921,12 +924,12 @@
         grad_qkv[:, 0].reshape(w_query.shape),
         grad_qkv[:, 1].reshape(w_key.shape),
         grad_qkv[:, 2].reshape(w_value.shape),
-        grad_out,
-        grad_gu[:, 0].reshape(w_gate.shape),
-        grad_gu[:, 1].reshape(w_up.shape),
-        grad_down,
-        gain_rows[0],
-        gain_rows[1],
+        grad_out.reshape(w_out.shape).astype(f32),
+        grad_gate.reshape(w_gate.shape).astype(f32),
+        grad_up.reshape(w_up.shape).astype(f32),
+        grad_down.reshape(w_down.shape).astype(f32),
+        gains[0],
+        gains[1],
     )
 
 

time: 768 us -> 718 us (0.935)
  Pallas kernels: 546 us -> 502 us
  other arithmetic: 23.4 us -> 36.9 us
  local copies, waits for them, and re-layouts: 57.9 us -> 44.9 us
  matrix products: 117 us -> 109 us
    pallas_call x9 -> x8, Pallas kernels: 520 us -> 487 us  [line_comm(): pl.pallas_call(functools.partial(line_body, n, len(ag), len(rs), [(len(t[...]
    convert_element_type x2 -> x4, other arithmetic: 8.44 us -> 21.7 us  [the longest x1 6.81 us: local(): grad_down.reshape(w_down.shape).astype(f32)]
    slice x2 -> x1, local copies, waits for them, and re-layouts: 13.3 us -> 0.57 us  [local(): gains[1]]
    pallas_call x1 -> x0, Pallas kernels: 11.3 us -> none  [gain_sum(): pl.pallas_call(functools.partial(gain_body, n, nr), out_shape=jax.ShapeDt...]
    dot_general x4, matrix products: 40.1 us -> 31.5 us  [t_dot(): return lax.dot_general(a, b, dims_cols, preferred_element_type=f32)]
    unnamed x113 -> x112, local copies, waits for them, and re-layouts: 18.9 us -> 19.4 us
  transfers between devices with their start and end apart: 2 -> 3, of which waited for: 0 -> 0; matrix products, arithmetic and copies ran while one was open for 11% -> 13% of each run, Pallas kernels for 30% -> 43%
where the time goes in v4:
time: 718 us; the launch traced here: 708 us
  Pallas kernels  502 us (70%)
  matrix products  109 us (15%)
  local copies, waits for them, and re-layouts  44.9 us (6%)
  other arithmetic  36.9 us (5%)
  between operations  14.6 us (2%)
    pallas_call x8, Pallas kernels, line_comm(): pl.pallas_call(functools.partial(line_body, n, len(ag), len(rs), [(len(t[...  487 us
    dot_general x5, matrix products, dot(): return jnp.dot(a, b, preferred_element_type=f32)  40.5 us
    dot_general x5, matrix products, dot_t(): return lax.dot_general(a, b, dims_rows, preferred_element_type=f32)  36.9 us
    dot_general x4, matrix products, t_dot(): return lax.dot_general(a, b, dims_cols, preferred_element_type=f32)  31.5 us
    unnamed x112, local copies, waits for them, and re-layouts  19.4 us
  transfers between devices with their start and end apart: 3, of which 0 were waited for; matrix products, arithmetic and copies ran while one was open for 13% of the time, Pallas kernels for 43%

profile of v4, /device:TPU:0, one launch (start us, length us, event | category | flops | bytes accessed | tf_op | source)
XLA Modules:
  0.0 707.7 jit_solution(3158490160625689342)
XLA Ops:
  8.6 1.3 copy.46
  15.3 25.8 %load_attn.1 = (bf16[8,64,256]{2,1,0:T(8,128)(2,1)S(1)}, bf16[8,64,256]{2,1,0:T(8,128)(2,1)S(1)}, bf16[8,64,256]{2,1,0:T(8,128)(2,1)S(1)}, s32[8,8,128]{2,1,0:T(8,128)S(1)}, f32[8,8,256]{2,1,0:T(8,128)S(1)}) custom-call(bf16[256,2048]{1,0:T(8,128)(2,1)S(1)} %copy-done.12, bf16[256,2048]{1,0:T(8,128)(2,1)S(1)} %copy-done.13, ...), custom_call_target="tpu_custom_call" | custom-call | flops 28750000128 | bytes 90000000 | tf_op jit(solution)/shard_map/load_attn/pallas_call | solution.py:574
  41.1 81.7 %load_ffn.1 = (bf16[8,128,2048]{2,1,0:T(8,128)(2,1)}, bf16[8,64,1024]{2,1,0:T(8,128)(2,1)S(1)}, bf16[8,64,1024]{2,1,0:T(8,128)(2,1)S(1)}, bf16[4,8,64,768]{3,2,1,0:T(8,128)(2,1)}) custom-call(bf16[128,2048]{1,0:T(8,128)(2,1)S(1)} %copy.48.refs_0_, bf16[256,8192]{1,0:T(8,128)(2,1)} %refs_1_.3, bf16[256,8192]{1,0:T(8,128)(2,1)} %refs_2_.3, ...), custom_call_target="tpu_custom_call" | custom-call | flops 92000002048 | bytes 288000000 | tf_op jit(solution)/shard_map/load_ffn/pallas_call | solution.py:574
  124.8 3.1 fusion.4
  129.0 1.9 fusion.19
  130.9 8.9 %fusion.12.lin = f32[1024,768]{1,0:T(8,128)} fusion(bf16[2048,768]{1,0:T(8,128)(2,1)} %bitcast.142, bf16[1024,2048]{1,0:T(8,128)(2,1)} %bitcast.107, f32[2048]{0:T(1024)S(1)} %mul.149, f32[1024]{0:T(1024)S(1)} %add_rsqrt_fusion), kind=kOutput, calls=%fused_computation.31 | convolution fusion | flops 3229614080 | bytes 10498048 | tf_op jit(solution)/shard_map/dot_general | solution.py:22
  140.2 7.7 %attention.1 = (bf16[1024,256]{1,0:T(8,128)(2,1)S(1)}, bf16[1024,768]{1,0:T(8,128)(2,1)S(1)}) custom-call(f32[1024,768]{1,0:T(8,128)} %fusion.12.lin, f32[1024,128]{1,0:T(8,128)S(1)} %get-tuple-element.163.cosine, f32[1024,128]{1,0:T(8,128)S(1)} %get-tuple-element.164.sine, s32[1024,1]{1,0:T(8,128)S(1)} %copy.50.piece), custom_call_target="tpu_custom_call" | custom-call | flops 536870912 | bytes 6291456 | tf_op jit(solution)/shard_map/attention/pallas_call | solution.py:635
  147.9 3.3 convolution_convert_fusion.1
  151.2 59.5 %attn_out.1 = (f32[128,2048]{1,0:T(8,128)S(1)}, bf16[4,8,64,1024]{3,2,1,0:T(8,128)(2,1)}, bf16[4,8,64,1024]{3,2,1,0:T(8,128)(2,1)}) custom-call(bf16[8,128,2048]{2,1,0:T(8,128)(2,1)} %bitcast.101, bf16[8,64,1024]{2,1,0:T(8,128)(2,1)S(1)} %copy-done.23, bf16[8,64,1024]{2,1,0:T(8,128)(2,1)S(1)} %copy-done.25), custom_call_target="tpu_custom_call" | custom-call | flops 57500000256 | bytes 180000000 | tf_op jit(solution)/shard_map/attn_out/pallas_call | solution.py:574
  212.9 2.0 copy.51
  214.9 1.9 copy.52
  216.8 2.0 copy.53.refs_0_
  219.9 42.3 %gather_n2.1 = (bf16[8,128,2048]{2,1,0:T(8,128)(2,1)S(1)}, bf16[4,8,64,1024]{3,2,1,0:T(8,128)(2,1)}, bf16[4,8,64,1024]{3,2,1,0:T(8,128)(2,1)}) custom-call(bf16[128,2048]{1,0:T(8,128)(2,1)S(1)} %copy-done.11, bf16[4,8,64,1024]{3,2,1,0:T(8,128)(2,1)} %get-tuple-element.110.refs_1_, ...), custom_call_target="tpu_custom_call", output_to_operand_aliasing={{1}: (1, {}), {2}: (2, {})} | custom-call | flops 46000001024 | bytes 144000000 | tf_op jit(solution)/shard_map/gather_n2/pallas_call | solution.py:574
  262.2 2.0 copy-done.19
  264.2 8.3 %fusion.25 = f32[1024,1024]{0,1:T(8,128)} fusion(bf16[1024,2048]{1,0:T(8,128)(2,1)S(1)} %bitcast.96, bf16[2048,1024]{1,0:T(8,128)(2,1)} %bitcast.139), kind=kOutput, calls=%fused_computation.67 | convolution fusion | flops 4294967296 | bytes 12582912 | tf_op jit(solution)/shard_map/dot_general | solution.py:22
  272.5 10.1 %fusion.26 = f32[1024,1024]{0,1:T(8,128)} fusion(bf16[1024,2048]{1,0:T(8,128)(2,1)} %all-gather.4.cloned.1.call-done, bf16[1024,2048]{1,0:T(8,128)(2,1)} %param.28), kind=kOutput, calls=%fused_computation.68 | convolution fusion | flops 4294967296 | bytes 12582912 | tf_op jit(solution)/shard_map/dot_general | solution.py:26
  282.6 10.4 %multiply_convert_fusion.1 = (bf16[1024,1024]{0,1:T(8,128)(2,1)}, bf16[1024,1024]{0,1:T(8,128)(2,1)}, bf16[1024,1024]{0,1:T(8,128)(2,1)}) fusion(f32[1024,1024]{0,1:T(8,128)} %fusion.26, f32[1024,1024]{0,1:T(8,128)} %fusion.25, bf16[1024,2048]{1,0:T(8,128)(2,1)S(1)} %bitcast.97, bf16[2048,1024]{1,0:T(8,128)(2,1)S(1)} %bitcast.137), kind=kOutput, calls=%fused_computation.16 | convolution fusion | flops 4310695936 | bytes 23068672 | tf_op jit(solution)/shard_map/dot_general | solution.py:22
  293.0 8.6 %fusion.27 = f32[1024,2048]{1,0:T(8,128)} fusion(bf16[1024,1024]{0,1:T(8,128)(2,1)} %get-tuple-element.143, bf16[2048,1024]{1,0:T(8,128)(2,1)S(1)} %bitcast.138), kind=kOutput, calls=%fused_computation.69 | convolution fusion | flops 4294967296 | bytes 14680064 | tf_op jit(solution)/shard_map/dot_general | solution.py:26
  301.6 12.4 %convolution_convert_fusion = bf16[2048,2048]{1,0:T(8,128)(2,1)} fusion(bf16[1024,2048]{1,0:T(8,128)(2,1)S(1)} %bitcast.98, bf16[1024,1024]{0,1:T(8,128)(2,1)S(1)} %copy-done.54, bf16[1024,1024]{0,1:T(8,128)(2,1)S(1)} %copy-done.53), kind=kOutput, calls=%fused_computation.8 | convolution fusion | flops 8602517504 | bytes 16777216 | tf_op jit(solution)/shard_map/dot_general | solution.py:30
  314.0 11.8 %add_convert_fusion = bf16[1024,2048]{1,0:T(8,128)(2,1)} fusion(f32[1024,2048]{1,0:T(8,128)} %fusion.27, bf16[1024,1024]{0,1:T(8,128)(2,1)} %get-tuple-element.144, bf16[2048,1024]{1,0:T(8,128)(2,1)} %bitcast.140), kind=kOutput, calls=%fused_computation.7 | convolution fusion | flops 4299161600 | bytes 18874368 | tf_op jit(solution)/shard_map/dot_general | solution.py:26
  326.4 2.2 copy-done.21
  328.6 44.4 %scatter_gn2.1 = f32[128,2048]{1,0:T(8,128)S(1)} custom-call(bf16[8,128,2048]{2,1,0:T(8,128)(2,1)S(1)} %bitcast.99), custom_call_target="tpu_custom_call" | custom-call | flops 50600001536 | bytes 158400000 | tf_op jit(solution)/shard_map/scatter_gn2/pallas_call | solution.py:574
  374.0 2.5 copy.54
  376.5 2.3 copy.55
  378.8 2.5 copy.56
  381.4 1.9 multiply_reduce_fusion
  383.3 2.0 fusion.21.refs_0_
  385.3 10.0 %convolution_convert_fusion.2 = bf16[1024,2048]{1,0:T(8,128)(2,1)} fusion(bf16[1024,1024]{0,1:T(8,128)(2,1)} %get-tuple-element.145, bf16[1024,2048]{1,0:T(8,128)(2,1)} %all-gather.4.cloned.1.call-done), kind=kOutput, calls=%fused_computation.21 | convolution fusion | flops 4297064448 | bytes 10485760 | tf_op jit(solution)/shard_map/dot_general | solution.py:30
  395.3 50.7 %gather_ga.1 = (bf16[8,128,2048]{2,1,0:T(8,128)(2,1)S(1)}, bf16[256,2048]{1,0:T(8,128)(2,1)S(1)}) custom-call(bf16[128,2048]{1,0:T(8,128)(2,1)S(1)} %fusion.21.refs_0_, bf16[4,256,2048]{2,1,0:T(8,128)(2,1)} %bitcast.141), custom_call_target="tpu_custom_call" | custom-call | flops 57500000256 | bytes 180000000 | tf_op jit(solution)/shard_map/gather_ga/pallas_call | solution.py:574
  447.0 2.0 copy-done.17
  449.0 9.6 %convolution_convert_fusion.3 = bf16[1024,2048]{1,0:T(8,128)(2,1)} fusion(bf16[1024,1024]{0,1:T(8,128)(2,1)} %get-tuple-element.145, bf16[1024,2048]{1,0:T(8,128)(2,1)} %param.28), kind=kOutput, calls=%fused_computation.22 | convolution fusion | flops 4297064448 | bytes 10485760 | tf_op jit(solution)/shard_map/dot_general | solution.py:22
  458.7 1.3 convolution_convert_fusion.6.go
  460.0 7.4 %attention_back.1 = bf16[1024,768]{1,0:T(8,128)(2,1)S(1)} custom-call(bf16[1024,768]{1,0:T(8,128)(2,1)S(1)} %get-tuple-element.122.rot, bf16[1024,256]{1,0:T(8,128)(2,1)S(1)} %convolution_convert_fusion.6.go, f32[1024,128]{1,0:T(8,128)S(1)} %copy-done.2, f32[1024,128]{1,0:T(8,128)S(1)} %copy-done.4, s32[1024,1]{1,0:T(8,128)S(1)} %copy.50.piece), custom_call_target="tpu_custom_call" | custom-call | flops 1342177280 | bytes 6291456 | tf_op jit(solution)/shard_map/attention_back/pallas_call | solution.py:693
  467.5 5.0 fusion.3
  472.7 3.6 convolution_convert_fusion.5
  476.5 5.5 convolution_convert_fusion.4
  482.0 93.2 %scatter_gn1.1 = (f32[128,2048]{1,0:T(8,128)S(1)}, bf16[64,8192]{1,0:T(8,128)(2,1)}, bf16[64,8192]{1,0:T(8,128)(2,1)S(1)}, f32[8,16,256]{2,1,0:T(8,128)S(1)}, bf...) custom-call(bf16[8,128,2048]{2,1,0:T(8,128)(2,1)} %bitcast.105, ...), custom_call_target="tpu_custom_call" | custom-call | flops 1150000000 | bytes 3600000 | tf_op jit(solution)/shard_map/scatter_gn1/pallas_call | solution.py:574
  576.0 1.3 copy.61
  577.4 2.3 copy.62
  579.7 1.6 copy.63
  581.3 1.7 fusion.14
  583.0 6.6 bitcast_convert_fusion.2
  590.7 89.7 %rows_attn.1 = (f32[128,2048]{1,0:T(8,128)S(1)}, bf16[192,2048]{1,0:T(8,128)(2,1)}, bf16[4,64,8192]{2,1,0:T(8,128)(2,1)}, bf16[4,64,2048]{2,1,0:T(8,128)(2,1)S(1...) custom-call(bf16[8,128,2048]{2,1,0:T(8,128)(2,1)} %bitcast.136, bf16[8,64,768]{2,1,0:T(8,128)(2,1)S(1)} %bitcast.93, ...), custom_call_target="tpu_custom_call" | custom-call | flops 80499998720 | bytes 252000000 | tf_op jit(solution)/shard_map/rows_attn/pallas_call | solution.py:574
  680.5 6.7 bitcast_convert_fusion.1
  687.2 2.9 fusion.22
  690.1 1.6 bitcast_convert_fusion.3
  692.4 6.8 bitcast_convert_fusion
  699.3 1.7 fusion.17
  (150 shorter events, 19.0 us)
Async XLA Ops:
  7.2 140.7 %copy-start = (bf16[256,2048]{1,0:T(8,128)(2,1)S(1)}, bf16[256,2048]{1,0:T(8,128)(2,1)}, u32[]{:S(2)}) copy-start(bf16[256,2048]{1,0:T(8,128)(2,1)} %param.25) | copy-start | bytes 3145732
  7.2 265.3 %all-gather.4.cloned.1.call-start = ((), (), s32[]{:S(2)}) async-start(), calls=%async_computation.1 | async-start | bytes 4718592 | tf_op jit(solution)/shard_map/all_gather | solution.py:815
  11.6 1.2 copy-start.12
  12.8 1.2 copy-start.13
  124.8 324.2 %reduce-scatter.2.cloned.1.call-start = ((), (), s32[]{:S(2)}) async-start(), calls=%async_computation.2 | async-start | bytes 10485760 | tf_op jit(solution)/shard_map/reduce_scatter | solution.py:763
  127.9 11.9 %copy-start.46 = (f32[1024]{0:T(1024)}, f32[1024]{0:T(1024)S(1)}, u32[]{:S(2)}) copy-start(f32[1024]{0:T(1024)S(1)} %add_rsqrt_fusion) | copy-start | bytes 12292
  128.6 82.4 %copy-start.37 = (f32[8,1,256]{2,1,0:T(1,128)}, f32[8,1,256]{2,1,0:T(1,128)S(1)}, u32[]{:S(2)}) copy-start(f32[8,1,256]{2,1,0:T(1,128)S(1)} %get-tuple-element.154) | copy-start | bytes 24580
  128.7 11.1 %copy-start.41 = (f32[2048]{0:T(1024)}, f32[2048]{0:T(1024)S(1)}, u32[]{:S(2)}) copy-start(f32[2048]{0:T(1024)S(1)} %mul.149) | copy-start | bytes 24580
  140.1 11.0 %copy-start.1 = (f32[1024,128]{1,0:T(8,128)}, f32[1024,128]{1,0:T(8,128)S(1)}, u32[]{:S(2)}) copy-start(f32[1024,128]{1,0:T(8,128)S(1)} %get-tuple-element.163.cosine) | copy-start | bytes 1572868
  140.1 11.0 %copy-start.3 = (f32[1024,128]{1,0:T(8,128)}, f32[1024,128]{1,0:T(8,128)S(1)}, u32[]{:S(2)}) copy-start(f32[1024,128]{1,0:T(8,128)S(1)} %get-tuple-element.164.sine) | copy-start | bytes 1572868
  147.8 3.3 copy-start.7
  147.8 3.3 copy-start.23
  147.8 3.3 copy-start.25
  151.2 59.5 %copy-start.32 = (bf16[128,2048]{1,0:T(8,128)(2,1)S(1)}, bf16[128,2048]{1,0:T(8,128)(2,1)}, u32[]{:S(2)}) copy-start(bf16[128,2048]{1,0:T(8,128)(2,1)} %param.21) | copy-start | bytes 1572868
  262.2 2.0 copy-start.19
  272.5 10.1 %copy-start.20 = (bf16[8,128,2048]{2,1,0:T(8,128)(2,1)S(1)}, bf16[8,128,2048]{2,1,0:T(8,128)(2,1)}, u32[]{:S(2)}) copy-start(bf16[8,128,2048]{2,1,0:T(8,128)(2,1)} %copy-done.19) | copy-start | bytes 12582916
  272.5 10.1 %copy-start.51 = (bf16[4,8,64,1024]{3,2,1,0:T(8,128)(2,1)S(1)}, bf16[4,8,64,1024]{3,2,1,0:T(8,128)(2,1)}, u32[]{:S(2)}) copy-start(bf16[4,8,64,1024]{3,2,1,0:T(8,128)(2,1)} %get-tuple-element.113) | copy-start | bytes 12582916
  293.0 8.6 %copy-start.53 = (bf16[1024,1024]{0,1:T(8,128)(2,1)S(1)}, bf16[1024,1024]{0,1:T(8,128)(2,1)}, u32[]{:S(2)}) copy-start(bf16[1024,1024]{0,1:T(8,128)(2,1)} %get-tuple-element.143) | copy-start | bytes 6291460
  293.0 8.6 %copy-start.54 = (bf16[1024,1024]{0,1:T(8,128)(2,1)S(1)}, bf16[1024,1024]{0,1:T(8,128)(2,1)}, u32[]{:S(2)}) copy-start(bf16[1024,1024]{0,1:T(8,128)(2,1)} %get-tuple-element.144) | copy-start | bytes 6291460
  325.8 263.7 %all-gather.6.cloned.1.call-start = ((), (), s32[]{:S(2)}) async-start(), calls=%async_computation.3 | async-start | bytes 5242880 | tf_op jit(solution)/shard_map/all_gather | solution.py:767
  326.4 2.2 copy-start.21
  374.0 7.4 %copy-start.38 = (f32[8,1,256]{2,1,0:T(1,128)S(1)}, f32[8,1,256]{2,1,0:T(1,128)}, u32[]{:S(2)}) copy-start(f32[8,1,256]{2,1,0:T(1,128)} %copy-done.37) | copy-start | bytes 24580
  374.0 7.4 %copy-start.44 = (f32[128]{0:T(128)S(1)}, f32[128]{0:T(128)}, u32[]{:S(2)}) copy-start(f32[128]{0:T(128)} %copy-done.43) | copy-start | bytes 1540
  383.3 12.0 %copy-start.49 = (f32[128]{0:T(128)}, f32[128]{0:T(128)S(1)}, u32[]{:S(2)}) copy-start(f32[128]{0:T(128)S(1)} %broadcast_multiply_fusion.1) | copy-start | bytes 1540
  447.0 2.0 copy-start.17
  449.0 9.6 %copy-start.18 = (bf16[8,128,2048]{2,1,0:T(8,128)(2,1)S(1)}, bf16[8,128,2048]{2,1,0:T(8,128)(2,1)}, u32[]{:S(2)}) copy-start(bf16[8,128,2048]{2,1,0:T(8,128)(2,1)} %copy-done.17) | copy-start | bytes 12582916
  458.6 1.3 copy-start.2
  458.6 1.3 copy-start.4
  458.7 8.8 %copy-start.52 = (bf16[4,8,64,768]{3,2,1,0:T(8,128)(2,1)S(1)}, bf16[4,8,64,768]{3,2,1,0:T(8,128)(2,1)}, u32[]{:S(2)}) copy-start(bf16[4,8,64,768]{3,2,1,0:T(8,128)(2,1)} %get-tuple-element.104) | copy-start | bytes 9437188
  460.0 7.5 %copy-start.35 = (bf16[8,128,2048]{2,1,0:T(8,128)(2,1)S(1)}, bf16[8,128,2048]{2,1,0:T(8,128)(2,1)}, u32[]{:S(2)}) copy-start(bf16[8,128,2048]{2,1,0:T(8,128)(2,1)} %get-tuple-element.101) | copy-start | bytes 12582916
  460.0 7.5 %copy-start.47 = (f32[1024]{0:T(1024)S(1)}, f32[1024]{0:T(1024)}, u32[]{:S(2)}) copy-start(f32[1024]{0:T(1024)} %copy-done.46) | copy-start | bytes 12292
  467.4 5.1 copy-start.5
  467.5 5.3 copy-start.8
  472.5 3.8 copy-start.42
  472.5 3.8 copy-start.6
  472.7 3.8 copy-start.36
  576.0 5.2 copy-start.40
  576.0 5.2 copy-start.48
  581.2 8.3 %copy-start.30 = (f32[128,2048]{1,0:T(8,128)}, f32[128,2048]{1,0:T(8,128)S(1)}, u32[]{:S(2)}) copy-start(f32[128,2048]{1,0:T(8,128)S(1)} %copy.63) | copy-start | bytes 3145732
  680.5 6.7 copy-start.29
  692.4 6.9 copy-start.27
  692.4 6.9 copy-start.28
  692.4 6.9 copy-start.31
  692.4 6.9 copy-start.33
  692.4 6.9 copy-start.34
  692.4 6.9 copy-start.39
  692.4 6.9 copy-start.45
  692.4 6.9 copy-start.50
  (10 other events, 10.1 us)
Sparse Core Ops, SparseCore 0:
  124.9 52.7 all-gather.3
  325.9 95.1 reduce-scatter.1
  449.1 63.5 all-gather.5

commit v5 on v4

--- a/solution.py
+++ b/solution.py
@@ -57,22 +57,25 @@
     pl.semaphore_signal(sem, inc=1, device_id={axis: to}, device_id_type=pl.DeviceIdType.MESH)
 
 
-def line_body(n, n_ag, n_rs, a2a_blocks, spreads, n_sum, chain, chain_at, parts, *refs):
+def line_body(n, n_ag, products, a2a_blocks, spreads, n_sum, chain, chain_at, work, parts, *refs):
     refs = list(refs)
     nz = n // 2
     n_a2a = len(a2a_blocks)
     take = lambda count: [refs.pop(0) for _ in range(count)]
-    n_sp = len(spreads)
-    ag_in, rs_in, a2a_in = take(n_ag), take(n_rs), [take(t[0]) for t in a2a_blocks]
+    n_sp, n_rs = len(spreads), len(products)
+    ag_in, rs_in, a2a_in = take(n_ag), [take(2 * len(t) or 1) for t in products], [take(t[0]) for t in a2a_blocks]
     sp_in, sum_in = take(n_sp), take(n_sum)
+    work_in = take(work[1]) if work else []
     ag_out, rs_out, a2a_out, sp_out, sum_out = take(n_ag), take(n_rs), take(n_a2a), take(n_sp), take(n_sum)
     chain_out = take(len(chain))
+    work_out = take(work[2]) if work else []
     ag_sem = [take(7) for _ in range(n_ag)]
-    rs_scr = [take(9) for _ in range(n_rs)]
+    rs_scr = [take(10 if t else 9) for t in products]
     a2a_sem = [take(3) for _ in range(n_a2a)]
     sp_sem = [take(5) for _ in range(n_sp)]
     sum_scr = [take(6) for _ in range(n_sum)]
     chain_sem = [take(5) for _ in chain]
+    work_scr = take(work[3]) if work else []
     me = lax.axis_index("inner")
     z, c = me // 2, lax.rem(me, 2)
     sib = me + 1 - 2 * c
@@ -107,7 +110,7 @@
 
     class Gather:
         def __init__(self, x, out, sems):
-            self.x, self.out = x, out
+            self.x, self.out, self.here = x, out, set()
             self.own_sem, self.rs, self.rr, self.ls, self.lr, self.ss, self.sr = sems
 
         def own(self):
@@ -183,9 +186,27 @@
 
                 self.side(s, 1, j).start()
 
+        def arrive(self, s):
+            self.here.add(s)
+            if s == 0:
+                self.own().wait()
+
+            @pl.loop(0, parts)
+            def _(j):
+                @pl.when(z >= s)
+                def _():
+                    self.from_side(s, 0, j).wait_recv()
+
+                if s > 0:
+                    @pl.when(z + s < nz)
+                    def _():
+                        self.from_side(s, 1, j).wait_recv()
+
         def end(self):
-            self.own().wait()
             for s in range(nz):
+                if s not in self.here:
+                    self.arrive(s)
+
                 @pl.loop(0, parts)
                 def _(j):
                     @pl.when(z >= s)
@@ -195,7 +216,6 @@
                             self.right(s, j).wait_send()
 
                         self.side(s, 0, j).wait_send()
-                        self.from_side(s, 0, j).wait_recv()
 
                     @pl.when(z + s < nz)
                     def _():
@@ -205,11 +225,11 @@
 
                         if s > 0:
                             self.side(s, 1, j).wait_send()
-                            self.from_side(s, 1, j).wait_recv()
 
     class Scatter:
-        def __init__(self, p, out, scratch):
-            self.p, self.out = p, out
+        def __init__(self, operands, flips, out, scratch):
+            self.pairs, self.out = [(x, w) + t for x, w, t in zip(operands[::2], operands[1::2], flips)], out
+            self.p, *scratch = scratch if flips else operands + scratch
             self.sib_buf, self.l_buf, self.r_buf, self.ss, self.sr, self.rs, self.rr, self.ls, self.lr = scratch
             self.count = out.shape[0] // parts
 
@@ -225,51 +245,81 @@
             rows = rows_of(self.out, j)
             return rcopy(self.r_buf.at[d, rows], self.r_buf.at[d, rows], self.ls.at[d, j], self.lr.at[d, j], me + to)
 
+        def product(self, d):
+            own, width = self.out.shape
+            rows = pl.ds(d * 2 * own, 2 * own)
+            tile = min(512, width)
+
+            @pl.loop(0, width // tile)
+            def _(t):
+                cols = pl.ds(pl.multiple_of(t * tile, tile), tile)
+                total = 0.0
+                for x, w, flip, first in self.pairs:
+                    x = x[rows, first : first + w.shape[1 if flip else 0]]
+                    total += dot_t(x, w[cols, :]) if flip else dot(x, w[:, cols])
+                total = total.astype(bf16)
+                self.p[2 * d, :, cols] = total[:own]
+                self.p[2 * d + 1, :, cols] = total[own:]
+
         def begin(self):
-            for s in range(nz // 2):
-                for d in (nz - 1 - s, s):
-                    @pl.loop(0, parts)
-                    def _(j):
-                        self.side(d, j).start()
+            for s in range(1 if self.pairs else nz // 2):
+                self.offer(s)
+
+        def offer(self, s):
+            for d in (nz - 1 - s, s):
+                if self.pairs:
+                    self.product(d)
+
+                @pl.loop(0, parts)
+                def _(j):
+                    self.side(d, j).start()
+
+        def after_step(self, s):
+            if self.pairs and s < nz // 2:
+                self.offer(s)
 
         def pair(self, d, rows):
             return self.p[2 * d + c, rows, :].astype(f32) + self.sib_buf[d, rows, :].astype(f32)
 
         def step(self, s, j):
-            rows = rows_of(self.out, j)
-            d = nz - s
-
-            @pl.when(d > z)
+            tick = (s - 1) * parts + j
+            k = tick - z
+
+            @pl.when((k >= 0) & (k < (nz - 1 - z) * parts))
             def _():
-                self.side(d, j).wait_recv()
+                d, i = nz - 1 - k // parts, lax.rem(k, parts)
+                rows = rows_of(self.out, i)
+                self.side(d, i).wait_recv()
 
                 @pl.when(z > 0)
                 def _():
-                    self.right(d, j, -2).wait_recv()
+                    self.right(d, i, -2).wait_recv()
                     self.l_buf[d, rows, :] = (self.pair(d, rows) + self.l_buf[d, rows, :].astype(f32)).astype(bf16)
 
                 @pl.when(z == 0)
                 def _():
                     self.l_buf[d, rows, :] = self.pair(d, rows).astype(bf16)
 
-                self.right(d, j).start()
-
-            e = s - 1
-
-            @pl.when(e < z)
+                self.right(d, i).start()
+
+            m = tick - (nz - 1 - z)
+
+            @pl.when((m >= 0) & (m < z * parts))
             def _():
-                self.side(e, j).wait_recv()
+                d, i = m // parts, lax.rem(m, parts)
+                rows = rows_of(self.out, i)
+                self.side(d, i).wait_recv()
 
                 @pl.when(z + 1 < nz)
                 def _():
-                    self.left(e, j, 2).wait_recv()
-                    self.r_buf[e, rows, :] = (self.pair(e, rows) + self.r_buf[e, rows, :].astype(f32)).astype(bf16)
+                    self.left(d, i, 2).wait_recv()
+                    self.r_buf[d, rows, :] = (self.pair(d, rows) + self.r_buf[d, rows, :].astype(f32)).astype(bf16)
 
                 @pl.when(z + 1 == nz)
                 def _():
-                    self.r_buf[e, rows, :] = self.pair(e, rows).astype(bf16)
-
-                self.left(e, j).start()
+                    self.r_buf[d, rows, :] = self.pair(d, rows).astype(bf16)
+
+                self.left(d, i).start()
 
         def end(self):
             @pl.loop(0, parts)
@@ -362,7 +412,7 @@
         def __init__(self, src, out, sems, phases):
             self.src, self.out, self.phases = src, out, phases
             self.own_sem, self.send, self.recv, self.send_half, self.recv_half = sems
-            self.half = out.shape[1] // 2
+            self.half, self.here = out.shape[1] // 2, False
 
         def own(self):
             return pltpu.make_async_copy(self.src, self.out.at[r], self.own_sem)
@@ -417,11 +467,14 @@
             if 2 in self.phases:
                 for axis in (0, 1):
                     self.second(axis).wait_send()
-                    self.second_came(axis).wait_recv()
-
-    parts_of = [Gather(*t) for t in zip(ag_in, ag_out, ag_sem)]
-    parts_of += [Scatter(*t) for t in zip(rs_in, rs_out, rs_scr)]
-    parts_of += [Exchange(*t) for t in zip(a2a_in, a2a_out, a2a_sem, a2a_blocks)]
+                if not self.here:
+                    self.arrive()
+
+        def arrive(self):
+            self.here = True
+            for axis in (0, 1):
+                self.second_came(axis).wait_recv()
+
     class Sum:
         def __init__(self, p, out, scratch):
             self.p, self.out = p, out
@@ -494,98 +547,230 @@
                     self.first(h, k).wait_send()
                 self.second(h).wait_send()
 
+    gathers = [Gather(*t) for t in zip(ag_in, ag_out, ag_sem)]
+    scatters = [Scatter(*t) for t in zip(rs_in, products, rs_out, rs_scr)]
+    exchanges = [Exchange(*t) for t in zip(a2a_in, a2a_out, a2a_sem, a2a_blocks)]
     square_parts = [Spread(*t) for t in zip(sp_in, sp_out, sp_sem, spreads)]
     square_parts += [Sum(*t) for t in zip(sum_in, sum_out, sum_scr)]
-    exchanges = parts_of[n_ag + n_rs :]
     chained = [Spread(a2a_out[i], out, sems, (1, 2)) for i, out, sems in zip(chain, chain_out, chain_sem)]
+    worker = work[0](gathers[0], square_parts, nz, z, (r, across_x, across_y, 3 - r), work_in, work_out, work_scr) if work else None
 
     def begin_chain():
         for i, part in zip(chain, chained):
             exchanges[i].arrive()
             part.begin()
 
-    parts_of += square_parts
-    for part in parts_of:
+    line_parts = gathers + scatters
+    for part in gathers + exchanges + square_parts + scatters:
         part.begin()
-    if n_ag + n_rs:
+    if worker:
+        worker.begin()
+    if line_parts:
         if chain_at == 0:
             begin_chain()
         for s in range(1, nz):
             @pl.loop(0, parts)
             def _(j):
-                for part in parts_of:
+                for part in line_parts:
                     part.step(s, j)
 
-            for part in exchanges:
+            for part in exchanges + scatters:
                 part.after_step(s)
             if s == chain_at:
                 begin_chain()
             if s == max(1, chain_at):
                 for part in square_parts:
                     part.mid()
+            if worker:
+                worker.after_step(s)
     else:
         begin_chain()
         for part in square_parts:
             part.mid()
-    if chained:
-        for part in parts_of[: n_ag + n_rs]:
-            part.end()
-        for part in chained:
-            part.mid()
-        parts_of = parts_of[n_ag + n_rs :] + chained
-    for part in parts_of:
+    for part in line_parts:
         part.end()
-
-
-def line_comm(cid, name, us, ag=(), rs=(), a2a=(), spread=(), sums=(), chain=(), chain_at=None, parts=2):
+    for part in chained:
+        part.mid()
+    for part in exchanges + square_parts + chained:
+        part.end()
+
+
+class Forward:
+    def __init__(self, gather, spreads, nz, z, blocks, ins, outs, scratch):
+        self.gather, self.spreads, self.nz, self.z, self.blocks = gather, spreads, nz, z, blocks
+        self.cot, self.w_down = ins[:2]
+        self.hid, self.ggu = outs
+        self.ghid = scratch[0]
+        if spreads:
+            self.w, self.sem = scratch[1:]
+        else:
+            self.w = ins[2:]
+        self.rows = 2 * gather.x.shape[0]
+        self.tile = min(256, self.hid.shape[1])
+
+    def load(self, i, k):
+        q = self.blocks[k]
+        return pltpu.make_async_copy(self.spreads[i].out.at[q], self.w.at[i, q], self.sem.at[i, k])
+
+    def each_tile(self, put):
+        @pl.loop(0, self.hid.shape[1] // self.tile)
+        def _(t):
+            put(pl.multiple_of(t * self.tile, self.tile))
+
+    def begin(self):
+        if self.spreads:
+            for i in (0, 1):
+                for k in (0, 1, 2):
+                    self.load(i, k).start()
+
+        @pl.loop(0, self.nz)
+        def _(b):
+            rows = pl.ds(pl.multiple_of(b * self.rows, self.rows), self.rows)
+
+            def put(first):
+                cols = pl.ds(first, self.tile)
+                self.ghid[rows, cols] = dot_t(self.cot[rows, :], self.w_down[cols, :])
+
+            self.each_tile(put)
+
+    def weights(self):
+        if self.spreads:
+            for i in (0, 1):
+                self.spreads[i].arrive()
+                self.load(i, 3).start()
+            for i in (0, 1):
+                for k in range(4):
+                    self.load(i, k).wait()
+
+    def chip(self, d):
+        width = self.hid.shape[1]
+        rows = pl.ds(pl.multiple_of(d * self.rows, self.rows), self.rows)
+
+        def put(first):
+            cols = pl.ds(first, self.tile)
+            x = self.gather.out[pl.ds(2 * d, 2)].reshape(self.rows, -1)
+            if self.spreads:
+                gate, up = [dot(x, self.w[i, :, :, :, cols].reshape(x.shape[1], self.tile)) for i in (0, 1)]
+            else:
+                gate, up = [dot(x, w[:, cols]) for w in self.w]
+            ghid = self.ghid[rows, cols]
+            s = 1.0 / (1.0 + jnp.exp(-gate))
+            silu = gate * s
+            self.hid[rows, cols] = (silu * up).astype(bf16)
+            self.ggu[rows, cols] = (ghid * up * s * (1.0 + gate * (1.0 - s))).astype(bf16)
+            self.ggu[rows, pl.ds(width + first, self.tile)] = (ghid * silu).astype(bf16)
+
+        self.each_tile(put)
+
+    def away(self, s):
+        self.gather.arrive(s)
+
+        @pl.when(self.z >= s)
+        def _():
+            self.chip(self.z - s)
+
+        if s > 0:
+            @pl.when(self.z + s < self.nz)
+            def _():
+                self.chip(self.z + s)
+
+    def after_step(self, s):
+        last = max(1, self.nz - 2)
+        if s == last:
+            self.weights()
+            for k in range(last):
+                self.away(k)
+        if s == self.nz - 1:
+            for k in range(last, self.nz):
+                self.away(k)
+
+
+def line_comm(cid, name, us, ag=(), rs=(), a2a=(), spread=(), sums=(), chain=(), chain_at=None, work=None, parts=2):
     n = lax.axis_size("inner")
     nz = n // 2
     chain_at = nz - 2 if chain_at is None else chain_at
     dma = pltpu.SemaphoreType.DMA
     hbm = pl.BlockSpec(memory_space=pl.ANY)
     vmem = pl.BlockSpec(memory_space=pltpu.VMEM)
-    rs = [p.reshape((n, p.shape[0] // n) + p.shape[1:]) for p in rs]
-    out_shape = [jax.ShapeDtypeStruct((n,) + x.shape, x.dtype) for x in ag]
-    out_shape += [jax.ShapeDtypeStruct(p.shape[1:], f32) for p in rs]
-    out_shape += [jax.ShapeDtypeStruct(t[1], t[0][0].dtype) for t in a2a]
-    out_shape += [jax.ShapeDtypeStruct(b.shape if 1 not in ph else (4,) + b.shape, b.dtype) for b, ph in spread]
-    out_shape += [jax.ShapeDtypeStruct((p.shape[0] // 4, p.shape[1]), bf16) for p in sums]
-    out_shape += [jax.ShapeDtypeStruct((4,) + a2a[i][1], a2a[i][0][0].dtype) for i in chain]
+    products = [tuple(t[2:] for t in p) if isinstance(p, list) else () for p in rs]
+    rs_out = [
+        (p[0][0].shape[0] // n, p[0][1].shape[0 if p[0][2] else 1]) if isinstance(p, list) else (p.shape[0] // n, p.shape[1])
+        for p in rs
+    ]
+    rs_in = []
+    for p, shape in zip(rs, rs_out):
+        rs_in += [a for t in p for a in t[:2]] if isinstance(p, list) else [p.reshape((n,) + shape)]
     sums = [p.reshape((4, p.shape[0] // 4) + p.shape[1:]) for p in sums]
-    first_in = len(ag) + len(rs) + sum(len(t[0]) for t in a2a)
-    first_out = len(ag) + len(rs) + len(a2a)
-    aliases = {first_in + i: first_out + i for i, (b, ph) in enumerate(spread) if 1 not in ph}
-    scratch = []
-    for _ in ag:
+    work_in, work_out, work_scratch = work[1:] if work else ((), (), [])
+    inputs, in_specs, out_shape, out_specs, scratch = [], [], [], [], []
+
+    def give(arrays, space):
+        inputs.extend(arrays)
+        in_specs.extend([space] * len(arrays))
+
+    def get(shape, dtype, space):
+        out_shape.append(jax.ShapeDtypeStruct(shape, dtype))
+        out_specs.append(space)
+
+    near = vmem if work else hbm
+    give(ag, hbm)
+    give(rs_in, vmem)
+    give([w for t in a2a for w in t[0]], hbm)
+    aliases = {len(inputs) + i: len(ag) + len(rs) + len(a2a) + i for i, (_, ph) in enumerate(spread) if 1 not in ph}
+    give([b for b, _ in spread], hbm)
+    give(sums, vmem)
+    give(work_in, vmem)
+    for x in ag:
+        get((n,) + x.shape, x.dtype, near)
         scratch += [dma, dma((nz, parts)), dma((nz + 1, parts)), dma((nz, parts)), dma((nz + 1, parts))]
         scratch += [dma((2, nz, parts)), dma((2, nz, parts))]
-    for p in rs:
-        scratch += [pltpu.VMEM((nz,) + p.shape[1:], bf16)] * 3 + [dma((nz, parts))] * 6
+    for shape, flips in zip(rs_out, products):
+        get(shape, f32, vmem)
+        scratch += [pltpu.VMEM((n,) + shape, bf16)] if flips else []
+        scratch += [pltpu.VMEM((nz,) + shape, bf16)] * 3 + [dma((nz, parts))] * 6
     for t in a2a:
+        get(t[1], t[0][0].dtype, hbm)
         scratch += [dma((t[4],)), dma((n, t[4])), dma((n, t[4]))]
-    for _ in spread:
+    for b, phases in spread:
+        get(b.shape if 1 not in phases else (4,) + b.shape, b.dtype, hbm)
         scratch += [dma, dma((2,)), dma((2,)), dma((2,)), dma((2,))]
     for p in sums:
+        get(p.shape[1:], bf16, vmem)
         half = (p.shape[1] // 2, p.shape[2])
         scratch += [pltpu.VMEM((2, 2) + half, bf16), pltpu.VMEM((2,) + half, bf16)]
         scratch += [dma((2, 2)), dma((2, 2)), dma((2,)), dma((2,))]
-    for _ in chain:
+    for i in chain:
+        get((4,) + a2a[i][1], a2a[i][0][0].dtype, hbm)
         scratch += [dma, dma((2,)), dma((2,)), dma((2,)), dma((2,))]
+    for shape in work_out:
+        get(shape, bf16, vmem)
+    scratch += work_scratch
     outs = pl.pallas_call(
-        functools.partial(line_body, n, len(ag), len(rs), [(len(t[0]),) + t[2:6] for t in a2a], [ph for _, ph in spread], len(sums), chain, chain_at, parts),
+        functools.partial(
+            line_body,
+            n,
+            len(ag),
+            products,
+            [(len(t[0]),) + t[2:6] for t in a2a],
+            [ph for _, ph in spread],
+            len(sums),
+            chain,
+            chain_at,
+            (work[0], len(work_in), len(work_out), len(work_scratch)) if work else None,
+            parts,
+        ),
         out_shape=out_shape,
-        in_specs=[hbm] * len(ag) + [vmem] * len(rs) + [hbm] * (sum(len(t[0]) for t in a2a) + len(spread)) + [vmem] * len(sums),
-        out_specs=[hbm] * len(ag) + [vmem] * len(rs) + [hbm] * (len(a2a) + len(spread)) + [vmem] * len(sums) + [hbm] * len(chain),
+        in_specs=in_specs,
+        out_specs=out_specs,
         input_output_aliases=aliases,
         scratch_shapes=scratch,
         compiler_params=pltpu.CompilerParams(
-            collective_id=cid, has_side_effects=True, vmem_limit_bytes=48 * 2**20
+            collective_id=cid, has_side_effects=True, vmem_limit_bytes=62 * 2**20
         ),
         cost_estimate=pl.CostEstimate(flops=us * 1150000000, bytes_accessed=us * 3600000, transcendentals=0),
         name=name,
-    )(*ag, *rs, *[w for t in a2a for w in t[0]], *[b for b, _ in spread], *sums)
-    outs = [o.reshape((-1,) + o.shape[2:]) if i < len(ag) else o for i, o in enumerate(outs)]
-    return outs
+    )(*inputs)
+    return [o.reshape((-1,) + o.shape[2:]) if i < len(ag) else o for i, o in enumerate(outs)]
 
 
 def rotate(flat, cosine, sine):
@@ -821,36 +1006,38 @@
     u1 = x * rms_scale(x)
     n1 = (u1 * shares_first(attn_gain)).astype(bf16)
     o, rot = attention(dot(n1, w_qkv), cosine, sine, pieces)
-    a_part = dot(o, w_out).astype(bf16)
     if square:
-        a, w_g, w_u = line_comm(2, "attn_out", 50, rs=[a_part], spread=[(g_share, (1,)), (u_share, (1,))])
+        a, w_g, w_u = line_comm(2, "attn_out", 50, rs=[[(o, w_out, False, 0)]], spread=[(g_share, (1,)), (u_share, (1,))])
     else:
         w_g, w_u = join(g_share), join(u_share)
-        (a,) = line_comm(2, "attn_out", 50, rs=[a_part])
+        (a,) = line_comm(2, "attn_out", 50, rs=[[(o, w_out, False, 0)]])
     mid = tokens.astype(f32) + a
     r2 = rms_scale(mid)
     u2 = mid * r2
     n2 = shares_first((u2 * ffn_gain).astype(bf16))
+    ffn = w_down.shape[0]
+    results = [(length, ffn), (length, 2 * ffn)]
+    held = [pltpu.VMEM((length, ffn), f32)]
     if square:
-        n2, w_g, w_u = line_comm(3, "gather_n2", 40, ag=[n2], spread=[(w_g, (2,)), (w_u, (2,))])
+        held += [pltpu.VMEM((2,) + w_g.shape, bf16), pltpu.SemaphoreType.DMA((2, 4))]
+        n2, w_g, w_u, hid, ggu = line_comm(
+            3,
+            "ffn_forward",
+            60,
+            ag=[n2],
+            spread=[(w_g, (2,)), (w_u, (2,))],
+            work=(Forward, [cot, w_down], results, held),
+        )
+        w_g, w_u = flat(w_g), flat(w_u)
     else:
-        (n2,) = line_comm(3, "gather_n2", 40, ag=[n2])
-    w_g, w_u = flat(w_g), flat(w_u)
-
-    gate = dot(n2, w_g)
-    up = dot(n2, w_u)
-    s = jax.nn.sigmoid(gate)
-    silu = gate * s
-    hid = (silu * up).astype(bf16)
+        w_g, w_u = flat(w_g), flat(w_u)
+        n2, hid, ggu = line_comm(3, "ffn_forward", 60, ag=[n2], work=(Forward, [cot, w_down, w_g, w_u], results, held))
+
     g_down = t_dot(hid, cot).astype(bf16)
-    ghid = dot_t(cot, w_down)
-    ggate = (ghid * up * s * (1.0 + gate * (1.0 - s))).astype(bf16)
-    gup = (ghid * silu).astype(bf16)
-    gu = t_dot(n2, jnp.concatenate([ggate, gup], axis=1)).astype(bf16)
-    gn2_part = (dot_t(ggate, w_g) + dot_t(gup, w_u)).astype(bf16)
-    gu, gn2_part = after((gu, gn2_part))
+    gu = t_dot(n2, ggu).astype(bf16)
+    gu, ggu = after((gu, ggu))
     gu_share = sum_share(gu)
-    (gn2,) = line_comm(4, "scatter_gn2", 44, rs=[gn2_part])
+    (gn2,) = line_comm(4, "scatter_gn2", 44, rs=[[(ggu, w_g, True, 0), (ggu, w_u, True, w_g.shape[1])]])
     gn2 = owners_first(gn2)
     gu2 = gn2 * ffn_gain
     ffn_gain_part = jnp.sum(gn2 * u2, axis=0)
@@ -886,14 +1073,14 @@
             chain=(0,),
             chain_at=0,
         )
-        mlp_part, gains = dot(hid, w_down).astype(bf16), jnp.sum(gains, axis=0)
+        gains = jnp.sum(gains, axis=0)
         qkv_back = rows_back(qkv_share.reshape(n, -1, 3 * head_cols), (0, head_cols), 3)
-        mlp_part, grad_down = after((mlp_part, grad_down))
+        gains, grad_down = after((gains, grad_down))
         mlp, qkv_rows, grad_up, grad_out, gains, grad_qkv = line_comm(
             7,
             "rows_attn",
             70,
-            rs=[mlp_part],
+            rs=[[(hid, w_down, False, 0)]],
             a2a=[qkv_back],
             spread=[(up_rows, (1, 2)), (out_share, (1, 2)), (gains, (1, 2))],
             chain=(0,),
@@ -905,8 +1092,7 @@
         gn1, gu_rows, gains = line_comm(6, "scatter_gn1", 80, rs=[gn1_part], a2a=[gu_back, sum_blocks(gains)])
         gains = lax.psum(jnp.sum(gains, axis=0), "replica")
         qkv_back = rows_back(sum_share(g_qkv).reshape(n, -1, 3 * head_cols), (0, head_cols), 3)
-        mlp_part = dot(hid, w_down).astype(bf16)
-        mlp, qkv_rows = line_comm(7, "rows_attn", 75, rs=[mlp_part], a2a=[qkv_back])
+        mlp, qkv_rows = line_comm(7, "rows_attn", 75, rs=[[(hid, w_down, False, 0)]], a2a=[qkv_back])
         grad_gu = join(gu_rows).reshape(nr, 2, -1, n * cols)
         grad_gate, grad_up, grad_out, grad_qkv = grad_gu[:, 0], grad_gu[:, 1], join(sum_share(g_out)), join(qkv_rows)
     output = (mid + mlp).astype(bf16)

time: 718 us -> 656 us (0.914)
  matrix products: 109 us -> 49.7 us
  local copies, waits for them, and re-layouts: 44.9 us -> 26.1 us
  Pallas kernels: 502 us -> 519 us
    dot_general x5 -> x1, matrix products: 40.5 us -> 8.7 us  [dot(): return jnp.dot(a, b, preferred_element_type=f32)]
    dot_general x5 -> x2, matrix products: 36.9 us -> 8.98 us  [dot_t(): return lax.dot_general(a, b, dims_rows, preferred_element_type=f32)]
    pallas_call x8, Pallas kernels: 487 us -> 504 us  [line_comm(): pl.pallas_call(functools.partial(line_body, n, len(ag), products, [(len(t...]
    unnamed x112 -> x82, local copies, waits for them, and re-layouts: 19.4 us -> 5.43 us
  transfers between devices with their start and end apart: 3 -> 3, of which waited for: 0 -> 0; matrix products, arithmetic and copies ran while one was open for 13% -> 11% of each run, Pallas kernels for 43% -> 43%
where the time goes in v5:
time: 656 us; the launch traced here: 649 us
  Pallas kernels  519 us (79%)
  matrix products  49.7 us (8%)
  other arithmetic  38.6 us (6%)
  local copies, waits for them, and re-layouts  26.1 us (4%)
  between operations  14.8 us (2%)
    pallas_call x8, Pallas kernels, line_comm(): pl.pallas_call(functools.partial(line_body, n, len(ag), products, [(len(t...  504 us
    dot_general x4, matrix products, t_dot(): return lax.dot_general(a, b, dims_cols, preferred_element_type=f32)  32.1 us
  transfers between devices with their start and end apart: 3, of which 0 were waited for; matrix products, arithmetic and copies ran while one was open for 11% of the time, Pallas kernels for 43%

profile of v5, /device:TPU:0, one launch (start us, length us, event | category | flops | bytes accessed | tf_op | source)
XLA Modules:
  0.0 648.5 jit_solution(17902664927352975355)
XLA Ops:
  7.2 0.7 reshape.255
  7.9 0.7 convert.12
  8.5 1.3 copy.46
  9.9 1.0 copy.48.refs_0_
  10.9 0.7 scatter.16
  11.6 0.7 scatter.19.refs_3_
  13.4 26.1 %load_attn.1 = (bf16[8,64,256]{2,1,0:T(8,128)(2,1)}, bf16[8,64,256]{2,1,0:T(8,128)(2,1)}, bf16[8,64,256]{2,1,0:T(8,128)(2,1)}, s32[8,8,128]{2,1,0:T(8,128)}, f32[8,8,256]{2,1,0:T(8,128)}) custom-call(bf16[256,2048]{1,0:T(8,128)(2,1)} %refs_0_.1, bf16[256,2048]{1,0:T(8,128)(2,1)} %refs_1_.4, bf16[256,2048]{1,0:T(8,128)(2,1)} %refs_2_.2, s32[8,128]{1,0:T(8,128)} %copy-done.32, ...), custom_call_target="tpu_custom_call" | custom-call | flops 28750000128 | bytes 90000000 | tf_op jit(solution)/shard_map/load_attn/pallas_call | solution.py:748
  39.6 2.0 pad_maximum_fusion.refs_3_
  41.6 81.8 %load_ffn.1 = (bf16[8,128,2048]{2,1,0:T(8,128)(2,1)}, bf16[8,64,1024]{2,1,0:T(8,128)(2,1)}, bf16[8,64,1024]{2,1,0:T(8,128)(2,1)}, bf16[4,8,64,768]{3,2,1,0:T(8,128)(2,1)}) custom-call(bf16[128,2048]{1,0:T(8,128)(2,1)} %copy.48.refs_0_, bf16[256,8192]{1,0:T(8,128)(2,1)} %refs_1_.5, bf16[256,8192]{1,0:T(8,128)(2,1)} %refs_2_.3, ...), custom_call_target="tpu_custom_call" | custom-call | flops 92000002048 | bytes 288000000 | tf_op jit(solution)/shard_map/load_ffn/pallas_call | solution.py:748
  123.5 0.8 slice_bitcast_fusion
  124.3 1.5 fusion.18
  125.9 3.1 fusion.4
  129.0 1.9 fusion.15
  131.6 8.7 %fusion.8.lin = f32[1024,768]{1,0:T(8,128)} fusion(bf16[2048,768]{1,0:T(8,128)(2,1)} %bitcast.119, bf16[1024,2048]{1,0:T(8,128)(2,1)} %bitcast.81, f32[2048]{0:T(1024)S(1)} %mul.128, f32[1024]{0:T(1024)S(1)} %add_rsqrt_fusion), kind=kOutput, calls=%fused_computation.20 | convolution fusion | flops 3229614080 | bytes 10498048 | tf_op jit(solution)/shard_map/dot_general | solution.py:22
  140.4 7.3 %attention.1 = (bf16[1024,256]{1,0:T(8,128)(2,1)S(1)}, bf16[1024,768]{1,0:T(8,128)(2,1)S(1)}) custom-call(f32[1024,768]{1,0:T(8,128)} %fusion.8.lin, f32[1024,128]{1,0:T(8,128)S(1)} %get-tuple-element.164.cosine, f32[1024,128]{1,0:T(8,128)S(1)} %get-tuple-element.165.sine, s32[1024,1]{1,0:T(8,128)S(1)} %copy.50.piece), custom_call_target="tpu_custom_call" | custom-call | flops 536870912 | bytes 6291456 | tf_op jit(solution)/shard_map/attention/pallas_call | solution.py:820
  147.6 0.8 copy-done.6
  148.4 70.2 %attn_out.1 = (f32[128,2048]{1,0:T(8,128)}, bf16[4,8,64,1024]{3,2,1,0:T(8,128)(2,1)}, bf16[4,8,64,1024]{3,2,1,0:T(8,128)(2,1)}) custom-call(bf16[1024,256]{1,0:T(8,128)(2,1)} %copy-done.6, bf16[256,2048]{1,0:T(8,128)(2,1)} %refs_1_.6, bf16[8,64,1024]{2,1,0:T(8,128)(2,1)} %get-tuple-element.109.refs_2_, bf16[8,64,1024]{2,1,0:T(8,128)(2,1)} %get-tuple-element.110.refs_3_), custom_call_target="tpu_custom_call" | custom-call | flops 57500000256 | bytes 180000000 | tf_op jit(solution)/shard_map/attn_out/pallas_call | solution.py:748
  218.6 2.2 multiply_reduce_fusion.2
  220.8 1.0 copy-done.8
  222.2 1.0 copy.53.refs_0_
  223.2 52.1 %ffn_forward.1 = (bf16[8,128,2048]{2,1,0:T(8,128)(2,1)}, bf16[4,8,64,1024]{3,2,1,0:T(8,128)(2,1)}, bf16[4,8,64,1024]{3,2,1,0:T(8,128)(2,1)}, bf16[1024,1024]{1,0:T(8,128)(2,1)}, bf16[1024,2048]{1,0:T(8,128)(2,1)}) custom-call(bf16[128,2048]{1,0:T(8,128)(2,1)} %copy.53.refs_0_, ...), custom_call_target="tpu_custom_call", output_to_operand_aliasing={{1}: (1, {}), {2}: (2, {})} | custom-call | flops 69000003584 | bytes 216000000 | tf_op jit(solution)/shard_map/ffn_forward/pallas_call | solution.py:748
  275.3 14.0 %convolution_convert_fusion = bf16[2048,2048]{1,0:T(8,128)(2,1)} fusion(bf16[1024,2048]{1,0:T(8,128)(2,1)} %bitcast.117, bf16[1024,2048]{1,0:T(8,128)(2,1)} %get-tuple-element.119.refs_0_.refs_2_), kind=kOutput, calls=%fused_computation.7 | convolution fusion | flops 8594128896 | bytes 16777216 | tf_op jit(solution)/shard_map/dot_general | solution.py:30
  289.4 48.1 %scatter_gn2.1 = f32[128,2048]{1,0:T(8,128)} custom-call(bf16[1024,2048]{1,0:T(8,128)(2,1)} %get-tuple-element.119.refs_0_.refs_2_, bf16[2048,1024]{1,0:T(8,128)(2,1)} %bitcast.115, bf16[1024,2048]{1,0:T(8,128)(2,1)} %get-tuple-element.119.refs_0_.refs_2_, bf16[2048,1024]{1,0:T(8,128)(2,1)} %bitcast.116), custom_call_target="tpu_custom_call" | custom-call | flops 50600001536 | bytes 158400000 | tf_op jit(solution)/shard_map/scatter_gn2/pallas_call | solution.py:748
  337.6 2.7 copy.54
  340.3 2.4 copy.55
  342.6 2.6 copy.56
  345.2 1.7 multiply_reduce_fusion
  346.9 2.3 fusion.16.refs_0_
  349.3 7.8 %convolution_convert_fusion.1 = bf16[1024,2048]{1,0:T(8,128)(2,1)} fusion(bf16[1024,1024]{1,0:T(8,128)(2,1)} %get-tuple-element.115.refs_0_, bf16[1024,2048]{1,0:T(8,128)(2,1)S(1)} %copy-done.38), kind=kOutput, calls=%fused_computation.11 | convolution fusion | flops 4297064448 | bytes 10485760 | tf_op jit(solution)/shard_map/dot_general | solution.py:30
  357.1 52.1 %gather_ga.1 = (bf16[8,128,2048]{2,1,0:T(8,128)(2,1)}, bf16[256,2048]{1,0:T(8,128)(2,1)}) custom-call(bf16[128,2048]{1,0:T(8,128)(2,1)} %fusion.16.refs_0_, bf16[4,256,2048]{2,1,0:T(8,128)(2,1)} %bitcast.118), custom_call_target="tpu_custom_call" | custom-call | flops 57500000256 | bytes 180000000 | tf_op jit(solution)/shard_map/gather_ga/pallas_call | solution.py:748
  409.4 3.9 convolution_convert_fusion.4.go
  413.3 7.4 %attention_back.1 = bf16[1024,768]{1,0:T(8,128)(2,1)S(1)} custom-call(bf16[1024,768]{1,0:T(8,128)(2,1)S(1)} %get-tuple-element.116.rot, bf16[1024,256]{1,0:T(8,128)(2,1)S(1)} %convolution_convert_fusion.4.go, f32[1024,128]{1,0:T(8,128)S(1)} %copy-done.1, f32[1024,128]{1,0:T(8,128)S(1)} %copy-done.3, s32[1024,1]{1,0:T(8,128)S(1)} %copy-done.5), custom_call_target="tpu_custom_call" | custom-call | flops 1342177280 | bytes 6291456 | tf_op jit(solution)/shard_map/attention_back/pallas_call | solution.py:878
  420.8 5.0 fusion.3
  426.0 0.7 pad.15.clone
  426.7 4.8 convolution_convert_fusion.3
  431.5 5.4 convolution_convert_fusion.2
  437.0 94.9 %scatter_gn1.1 = (f32[128,2048]{1,0:T(8,128)}, bf16[64,8192]{1,0:T(8,128)(2,1)}, bf16[64,8192]{1,0:T(8,128)(2,1)}, f32[8,16,256]{2,1,0:T(8,128)}, bf16[64,2048]{...) custom-call(bf16[8,128,2048]{2,1,0:T(8,128)(2,1)} %bitcast.79, bf16[8,64,2048]{2,1,0:T(8,128)(2,1)} %bitcast.76, ...), custom_call_target="tpu_custom_call" | custom-call | flops 1150000000 | bytes 3600000 | tf_op jit(solution)/shard_map/scatter_gn1/pallas_call | solution.py:748
  531.9 1.6 reduce_sum.86.refs_5_
  533.5 1.5 copy.61
  535.8 6.6 %bitcast_convert_fusion.2 = f32[256,8192]{1,0:T(8,128)} fusion(bf16[4,64,8192]{2,1,0:T(8,128)(2,1)} %get-tuple-element.137), kind=kLoop, calls=%fused_computation.10 | loop fusion | flops 2097152 | bytes 12582912 | tf_op jit(solution)/shard_map/convert_element_type | solution.py:1114
  542.4 79.2 %rows_attn.1 = (f32[128,2048]{1,0:T(8,128)}, bf16[192,2048]{1,0:T(8,128)(2,1)}, bf16[4,64,8192]{2,1,0:T(8,128)(2,1)}, bf16[4,64,2048]{2,1,0:T(8,128)(2,1)}, f32[...) custom-call(bf16[1024,1024]{1,0:T(8,128)(2,1)} %get-tuple-element.115.refs_0_, bf16[1024,2048]{1,0:T(8,128)(2,1)} %refs_1_.7, ...), custom_call_target="tpu_custom_call" | custom-call | flops 80499998720 | bytes 252000000 | tf_op jit(solution)/shard_map/rows_attn/pallas_call | solution.py:748
  621.6 1.0 reduce_sum.89
  623.2 2.8 bitcast_convert_fusion.3
  626.0 3.4 fusion.17
  629.4 1.0 copy-done.20
  630.4 4.7 bitcast_convert_fusion.1
  635.1 4.7 bitcast_convert_fusion
  639.9 1.6 fusion.13
  (113 shorter events, 4.3 us)
Async XLA Ops:
  7.2 216.1 %all-gather.4.cloned.1.call-start = ((), (), s32[]{:S(2)}) async-start(), calls=%async_computation.1 | async-start | bytes 4718592 | tf_op jit(solution)/shard_map/all_gather | solution.py:1000
  12.2 0.6 copy-start.32
  12.8 0.6 copy-start.29
  123.4 285.8 %reduce-scatter.2.cloned.1.call-start = ((), (), s32[]{:S(2)}) async-start(), calls=%async_computation.2 | async-start | bytes 10485760 | tf_op jit(solution)/shard_map/reduce_scatter | solution.py:948
  125.9 221.0 %copy-start.24 = (f32[8,1,256]{2,1,0:T(1,128)}, f32[8,1,256]{2,1,0:T(1,128)S(1)}, u32[]{:S(2)}) copy-start(f32[8,1,256]{2,1,0:T(1,128)S(1)} %get-tuple-element.155) | copy-start | bytes 24580
  129.0 11.4 %copy-start.33 = (f32[1024]{0:T(1024)}, f32[1024]{0:T(1024)S(1)}, u32[]{:S(2)}) copy-start(f32[1024]{0:T(1024)S(1)} %add_rsqrt_fusion) | copy-start | bytes 12292
  131.2 9.1 %copy-start = (f32[1024,128]{1,0:T(8,128)}, f32[1024,128]{1,0:T(8,128)S(1)}, u32[]{:S(2)}) copy-start(f32[1024,128]{1,0:T(8,128)S(1)} %get-tuple-element.164.cosine) | copy-start | bytes 1572868
  131.2 9.1 %copy-start.2 = (f32[1024,128]{1,0:T(8,128)}, f32[1024,128]{1,0:T(8,128)S(1)}, u32[]{:S(2)}) copy-start(f32[1024,128]{1,0:T(8,128)S(1)} %get-tuple-element.165.sine) | copy-start | bytes 1572868
  131.4 8.9 %copy-start.27 = (f32[2048]{0:T(1024)}, f32[2048]{0:T(1024)S(1)}, u32[]{:S(2)}) copy-start(f32[2048]{0:T(1024)S(1)} %mul.128) | copy-start | bytes 24580
  131.6 8.7 %copy-start.4 = (s32[1024,1]{1,0:T(8,128)}, s32[1024,1]{1,0:T(8,128)S(1)}, u32[]{:S(2)}) copy-start(s32[1024,1]{1,0:T(8,128)S(1)} %copy.50.piece) | copy-start | bytes 12292
  147.6 0.8 copy-start.6
  220.8 1.0 copy-start.8
  220.8 126.1 %copy-start.30 = (f32[128]{0:T(128)}, f32[128]{0:T(128)S(1)}, u32[]{:S(2)}) copy-start(f32[128]{0:T(128)S(1)} %add_rsqrt_fusion.2) | copy-start | bytes 1540
  289.4 253.1 %all-gather.6.cloned.1.call-start = ((), (), s32[]{:S(2)}) async-start(), calls=%async_computation.3 | async-start | bytes 5242880 | tf_op jit(solution)/shard_map/all_gather | solution.py:952
  337.6 7.6 %copy-start.9 = (f32[128,2048]{1,0:T(8,128)S(1)}, f32[128,2048]{1,0:T(8,128)}, u32[]{:S(2)}) copy-start(f32[128,2048]{1,0:T(8,128)} %copy-done.8) | copy-start | bytes 3145732
  337.6 9.4 %copy-start.17 = (bf16[128,2048]{1,0:T(8,128)(2,1)S(1)}, bf16[128,2048]{1,0:T(8,128)(2,1)}, u32[]{:S(2)}) copy-start(bf16[128,2048]{1,0:T(8,128)(2,1)} %param.33) | copy-start | bytes 1572868
  345.2 4.1 copy-start.38
  346.9 2.4 copy-start.35
  357.1 52.2 %copy-start.37 = (f32[128]{0:T(128)S(1)}, f32[128]{0:T(128)}, u32[]{:S(2)}) copy-start(f32[128]{0:T(128)} %get-tuple-element.152) | copy-start | bytes 1540
  409.3 4.0 copy-start.1
  409.3 4.0 copy-start.3
  409.3 4.0 copy-start.5
  409.3 11.4 %copy-start.39 = (bf16[4,8,64,768]{3,2,1,0:T(8,128)(2,1)S(1)}, bf16[4,8,64,768]{3,2,1,0:T(8,128)(2,1)}, u32[]{:S(2)}) copy-start(bf16[4,8,64,768]{3,2,1,0:T(8,128)(2,1)} %get-tuple-element.106) | copy-start | bytes 9437188
  413.3 7.5 %copy-start.21 = (bf16[8,128,2048]{2,1,0:T(8,128)(2,1)S(1)}, bf16[8,128,2048]{2,1,0:T(8,128)(2,1)}, u32[]{:S(2)}) copy-start(bf16[8,128,2048]{2,1,0:T(8,128)(2,1)} %get-tuple-element.103) | copy-start | bytes 12582916
  413.3 7.5 %copy-start.34 = (f32[1024]{0:T(1024)S(1)}, f32[1024]{0:T(1024)}, u32[]{:S(2)}) copy-start(f32[1024]{0:T(1024)} %copy-done.33) | copy-start | bytes 12292
  420.8 5.9 copy-start.7
  425.9 5.7 copy-start.28
  426.0 5.5 copy-start.22
  531.9 3.6 copy-start.15
  531.9 3.6 copy-start.26
  535.5 7.0 %copy-start.13 = (f32[128,2048]{1,0:T(8,128)}, f32[128,2048]{1,0:T(8,128)S(1)}, u32[]{:S(2)}) copy-start(f32[128,2048]{1,0:T(8,128)S(1)} %copy.63) | copy-start | bytes 3145732
  621.6 4.4 copy-start.12
  626.0 4.4 copy-start.20
  630.4 4.7 copy-start.19
  635.0 4.8 copy-start.10
  635.1 4.8 copy-start.11
  635.1 4.8 copy-start.14
  635.1 4.8 copy-start.16
  635.1 4.8 copy-start.18
  635.1 4.8 copy-start.23
  635.1 4.8 copy-start.25
  635.1 4.8 copy-start.31
  635.1 4.8 copy-start.36
Sparse Core Ops, SparseCore 0:
  123.5 53.5 all-gather.3
  289.5 94.9 reduce-scatter.1
  409.4 67.8 all-gather.5

commit v6 on v5

--- a/solution.py
+++ b/solution.py
@@ -57,14 +57,14 @@
     pl.semaphore_signal(sem, inc=1, device_id={axis: to}, device_id_type=pl.DeviceIdType.MESH)
 
 
-def line_body(n, n_ag, products, a2a_blocks, spreads, n_sum, chain, chain_at, work, parts, *refs):
+def line_body(n, n_ag, products, a2a_blocks, spreads, sum_kinds, chain, chain_at, work, owners, parts, *refs):
     refs = list(refs)
     nz = n // 2
     n_a2a = len(a2a_blocks)
     take = lambda count: [refs.pop(0) for _ in range(count)]
-    n_sp, n_rs = len(spreads), len(products)
-    ag_in, rs_in, a2a_in = take(n_ag), [take(2 * len(t) or 1) for t in products], [take(t[0]) for t in a2a_blocks]
-    sp_in, sum_in = take(n_sp), take(n_sum)
+    n_sp, n_rs, n_sum = len(spreads), len(products), len(sum_kinds)
+    ag_in, rs_in, a2a_in = take(n_ag), [take(sum(2 - made for _, _, made in t) or 1) for t in products], [take(t[0]) for t in a2a_blocks]
+    sp_in, sum_in = take(n_sp), [take(2 if k == 2 else 1) for k in sum_kinds]
     work_in = take(work[1]) if work else []
     ag_out, rs_out, a2a_out, sp_out, sum_out = take(n_ag), take(n_rs), take(n_a2a), take(n_sp), take(n_sum)
     chain_out = take(len(chain))
@@ -72,9 +72,9 @@
     ag_sem = [take(7) for _ in range(n_ag)]
     rs_scr = [take(10 if t else 9) for t in products]
     a2a_sem = [take(3) for _ in range(n_a2a)]
-    sp_sem = [take(5) for _ in range(n_sp)]
-    sum_scr = [take(6) for _ in range(n_sum)]
-    chain_sem = [take(5) for _ in chain]
+    sp_sem = [take(5 + (1 in ph)) for ph in spreads]
+    sum_scr = [take(6 if k == 1 else 7) for k in sum_kinds]
+    chain_sem = [take(6) for _ in chain]
     work_scr = take(work[3]) if work else []
     me = lax.axis_index("inner")
     z, c = me // 2, lax.rem(me, 2)
@@ -228,7 +228,7 @@
 
     class Scatter:
         def __init__(self, operands, flips, out, scratch):
-            self.pairs, self.out = [(x, w) + t for x, w, t in zip(operands[::2], operands[1::2], flips)], out
+            self.pairs, self.out = [(x, w) + t[:2] for x, w, t in zip(operands[::2], operands[1::2], flips)], out
             self.p, *scratch = scratch if flips else operands + scratch
             self.sib_buf, self.l_buf, self.r_buf, self.ss, self.sr, self.rs, self.rr, self.ls, self.lr = scratch
             self.count = out.shape[0] // parts
@@ -321,6 +321,16 @@
 
                 self.left(d, i).start()
 
+        def owners_first(self, rows):
+            tiles = [self.out[rows, k * 128 : (k + 1) * 128] for k in range(self.out.shape[1] // 128)]
+            low = lax.broadcasted_iota(jnp.int32, tiles[0].shape, 1) < 64
+            for k in range(len(tiles)):
+                i = k // 2
+                first = 2 * (k % 2) * n + i
+                a, b = tiles[first // 2], tiles[(first + n) // 2]
+                new = jnp.where(low, pltpu.roll(a, 64, 1), b) if i % 2 else jnp.where(low, a, pltpu.roll(b, 64, 1))
+                self.out[rows, k * 128 : (k + 1) * 128] = new
+
         def end(self):
             @pl.loop(0, parts)
             def _(j):
@@ -337,6 +347,9 @@
                 def _():
                     self.left(z, j, 2).wait_recv()
                     self.out[rows, :] = self.out[rows, :] + self.r_buf[z, rows, :].astype(f32)
+
+                if owners:
+                    self.owners_first(rows)
 
             for d in range(nz):
                 @pl.loop(0, parts)
@@ -411,11 +424,15 @@
     class Spread:
         def __init__(self, src, out, sems, phases):
             self.src, self.out, self.phases = src, out, phases
+            if 1 in phases:
+                self.held, *sems = sems
             self.own_sem, self.send, self.recv, self.send_half, self.recv_half = sems
             self.half, self.here = out.shape[1] // 2, False
 
-        def own(self):
-            return pltpu.make_async_copy(self.src, self.out.at[r], self.own_sem)
+        def own(self, leg):
+            if leg == 0:
+                return pltpu.make_async_copy(self.src, self.held, self.own_sem.at[0])
+            return pltpu.make_async_copy(self.held, self.out.at[r], self.own_sem.at[1])
 
         def first(self, axis):
             to = across_y if axis else across_x
@@ -442,7 +459,7 @@
             if 1 in self.phases:
                 self.first(0).start()
                 self.first(1).start()
-                self.own().start()
+                self.own(0).start()
             else:
                 self.second(0).start()
                 self.second(1).start()
@@ -459,7 +476,9 @@
 
         def end(self):
             if 1 in self.phases:
-                self.own().wait()
+                self.own(0).wait()
+                self.own(1).start()
+                self.own(1).wait()
                 for axis in (0, 1):
                     self.first(axis).wait_send()
                     if 2 not in self.phases:
@@ -476,8 +495,9 @@
                 self.second_came(axis).wait_recv()
 
     class Sum:
-        def __init__(self, p, out, scratch):
-            self.p, self.out = p, out
+        def __init__(self, operands, out, scratch):
+            self.factors, self.out = operands if len(operands) > 1 else None, out
+            self.p, *scratch = scratch if self.factors else operands + scratch
             self.a, self.b, self.send_a, self.recv_a, self.send_b, self.recv_b = scratch
             self.half = out.shape[0] // 2
             self.bits = (lax.rem(r, 2), r // 2)
@@ -511,7 +531,25 @@
             rows = pl.ds(h * self.half + at, step)
             return self.p[q, rows, :].astype(f32) + self.a[h, k, pl.ds(at, step), :].astype(f32)
 
+        def product(self):
+            x, w = self.factors
+            rows, width = self.out.shape
+            tile = min(512, width)
+            while width % tile:
+                tile -= 128
+
+            @pl.loop(0, width // tile)
+            def _(t):
+                cols = pl.ds(pl.multiple_of(t * tile, tile), tile)
+                if rows % 128:
+                    self.p[:, :, cols] = t_dot(x[...], w[:, cols]).astype(bf16).reshape(4, rows, tile)
+                else:
+                    for q in range(4):
+                        self.p[q, :, cols] = t_dot(x[:, q * rows : (q + 1) * rows], w[:, cols]).astype(bf16)
+
         def begin(self):
+            if self.factors:
+                self.product()
             for h in (0, 1):
                 self.first(h, 1 - self.bits[1 - h]).start()
             for h in (0, 1):
@@ -548,12 +586,21 @@
                 self.second(h).wait_send()
 
     gathers = [Gather(*t) for t in zip(ag_in, ag_out, ag_sem)]
+
+    def operands(given, flips):
+        for i, (_, _, made) in enumerate(flips):
+            if made:
+                given.insert(2 * i, work_out[0])
+        return given
+
+    rs_in = [operands(*t) for t in zip(rs_in, products)]
+    sum_in = [given + work_out[:1] if k == 3 else given for given, k in zip(sum_in, sum_kinds)]
     scatters = [Scatter(*t) for t in zip(rs_in, products, rs_out, rs_scr)]
     exchanges = [Exchange(*t) for t in zip(a2a_in, a2a_out, a2a_sem, a2a_blocks)]
     square_parts = [Spread(*t) for t in zip(sp_in, sp_out, sp_sem, spreads)]
     square_parts += [Sum(*t) for t in zip(sum_in, sum_out, sum_scr)]
     chained = [Spread(a2a_out[i], out, sems, (1, 2)) for i, out, sems in zip(chain, chain_out, chain_sem)]
-    worker = work[0](gathers[0], square_parts, nz, z, (r, across_x, across_y, 3 - r), work_in, work_out, work_scr) if work else None
+    worker = work[0](gathers, square_parts, nz, z, (r, across_x, across_y, 3 - r), work_in, work_out, work_scr) if work else None
 
     def begin_chain():
         for i, part in zip(chain, chained):
@@ -561,12 +608,20 @@
             part.begin()
 
     line_parts = gathers + scatters
-    for part in gathers + exchanges + square_parts + scatters:
+    for part in gathers + exchanges:
         part.begin()
-    if worker:
+    if worker and worker.early:
+        worker.begin()
+    for part in square_parts:
+        part.begin()
+    if chain and worker:
+        begin_chain()
+    for part in scatters:
+        part.begin()
+    if worker and not worker.early:
         worker.begin()
     if line_parts:
-        if chain_at == 0:
+        if chain_at == 0 and not worker:
             begin_chain()
         for s in range(1, nz):
             @pl.loop(0, parts)
@@ -595,8 +650,57 @@
         part.end()
 
 
+class Backward:
+    early = True
+
+    def __init__(self, gathers, spreads, nz, z, blocks, ins, outs, scratch):
+        self.ga, self.w_out, self.rot, self.cosine, self.sine, self.piece = ins
+        (self.out,) = outs
+        self.go, self.gk, self.gv = scratch
+
+    def begin(self):
+        length, width = self.rot.shape
+        heads, blocks = width // 3 // HEAD_DIM, length // PIECE
+        rot, out, cosine, sine, gk, gv = self.rot, self.out, self.cosine, self.sine, self.gk, self.gv
+        inv_root = 1.0 / math.sqrt(HEAD_DIM)
+
+        @pl.loop(0, blocks)
+        def _(i):
+            rows = pl.ds(pl.multiple_of(i * PIECE, PIECE), PIECE)
+            self.go[rows, :] = dot_t(self.ga[rows, :], self.w_out[...]).astype(bf16)
+
+        @pl.loop(0, heads)
+        def _(h):
+            at = lambda part: pl.ds(pl.multiple_of((part * heads + h) * HEAD_DIM, HEAD_DIM), HEAD_DIM)
+            gk[...] = jnp.zeros_like(gk)
+            gv[...] = jnp.zeros_like(gv)
+            for i in range(blocks):
+                keys = (i + 1) * PIECE
+                own = pl.ds(i * PIECE, PIECE)
+                q, g = rot[own, at(0)], self.go[own, at(0)]
+                sg, visible = squash(q, rot[0:keys, at(1)], self.piece[own, :], keys, length)
+                p = masked(sg, visible, keys).astype(bf16)
+                gs = masked(dot_t(g, rot[0:keys, at(2)]) * sg * (1.0 - sg), visible, keys).astype(bf16)
+                gq = dot(gs, rot[0:keys, at(1)]) * inv_root
+                out[own, at(0)] = rotate(gq, cosine[own, :], -sine[own, :]).astype(bf16)
+                gk[0:keys, :] += t_dot(gs, q)
+                gv[0:keys, :] += t_dot(p, g)
+
+            @pl.loop(0, blocks)
+            def _(i):
+                rows = pl.ds(pl.multiple_of(i * PIECE, PIECE), PIECE)
+                out[rows, at(1)] = rotate(gk[rows, :] * inv_root, cosine[rows, :], -sine[rows, :]).astype(bf16)
+                out[rows, at(2)] = gv[rows, :].astype(bf16)
+
+    def after_step(self, s):
+        pass
+
+
 class Forward:
-    def __init__(self, gather, spreads, nz, z, blocks, ins, outs, scratch):
+    early = False
+
+    def __init__(self, gathers, spreads, nz, z, blocks, ins, outs, scratch):
+        (gather,) = gathers
         self.gather, self.spreads, self.nz, self.z, self.blocks = gather, spreads, nz, z, blocks
         self.cot, self.w_down = ins[:2]
         self.hid, self.ggu = outs
@@ -685,22 +789,43 @@
                 self.away(k)
 
 
-def line_comm(cid, name, us, ag=(), rs=(), a2a=(), spread=(), sums=(), chain=(), chain_at=None, work=None, parts=2):
+class Later:
+    early = False
+
+    def __init__(self, gathers, spreads, nz, z, blocks, ins, outs, scratch):
+        (self.x, self.w), (self.out,) = ins, outs
+        self.steps, self.tile = nz - 1, min(512, self.out.shape[1])
+
+    def begin(self):
+        pass
+
+    def after_step(self, s):
+        tiles = self.out.shape[1] // self.tile
+
+        @pl.loop(tiles * (s - 1) // self.steps, tiles * s // self.steps)
+        def _(t):
+            cols = pl.ds(pl.multiple_of(t * self.tile, self.tile), self.tile)
+            self.out[:, cols] = t_dot(self.x[...], self.w[:, cols]).astype(bf16)
+
+
+def line_comm(cid, name, us, ag=(), rs=(), a2a=(), spread=(), sums=(), chain=(), chain_at=None, work=None, owners=False, parts=2):
     n = lax.axis_size("inner")
     nz = n // 2
     chain_at = nz - 2 if chain_at is None else chain_at
     dma = pltpu.SemaphoreType.DMA
     hbm = pl.BlockSpec(memory_space=pl.ANY)
     vmem = pl.BlockSpec(memory_space=pltpu.VMEM)
-    products = [tuple(t[2:] for t in p) if isinstance(p, list) else () for p in rs]
+    products = [tuple(t[2:] + (t[0] is None,) for t in p) if isinstance(p, list) else () for p in rs]
     rs_out = [
-        (p[0][0].shape[0] // n, p[0][1].shape[0 if p[0][2] else 1]) if isinstance(p, list) else (p.shape[0] // n, p.shape[1])
+        (p[0][0].shape[0] // n if p[0][0] is not None else work[2][0][0] // n, p[0][1].shape[0 if p[0][2] else 1]) if isinstance(p, list) else (p.shape[0] // n, p.shape[1])
         for p in rs
     ]
     rs_in = []
     for p, shape in zip(rs, rs_out):
-        rs_in += [a for t in p for a in t[:2]] if isinstance(p, list) else [p.reshape((n,) + shape)]
-    sums = [p.reshape((4, p.shape[0] // 4) + p.shape[1:]) for p in sums]
+        rs_in += [a for t in p for a in t[:2] if a is not None] if isinstance(p, list) else [p.reshape((n,) + shape)]
+    sum_shapes = [(p[0].shape[1] // 4, p[2]) if isinstance(p, tuple) else (p.shape[0] // 4, p.shape[1]) for p in sums]
+    sum_kinds = [(3 if p[1] is None else 2) if isinstance(p, tuple) else 1 for p in sums]
+    sums = [p[:2] if isinstance(p, tuple) else (p.reshape((4,) + shape),) for p, shape in zip(sums, sum_shapes)]
     work_in, work_out, work_scratch = work[1:] if work else ((), (), [])
     inputs, in_specs, out_shape, out_specs, scratch = [], [], [], [], []
 
@@ -718,7 +843,7 @@
     give([w for t in a2a for w in t[0]], hbm)
     aliases = {len(inputs) + i: len(ag) + len(rs) + len(a2a) + i for i, (_, ph) in enumerate(spread) if 1 not in ph}
     give([b for b, _ in spread], hbm)
-    give(sums, vmem)
+    give([x for p in sums for x in p if x is not None], vmem)
     give(work_in, vmem)
     for x in ag:
         get((n,) + x.shape, x.dtype, near)
@@ -733,15 +858,17 @@
         scratch += [dma((t[4],)), dma((n, t[4])), dma((n, t[4]))]
     for b, phases in spread:
         get(b.shape if 1 not in phases else (4,) + b.shape, b.dtype, hbm)
-        scratch += [dma, dma((2,)), dma((2,)), dma((2,)), dma((2,))]
-    for p in sums:
-        get(p.shape[1:], bf16, vmem)
-        half = (p.shape[1] // 2, p.shape[2])
+        scratch += [pltpu.VMEM(b.shape, b.dtype)] if 1 in phases else []
+        scratch += [dma((2,)), dma((2,)), dma((2,)), dma((2,)), dma((2,))]
+    for p, shape in zip(sums, sum_shapes):
+        get(shape, bf16, vmem)
+        half = (shape[0] // 2, shape[1])
+        scratch += [pltpu.VMEM((4,) + shape, bf16)] if len(p) > 1 else []
         scratch += [pltpu.VMEM((2, 2) + half, bf16), pltpu.VMEM((2,) + half, bf16)]
         scratch += [dma((2, 2)), dma((2, 2)), dma((2,)), dma((2,))]
     for i in chain:
         get((4,) + a2a[i][1], a2a[i][0][0].dtype, hbm)
-        scratch += [dma, dma((2,)), dma((2,)), dma((2,)), dma((2,))]
+        scratch += [pltpu.VMEM(a2a[i][1], a2a[i][0][0].dtype), dma((2,)), dma((2,)), dma((2,)), dma((2,)), dma((2,))]
     for shape in work_out:
         get(shape, bf16, vmem)
     scratch += work_scratch
@@ -753,10 +880,11 @@
             products,
             [(len(t[0]),) + t[2:6] for t in a2a],
             [ph for _, ph in spread],
-            len(sums),
+            sum_kinds,
             chain,
             chain_at,
             (work[0], len(work_in), len(work_out), len(work_scratch)) if work else None,
+            owners,
             parts,
         ),
         out_shape=out_shape,
@@ -835,65 +963,6 @@
         ),
         name="attention",
     )(lin, cosine, sine, piece)
-
-
-def attn_back_body(heads, length, rot, go, cosine, sine, piece, out, gk, gv):
-    h, b = pl.program_id(0), pl.program_id(1)
-    at = lambda part: pl.ds(pl.multiple_of((part * heads + h) * HEAD_DIM, HEAD_DIM), HEAD_DIM)
-    blocks = length // PIECE
-    inv_root = 1.0 / math.sqrt(HEAD_DIM)
-
-    @pl.when(b == 0)
-    def _():
-        gk[...] = jnp.zeros_like(gk)
-        gv[...] = jnp.zeros_like(gv)
-
-    for i in range(blocks):
-        @pl.when(b == i)
-        def _():
-            keys = (i + 1) * PIECE
-            own = pl.ds(i * PIECE, PIECE)
-            q, g = rot[own, at(0)], go[...]
-            sg, visible = squash(q, rot[0:keys, at(1)], piece[...], keys, length)
-            p = masked(sg, visible, keys).astype(bf16)
-            gs = masked(dot_t(g, rot[0:keys, at(2)]) * sg * (1.0 - sg), visible, keys).astype(bf16)
-            gq = dot(gs, rot[0:keys, at(1)]) * inv_root
-            out[own, at(0)] = rotate(gq, cosine[own, :], -sine[own, :]).astype(bf16)
-            gk[0:keys, :] += t_dot(gs, q)
-            gv[0:keys, :] += t_dot(p, g)
-
-    @pl.when(b == blocks - 1)
-    def _():
-        @pl.loop(0, blocks)
-        def _(i):
-            rows = pl.ds(pl.multiple_of(i * PIECE, PIECE), PIECE)
-            out[rows, at(1)] = rotate(gk[rows, :] * inv_root, cosine[rows, :], -sine[rows, :]).astype(bf16)
-            out[rows, at(2)] = gv[rows, :].astype(bf16)
-
-
-def attention_back(rot, go, cosine, sine, piece):
-    length, width = rot.shape
-    heads = width // 3 // HEAD_DIM
-    whole = lambda x: pl.BlockSpec(x.shape, lambda h, b: (0, 0))
-    return pl.pallas_call(
-        functools.partial(attn_back_body, heads, length),
-        grid=(heads, length // PIECE),
-        out_shape=jax.ShapeDtypeStruct((length, width), bf16),
-        in_specs=[
-            whole(rot),
-            pl.BlockSpec((PIECE, HEAD_DIM), lambda h, b: (b, h)),
-            whole(cosine),
-            whole(sine),
-            pl.BlockSpec((PIECE, 1), lambda h, b: (b, 0)),
-        ],
-        out_specs=pl.BlockSpec((length, width), lambda h, b: (0, 0)),
-        scratch_shapes=[pltpu.VMEM((length, HEAD_DIM), f32)] * 2,
-        compiler_params=pltpu.CompilerParams(vmem_limit_bytes=48 * 2**20),
-        cost_estimate=pl.CostEstimate(
-            flops=10 * heads * length * length * HEAD_DIM // 2, bytes_accessed=8 * length * width, transcendentals=heads * length * length
-        ),
-        name="attention_back",
-    )(rot, go, cosine, sine, piece)
 
 
 def columns_out(w):
@@ -1033,12 +1102,12 @@
         w_g, w_u = flat(w_g), flat(w_u)
         n2, hid, ggu = line_comm(3, "ffn_forward", 60, ag=[n2], work=(Forward, [cot, w_down, w_g, w_u], results, held))
 
-    g_down = t_dot(hid, cot).astype(bf16)
     gu = t_dot(n2, ggu).astype(bf16)
     gu, ggu = after((gu, ggu))
     gu_share = sum_share(gu)
-    (gn2,) = line_comm(4, "scatter_gn2", 44, rs=[[(ggu, w_g, True, 0), (ggu, w_u, True, w_g.shape[1])]])
-    gn2 = owners_first(gn2)
+    tidy = square and width // n // nr == 64
+    gn2, g_down = line_comm(4, "scatter_gn2", 44, owners=tidy, work=(Later, [hid, cot], [w_down.shape], []), rs=[[(ggu, w_g, True, 0), (ggu, w_u, True, w_g.shape[1])]])
+    gn2 = gn2 if tidy else owners_first(gn2)
     gu2 = gn2 * ffn_gain
     ffn_gain_part = jnp.sum(gn2 * u2, axis=0)
     gmid = cotangent.astype(f32) + r2 * (gu2 - u2 * jnp.mean(gu2 * u2, axis=1, keepdims=True))
@@ -1050,58 +1119,62 @@
     ga, down_share, gu_share = after((ga, down_share, gu_share))
     grad_down = join(down_share)
 
-    go = dot_t(ga, w_out).astype(bf16)
-    gqkv = attention_back(rot, go, cosine, sine, pieces)
-    g_out = t_dot(o, ga).astype(bf16)
-    g_qkv = t_dot(n1, gqkv).astype(bf16)
-    gn1_part = dot_t(gqkv, w_qkv)
-    attn_gain_part = jnp.sum(gn1_part * u1, axis=0, keepdims=True)
-    gn1_part = gn1_part.astype(bf16)
-    gains = jnp.stack([owners_first(attn_gain_part)[0].reshape(n, rows), ffn_gain_part.reshape(n, rows)], axis=1)
-    gains = jnp.pad(gains, ((0, 0), (0, 14), (0, 0))).reshape(n * 16, rows)
     cols = w_gate.shape[1] // n
-    head_cols = gqkv.shape[1] // 3
+    heads_width = rot.shape[1] // 3
     gu_share = gu_share.reshape(n, -1, 2 * cols)
+    own_x = tokens.astype(f32)
+    r1 = rms_scale(own_x)
+    u1 = own_x * r1
+
+    def gain_parts(gn1):
+        both = jnp.stack([jnp.sum(gn1 * u1, axis=0).reshape(n, rows), ffn_gain_part.reshape(n, rows)], axis=1)
+        return sum_blocks(jnp.pad(both, ((0, 0), (0, 14), (0, 0))).reshape(n * 16, rows))
+
+    held = [pltpu.VMEM((length, heads_width), bf16)] + [pltpu.VMEM((length, HEAD_DIM), f32)] * 2
+    work = (Backward, [ga, w_out, rot, cosine, sine, pieces], [rot.shape], held)
+    gn1_part = [(None, w_qkv, True, 0)]
     if square:
-        gn1, gate_rows, up_rows, gains, out_share, qkv_share, grad_gate = line_comm(
+        gn1, gate_rows, up_rows, out_share, qkv_share, grad_gate, _ = line_comm(
             6,
             "scatter_gn1",
             1,
+            owners=tidy,
             rs=[gn1_part],
-            a2a=[rows_back(gu_share, (0, cols), 1), rows_back(gu_share, (1, cols), 1, True), sum_blocks(gains)],
-            sums=[g_out, g_qkv],
+            a2a=[rows_back(gu_share, (0, cols), 1), rows_back(gu_share, (1, cols), 1, False)],
+            sums=[(o, ga, width), (n1, None, rot.shape[1])],
             chain=(0,),
             chain_at=0,
+            work=work,
         )
-        gains = jnp.sum(gains, axis=0)
-        qkv_back = rows_back(qkv_share.reshape(n, -1, 3 * head_cols), (0, head_cols), 3)
-        gains, grad_down = after((gains, grad_down))
-        mlp, qkv_rows, grad_up, grad_out, gains, grad_qkv = line_comm(
+        gn1 = gn1 if tidy else owners_first(gn1)
+        qkv_back = rows_back(qkv_share.reshape(n, -1, 3 * heads_width), (0, heads_width), 3)
+        up_rows, grad_down = after((up_rows, grad_down))
+        mlp, _, _, grad_up, grad_out, grad_qkv, gains = line_comm(
             7,
             "rows_attn",
             70,
             rs=[[(hid, w_down, False, 0)]],
-            a2a=[qkv_back],
-            spread=[(up_rows, (1, 2)), (out_share, (1, 2)), (gains, (1, 2))],
-            chain=(0,),
+            a2a=[qkv_back, gain_parts(gn1)],
+            spread=[(up_rows, (1, 2)), (out_share, (1, 2))],
+            chain=(0, 1),
             chain_at=0,
         )
-        gains = jnp.sum(gains, axis=0)
+        gains = jnp.sum(gains, axis=(0, 1))
     else:
         gu_back = rows_back(gu_share, (0, cols), 2)
-        gn1, gu_rows, gains = line_comm(6, "scatter_gn1", 80, rs=[gn1_part], a2a=[gu_back, sum_blocks(gains)])
+        gn1, gu_rows, gqkv = line_comm(6, "scatter_gn1", 80, rs=[gn1_part], a2a=[gu_back], work=work)
+        gn1 = owners_first(gn1)
+        g_qkv = sum_share(t_dot(n1, gqkv))
+        qkv_back = rows_back(g_qkv.reshape(n, -1, 3 * heads_width), (0, heads_width), 3)
+        mlp, qkv_rows, gains = line_comm(
+            7, "rows_attn", 75, rs=[[(hid, w_down, False, 0)]], a2a=[qkv_back, gain_parts(gn1)]
+        )
         gains = lax.psum(jnp.sum(gains, axis=0), "replica")
-        qkv_back = rows_back(sum_share(g_qkv).reshape(n, -1, 3 * head_cols), (0, head_cols), 3)
-        mlp, qkv_rows = line_comm(7, "rows_attn", 75, rs=[[(hid, w_down, False, 0)]], a2a=[qkv_back])
         grad_gu = join(gu_rows).reshape(nr, 2, -1, n * cols)
-        grad_gate, grad_up, grad_out, grad_qkv = grad_gu[:, 0], grad_gu[:, 1], join(sum_share(g_out)), join(qkv_rows)
+        grad_gate, grad_up, grad_out, grad_qkv = grad_gu[:, 0], grad_gu[:, 1], join(sum_share(t_dot(o, ga))), join(qkv_rows)
     output = (mid + mlp).astype(bf16)
     grad_qkv = grad_qkv.reshape(nr, 3, -1, width).astype(f32)
 
-    gn1 = owners_first(gn1)
-    own_x = tokens.astype(f32)
-    r1 = rms_scale(own_x)
-    u1 = own_x * r1
     gu1 = gn1 * attn_gain
     grad_tokens = gmid + r1 * (gu1 - u1 * jnp.mean(gu1 * u1, axis=1, keepdims=True))
     return (

time: 656 us -> 639 us (0.974)
  matrix products: 49.7 us -> 22.6 us
  Pallas kernels: 519 us -> 536 us
  local copies, waits for them, and re-layouts: 26.1 us -> 15.8 us
    pallas_call x8, Pallas kernels: 504 us -> 528 us  [line_comm(): pl.pallas_call(functools.partial(line_body, n, len(ag), products, [(len(t...]
    dot_general x4 -> x1, matrix products: 32.1 us -> 14 us  [t_dot(): return lax.dot_general(a, b, dims_cols, preferred_element_type=f32)]
    dot_general x2 -> x0, matrix products: 8.98 us -> none  [dot_t(): return lax.dot_general(a, b, dims_rows, preferred_element_type=f32)]
    pallas_call x1 -> x0, Pallas kernels: 7.42 us -> none  [attention_back(): pl.pallas_call(functools.partial(attn_back_body, heads, length), grid=(he...]
  transfers between devices with their start and end apart: 3 -> 3, of which waited for: 0 -> 0; matrix products, arithmetic and copies ran while one was open for 11% -> 6% of each run, Pallas kernels for 43% -> 46%
where the time goes in v6:
time: 639 us; the launch traced here: 631 us
  Pallas kernels  536 us (84%)
  other arithmetic  42.2 us (7%)
  matrix products  22.6 us (4%)
  local copies, waits for them, and re-layouts  15.8 us (2%)
  between operations  14.4 us (2%)
    pallas_call x8, Pallas kernels, line_comm(): pl.pallas_call(functools.partial(line_body, n, len(ag), products, [(len(t...  528 us
    dot_general x1, matrix products, t_dot(): return lax.dot_general(a, b, dims_cols, preferred_element_type=f32)  14 us
  transfers between devices with their start and end apart: 3, of which 0 were waited for; matrix products, arithmetic and copies ran while one was open for 6% of the time, Pallas kernels for 46%

profile of v6, /device:TPU:0, one launch (start us, length us, event | category | flops | bytes accessed | tf_op | source)
XLA Modules:
  0.0 630.7 jit_solution(3951358549411728889)
XLA Ops:
  7.2 0.7 reshape.234
  7.9 0.7 convert.12
  8.5 1.3 copy.28
  9.9 1.0 copy.30.refs_0_
  10.9 0.7 scatter.16
  11.6 0.7 scatter.19.refs_3_
  12.3 0.6 copy-done.25
  12.8 0.6 copy-done.22
  13.4 26.1 %load_attn.1 = (bf16[8,64,256]{2,1,0:T(8,128)(2,1)}, bf16[8,64,256]{2,1,0:T(8,128)(2,1)}, bf16[8,64,256]{2,1,0:T(8,128)(2,1)}, s32[8,8,128]{2,1,0:T(8,128)}, f32[8,8,256]{2,1,0:T(8,128)}) custom-call(bf16[256,2048]{1,0:T(8,128)(2,1)} %refs_0_.1, bf16[256,2048]{1,0:T(8,128)(2,1)} %refs_1_.4, bf16[256,2048]{1,0:T(8,128)(2,1)} %refs_2_.2, s32[8,128]{1,0:T(8,128)} %copy-done.25, ...), custom_call_target="tpu_custom_call" | custom-call | flops 28750000128 | bytes 90000000 | tf_op jit(solution)/shard_map/load_attn/pallas_call | solution.py:875
  39.6 2.0 pad_maximum_fusion.refs_3_
  41.6 82.7 %load_ffn.1 = (bf16[8,128,2048]{2,1,0:T(8,128)(2,1)}, bf16[8,64,1024]{2,1,0:T(8,128)(2,1)}, bf16[8,64,1024]{2,1,0:T(8,128)(2,1)}, bf16[4,8,64,768]{3,2,1,0:T(8,128)(2,1)}) custom-call(bf16[128,2048]{1,0:T(8,128)(2,1)} %copy.30.refs_0_, bf16[256,8192]{1,0:T(8,128)(2,1)} %refs_1_.5, bf16[256,8192]{1,0:T(8,128)(2,1)} %refs_2_.3, ...), custom_call_target="tpu_custom_call" | custom-call | flops 92000002048 | bytes 288000000 | tf_op jit(solution)/shard_map/load_ffn/pallas_call | solution.py:875
  124.4 0.8 slice_bitcast_fusion
  125.2 1.5 fusion.15
  126.8 0.1 reshape_reshape_squeeze.3
  126.8 0.1 mul.128
  126.9 3.2 fusion
  130.2 1.9 fusion.12
  132.1 3.0 fusion.2.refs_5_
  135.1 0.3 pad_maximum_fusion.1
  135.5 0.2 copy.32.piece.refs_11_
  135.7 8.6 %fusion.17.lin = f32[1024,768]{1,0:T(8,128)} fusion(bf16[1024,2048]{1,0:T(8,128)(2,1)} %fusion.2.refs_5_, bf16[2048,768]{1,0:T(8,128)(2,1)} %bitcast.65), kind=kOutput, calls=%fused_computation.51 | convolution fusion | flops 3221225472 | bytes 10485760 | tf_op jit(solution)/shard_map/dot_general | solution.py:22
  144.3 7.3 %attention.1 = (bf16[1024,256]{1,0:T(8,128)(2,1)S(1)}, bf16[1024,768]{1,0:T(8,128)(2,1)S(1)}) custom-call(f32[1024,768]{1,0:T(8,128)} %fusion.17.lin, f32[1024,128]{1,0:T(8,128)S(1)} %get-tuple-element.165.cosine.refs_9_, f32[1024,128]{1,0:T(8,128)S(1)} %get-tuple-element.166.sine.refs_10_, s32[1024,1]{1,0:T(8,128)S(1)} %copy.32.piece.refs_11_), custom_call_target="tpu_custom_call" | custom-call | flops 536870912 | bytes 6291456 | tf_op jit(solution)/shard_map/attention/pallas_call | solution.py:948
  151.6 1.1 copy-done.3
  152.7 0.8 copy-done.4
  153.5 52.4 %attn_out.1 = (f32[128,2048]{1,0:T(8,128)}, bf16[4,8,64,1024]{3,2,1,0:T(8,128)(2,1)}, bf16[4,8,64,1024]{3,2,1,0:T(8,128)(2,1)}) custom-call(bf16[1024,256]{1,0:T(8,128)(2,1)} %copy-done.4, bf16[256,2048]{1,0:T(8,128)(2,1)} %refs_7_.1, bf16[8,64,1024]{2,1,0:T(8,128)(2,1)} %get-tuple-element.110.refs_2_, bf16[8,64,1024]{2,1,0:T(8,128)(2,1)} %get-tuple-element.111.refs_3_), custom_call_target="tpu_custom_call" | custom-call | flops 57500000256 | bytes 180000000 | tf_op jit(solution)/shard_map/attn_out/pallas_call | solution.py:875
  205.9 2.0 multiply_reduce_fusion.2
  208.0 0.2 multiply_convert_fusion
  208.1 0.3 copy.33
  208.4 1.0 copy.35.refs_0_
  209.4 53.0 %ffn_forward.1 = (bf16[8,128,2048]{2,1,0:T(8,128)(2,1)}, bf16[4,8,64,1024]{3,2,1,0:T(8,128)(2,1)}, bf16[4,8,64,1024]{3,2,1,0:T(8,128)(2,1)}, bf16[1024,1024]{1,0:T(8,128)(2,1)}, bf16[1024,2048]{1,0:T(8,128)(2,1)}) custom-call(bf16[128,2048]{1,0:T(8,128)(2,1)} %copy.35.refs_0_, ...), custom_call_target="tpu_custom_call", output_to_operand_aliasing={{1}: (1, {}), {2}: (2, {})} | custom-call | flops 69000003584 | bytes 216000000 | tf_op jit(solution)/shard_map/ffn_forward/pallas_call | solution.py:875
  262.4 14.0 %convolution_convert_fusion = bf16[2048,2048]{1,0:T(8,128)(2,1)} fusion(bf16[1024,2048]{1,0:T(8,128)(2,1)} %bitcast.94, bf16[1024,2048]{1,0:T(8,128)(2,1)} %get-tuple-element.119.refs_0_.refs_2_), kind=kOutput, calls=%fused_computation.5 | convolution fusion | flops 8594128896 | bytes 16777216 | tf_op jit(solution)/shard_map/dot_general | solution.py:30
  276.5 51.8 %scatter_gn2.1 = (f32[128,2048]{1,0:T(8,128)}, bf16[1024,2048]{1,0:T(8,128)(2,1)}) custom-call(bf16[1024,2048]{1,0:T(8,128)(2,1)} %get-tuple-element.119.refs_0_.refs_2_, bf16[2048,1024]{1,0:T(8,128)(2,1)} %bitcast.91, bf16[1024,2048]{1,0:T(8,128)(2,1)} %get-tuple-element.119.refs_0_.refs_2_, bf16[2048,1024]{1,0:T(8,128)(2,1)} %bitcast.92, ...), custom_call_target="tpu_custom_call" | custom-call | flops 50600001536 | bytes 158400000 | tf_op jit(solution)/shard_map/scatter_gn2/pallas_call | solution.py:875
  328.3 1.6 multiply_reduce_fusion
  330.0 2.4 fusion.13.refs_0_
  332.3 64.1 %gather_ga.1 = (bf16[8,128,2048]{2,1,0:T(8,128)(2,1)}, bf16[256,2048]{1,0:T(8,128)(2,1)}) custom-call(bf16[128,2048]{1,0:T(8,128)(2,1)} %fusion.13.refs_0_, bf16[4,256,2048]{2,1,0:T(8,128)(2,1)} %bitcast.93), custom_call_target="tpu_custom_call" | custom-call | flops 57500000256 | bytes 180000000 | tf_op jit(solution)/shard_map/gather_ga/pallas_call | solution.py:875
  396.5 115.2 %scatter_gn1.1 = (f32[128,2048]{1,0:T(8,128)}, bf16[64,8192]{1,0:T(8,128)(2,1)}, bf16[64,8192]{1,0:T(8,128)(2,1)}, bf16[64,2048]{1,0:T(8,128)(2,1)}, bf16[512,76...) custom-call(bf16[2048,768]{1,0:T(8,128)(2,1)} %bitcast.66, bf16[8,64,2048]{2,1,0:T(8,128)(2,1)} %bitcast.62, ...), custom_call_target="tpu_custom_call" | custom-call | flops 1150000000 | bytes 3600000 | tf_op jit(solution)/shard_map/scatter_gn1/pallas_call | solution.py:875
  511.8 1.6 fusion.7
  513.4 0.7 select_maximum_fusion
  514.1 6.6 %bitcast_convert_fusion.2 = f32[256,8192]{1,0:T(8,128)} fusion(bf16[4,64,8192]{2,1,0:T(8,128)(2,1)} %get-tuple-element.139), kind=kLoop, calls=%fused_computation.8 | loop fusion | flops 2097152 | bytes 12582912 | tf_op jit(solution)/shard_map/convert_element_type | solution.py:1187
  520.6 83.1 %rows_attn.1 = (f32[128,2048]{1,0:T(8,128)}, bf16[192,2048]{1,0:T(8,128)(2,1)}, f32[8,16,256]{2,1,0:T(8,128)}, bf16[4,64,8192]{2,1,0:T(8,128)(2,1)}, bf16[4,64,2...) custom-call(bf16[1024,1024]{1,0:T(8,128)(2,1)} %get-tuple-element.116.refs_4_.refs_0_, ...), custom_call_target="tpu_custom_call" | custom-call | flops 80499998720 | bytes 252000000 | tf_op jit(solution)/shard_map/rows_attn/pallas_call | solution.py:875
  603.7 1.2 reduce_sum.79
  605.0 0.6 fusion.16
  605.5 2.8 bitcast_convert_fusion.3
  608.3 3.4 fusion.14
  611.7 1.0 copy-done.16
  612.7 4.7 bitcast_convert_fusion.1
  617.5 4.7 bitcast_convert_fusion
  622.3 1.6 fusion.10
  (73 shorter events, 0.5 us)
Async XLA Ops:
  7.2 202.3 %all-gather.4.cloned.1.call-start = ((), (), s32[]{:S(2)}) async-start(), calls=%async_computation.1 | async-start | bytes 4718592 | tf_op jit(solution)/shard_map/all_gather | solution.py:1069
  12.2 0.6 copy-start.25
  12.8 0.6 copy-start.22
  124.3 272.1 %reduce-scatter.2.cloned.1.call-start = ((), (), s32[]{:S(2)}) async-start(), calls=%async_computation.2 | async-start | bytes 10485760 | tf_op jit(solution)/shard_map/reduce_scatter | solution.py:1017
  126.8 203.2 %copy-start.19 = (f32[8,1,256]{2,1,0:T(1,128)}, f32[8,1,256]{2,1,0:T(1,128)S(1)}, u32[]{:S(2)}) copy-start(f32[8,1,256]{2,1,0:T(1,128)S(1)} %get-tuple-element.157) | copy-start | bytes 24580
  126.9 5.1 copy-start.7
  135.5 8.8 %copy-start = (f32[1024,128]{1,0:T(8,128)}, f32[1024,128]{1,0:T(8,128)S(1)}, u32[]{:S(2)}) copy-start(f32[1024,128]{1,0:T(8,128)S(1)} %get-tuple-element.165.cosine.refs_9_) | copy-start | bytes 1572868
  135.5 8.8 %copy-start.1 = (f32[1024,128]{1,0:T(8,128)}, f32[1024,128]{1,0:T(8,128)S(1)}, u32[]{:S(2)}) copy-start(f32[1024,128]{1,0:T(8,128)S(1)} %get-tuple-element.166.sine.refs_10_) | copy-start | bytes 1572868
  135.7 8.6 %copy-start.2 = (s32[1024,1]{1,0:T(8,128)}, s32[1024,1]{1,0:T(8,128)S(1)}, u32[]{:S(2)}) copy-start(s32[1024,1]{1,0:T(8,128)S(1)} %copy.32.piece.refs_11_) | copy-start | bytes 12292
  151.6 1.1 copy-start.3
  152.7 0.8 copy-start.4
  153.5 52.4 %copy-start.10 = (bf16[128,2048]{1,0:T(8,128)(2,1)S(1)}, bf16[128,2048]{1,0:T(8,128)(2,1)}, u32[]{:S(2)}) copy-start(bf16[128,2048]{1,0:T(8,128)(2,1)} %param.21) | copy-start | bytes 1572868
  207.9 122.0 %copy-start.5 = (f32[128,2048]{1,0:T(8,128)}, f32[128,2048]{1,0:T(8,128)S(1)}, u32[]{:S(2)}) copy-start(f32[128,2048]{1,0:T(8,128)S(1)} %get-tuple-element.148) | copy-start | bytes 3145732
  207.9 122.0 %copy-start.23 = (f32[128]{0:T(128)}, f32[128]{0:T(128)S(1)}, u32[]{:S(2)}) copy-start(f32[128]{0:T(128)S(1)} %add_rsqrt_fusion.2) | copy-start | bytes 1540
  276.5 244.2 %all-gather.6.cloned.1.call-start = ((), (), s32[]{:S(2)}) async-start(), calls=%async_computation.3 | async-start | bytes 5242880 | tf_op jit(solution)/shard_map/all_gather | solution.py:1021
  276.5 53.4 %copy-start.13 = (bf16[128,2048]{1,0:T(8,128)(2,1)S(1)}, bf16[128,2048]{1,0:T(8,128)(2,1)}, u32[]{:S(2)}) copy-start(bf16[128,2048]{1,0:T(8,128)(2,1)} %param.33) | copy-start | bytes 1572868
  329.9 2.4 copy-start.26
  332.3 64.2 %copy-start.28 = (f32[128]{0:T(128)S(1)}, f32[128]{0:T(128)}, u32[]{:S(2)}) copy-start(f32[128]{0:T(128)} %get-tuple-element.154) | copy-start | bytes 1540
  396.5 115.2 %copy-start.11 = (bf16[128,2048]{1,0:T(8,128)(2,1)S(1)}, bf16[128,2048]{1,0:T(8,128)(2,1)}, u32[]{:S(2)}) copy-start(bf16[128,2048]{1,0:T(8,128)(2,1)} %param.21) | copy-start | bytes 1572868
  396.5 115.2 %copy-start.21 = (f32[8,1,256]{2,1,0:T(1,128)S(1)}, f32[8,1,256]{2,1,0:T(1,128)}, u32[]{:S(2)}) copy-start(f32[8,1,256]{2,1,0:T(1,128)} %get-tuple-element.155) | copy-start | bytes 24580
  603.7 4.6 copy-start.8
  608.3 4.4 copy-start.16
  612.7 4.7 copy-start.15
  617.4 4.8 copy-start.6
  617.4 4.8 copy-start.9
  617.4 4.8 copy-start.12
  617.4 4.8 copy-start.14
  617.4 4.8 copy-start.17
  617.4 4.8 copy-start.18
  617.4 4.8 copy-start.20
  617.4 4.8 copy-start.24
  617.4 4.8 copy-start.27
Sparse Core Ops, SparseCore 0:
  124.4 49.4 all-gather.3
  276.6 106.9 reduce-scatter.1
  396.6 78.5 all-gather.5

commit v7 on v6

--- a/solution.py
+++ b/solution.py
@@ -422,6 +422,8 @@
                     self.to(k, m).wait_send()
 
     class Spread:
+        factors = None
+
         def __init__(self, src, out, sems, phases):
             self.src, self.out, self.phases = src, out, phases
             if 1 in phases:
@@ -610,10 +612,17 @@
     line_parts = gathers + scatters
     for part in gathers + exchanges:
         part.begin()
+    early = []
     if worker and worker.early:
+        early = [part for part in square_parts if not part.factors]
+        for part in early:
+            part.begin()
         worker.begin()
-    for part in square_parts:
+    late = [part for part in square_parts if part not in early]
+    for part in late:
         part.begin()
+    for part in early:
+        part.mid()
     if chain and worker:
         begin_chain()
     for part in scatters:
@@ -634,13 +643,13 @@
             if s == chain_at:
                 begin_chain()
             if s == max(1, chain_at):
-                for part in square_parts:
+                for part in late:
                     part.mid()
             if worker:
                 worker.after_step(s)
     else:
         begin_chain()
-        for part in square_parts:
+        for part in late:
             part.mid()
     for part in line_parts:
         part.end()
@@ -1111,13 +1120,9 @@
     gu2 = gn2 * ffn_gain
     ffn_gain_part = jnp.sum(gn2 * u2, axis=0)
     gmid = cotangent.astype(f32) + r2 * (gu2 - u2 * jnp.mean(gu2 * u2, axis=1, keepdims=True))
-    if square:
-        ga, down_share = line_comm(5, "gather_ga", 50, ag=[gmid.astype(bf16)], sums=[g_down])
-    else:
-        (ga,) = line_comm(5, "gather_ga", 40, ag=[gmid.astype(bf16)])
-        down_share = sum_share(g_down)
-    ga, down_share, gu_share = after((ga, down_share, gu_share))
-    grad_down = join(down_share)
+    (ga,) = line_comm(5, "gather_ga", 40, ag=[gmid.astype(bf16)])
+    ga, gu_share, g_down = after((ga, gu_share, g_down))
+    grad_down = lax.psum(g_down, "replica")
 
     cols = w_gate.shape[1] // n
     heads_width = rot.shape[1] // 3

time: 639 us -> 635 us (level)
  Pallas kernels: 536 us -> 526 us
    pallas_call x8, Pallas kernels: 528 us -> 519 us  [line_comm(): pl.pallas_call(functools.partial(line_body, n, len(ag), products, [(len(t...]
  transfers between devices with their start and end apart: 3 -> 3, of which waited for: 0 -> 1; matrix products, arithmetic and copies ran while one was open for 6% -> 6% of each run, Pallas kernels for 46% -> 45%
where the time goes in v7:
time: 635 us; the launch traced here: 626 us
  Pallas kernels  526 us (83%)
  other arithmetic  42 us (7%)
  matrix products  22.6 us (4%)
  local copies, waits for them, and re-layouts  16.8 us (3%)
  between operations  14.4 us (2%)
    pallas_call x8, Pallas kernels, line_comm(): pl.pallas_call(functools.partial(line_body, n, len(ag), products, [(len(t...  519 us
    dot_general x1, matrix products, t_dot(): return lax.dot_general(a, b, dims_cols, preferred_element_type=f32)  14 us
  transfers between devices with their start and end apart: 3, of which 1 were waited for; matrix products, arithmetic and copies ran while one was open for 6% of the time, Pallas kernels for 45%

profile of v7, /device:TPU:0, one launch (start us, length us, event | category | flops | bytes accessed | tf_op | source)
XLA Modules:
  0.0 626.0 jit_solution(6661597873358140735)
XLA Ops:
  7.2 0.7 reshape.228
  7.9 0.7 convert.11
  8.5 1.3 copy.28
  9.9 1.0 copy.30.refs_0_
  10.9 0.7 scatter.16
  11.6 0.7 scatter.19.refs_3_
  12.3 0.6 copy-done.25
  12.8 0.6 copy-done.22
  13.4 26.1 %load_attn.1 = (bf16[8,64,256]{2,1,0:T(8,128)(2,1)}, bf16[8,64,256]{2,1,0:T(8,128)(2,1)}, bf16[8,64,256]{2,1,0:T(8,128)(2,1)}, s32[8,8,128]{2,1,0:T(8,128)}, f32[8,8,256]{2,1,0:T(8,128)}) custom-call(bf16[256,2048]{1,0:T(8,128)(2,1)} %refs_0_.1, bf16[256,2048]{1,0:T(8,128)(2,1)} %refs_1_.4, bf16[256,2048]{1,0:T(8,128)(2,1)} %refs_2_.2, s32[8,128]{1,0:T(8,128)} %copy-done.25, ...), custom_call_target="tpu_custom_call" | custom-call | flops 28750000128 | bytes 90000000 | tf_op jit(solution)/shard_map/load_attn/pallas_call | solution.py:884
  39.6 2.0 pad_maximum_fusion.refs_3_
  41.6 82.7 %load_ffn.1 = (bf16[8,128,2048]{2,1,0:T(8,128)(2,1)}, bf16[8,64,1024]{2,1,0:T(8,128)(2,1)}, bf16[8,64,1024]{2,1,0:T(8,128)(2,1)}, bf16[4,8,64,768]{3,2,1,0:T(8,128)(2,1)}) custom-call(bf16[128,2048]{1,0:T(8,128)(2,1)} %copy.30.refs_0_, bf16[256,8192]{1,0:T(8,128)(2,1)} %refs_1_.5, bf16[256,8192]{1,0:T(8,128)(2,1)} %refs_2_.3, ...), custom_call_target="tpu_custom_call" | custom-call | flops 92000002048 | bytes 288000000 | tf_op jit(solution)/shard_map/load_ffn/pallas_call | solution.py:884
  124.4 0.8 slice_bitcast_fusion
  125.2 1.5 fusion.15
  126.9 3.2 fusion
  130.1 1.9 fusion.12
  132.1 3.0 fusion.2.refs_5_
  135.1 0.3 pad_maximum_fusion.1
  135.5 0.2 copy.32.piece.refs_11_
  135.7 8.6 %fusion.17.lin = f32[1024,768]{1,0:T(8,128)} fusion(bf16[1024,2048]{1,0:T(8,128)(2,1)} %fusion.2.refs_5_, bf16[2048,768]{1,0:T(8,128)(2,1)} %bitcast.59), kind=kOutput, calls=%fused_computation.50 | convolution fusion | flops 3221225472 | bytes 10485760 | tf_op jit(solution)/shard_map/dot_general | solution.py:22
  144.3 7.3 %attention.1 = (bf16[1024,256]{1,0:T(8,128)(2,1)S(1)}, bf16[1024,768]{1,0:T(8,128)(2,1)S(1)}) custom-call(f32[1024,768]{1,0:T(8,128)} %fusion.17.lin, f32[1024,128]{1,0:T(8,128)S(1)} %get-tuple-element.161.cosine.refs_9_, f32[1024,128]{1,0:T(8,128)S(1)} %get-tuple-element.162.sine.refs_10_, s32[1024,1]{1,0:T(8,128)S(1)} %copy.32.piece.refs_11_), custom_call_target="tpu_custom_call" | custom-call | flops 536870912 | bytes 6291456 | tf_op jit(solution)/shard_map/attention/pallas_call | solution.py:957
  151.6 1.1 copy-done.3
  152.7 0.8 copy-done.4
  153.5 52.3 %attn_out.1 = (f32[128,2048]{1,0:T(8,128)}, bf16[4,8,64,1024]{3,2,1,0:T(8,128)(2,1)}, bf16[4,8,64,1024]{3,2,1,0:T(8,128)(2,1)}) custom-call(bf16[1024,256]{1,0:T(8,128)(2,1)} %copy-done.4, bf16[256,2048]{1,0:T(8,128)(2,1)} %refs_7_.1, bf16[8,64,1024]{2,1,0:T(8,128)(2,1)} %get-tuple-element.108.refs_2_, bf16[8,64,1024]{2,1,0:T(8,128)(2,1)} %get-tuple-element.109.refs_3_), custom_call_target="tpu_custom_call" | custom-call | flops 57500000256 | bytes 180000000 | tf_op jit(solution)/shard_map/attn_out/pallas_call | solution.py:884
  205.8 2.0 multiply_reduce_fusion.2
  208.0 0.3 copy.33
  208.4 1.0 copy.35.refs_0_
  209.4 53.1 %ffn_forward.1 = (bf16[8,128,2048]{2,1,0:T(8,128)(2,1)}, bf16[4,8,64,1024]{3,2,1,0:T(8,128)(2,1)}, bf16[4,8,64,1024]{3,2,1,0:T(8,128)(2,1)}, bf16[1024,1024]{1,0:T(8,128)(2,1)}, bf16[1024,2048]{1,0:T(8,128)(2,1)}) custom-call(bf16[128,2048]{1,0:T(8,128)(2,1)} %copy.35.refs_0_, ...), custom_call_target="tpu_custom_call", output_to_operand_aliasing={{1}: (1, {}), {2}: (2, {})} | custom-call | flops 69000003584 | bytes 216000000 | tf_op jit(solution)/shard_map/ffn_forward/pallas_call | solution.py:884
  262.5 14.0 %convolution_convert_fusion = bf16[2048,2048]{1,0:T(8,128)(2,1)} fusion(bf16[1024,2048]{1,0:T(8,128)(2,1)} %bitcast.87, bf16[1024,2048]{1,0:T(8,128)(2,1)} %get-tuple-element.117.refs_0_.refs_2_), kind=kOutput, calls=%fused_computation.5 | convolution fusion | flops 8594128896 | bytes 16777216 | tf_op jit(solution)/shard_map/dot_general | solution.py:30
  276.6 51.8 %scatter_gn2.1 = (f32[128,2048]{1,0:T(8,128)}, bf16[1024,2048]{1,0:T(8,128)(2,1)}) custom-call(bf16[1024,2048]{1,0:T(8,128)(2,1)} %get-tuple-element.117.refs_0_.refs_2_, bf16[2048,1024]{1,0:T(8,128)(2,1)} %bitcast.85, bf16[1024,2048]{1,0:T(8,128)(2,1)} %get-tuple-element.117.refs_0_.refs_2_, bf16[2048,1024]{1,0:T(8,128)(2,1)} %bitcast.86, ...), custom_call_target="tpu_custom_call" | custom-call | flops 50600001536 | bytes 158400000 | tf_op jit(solution)/shard_map/scatter_gn2/pallas_call | solution.py:884
  328.4 1.6 multiply_reduce_fusion
  330.0 0.5 copy-done.26
  330.5 2.3 fusion.13.refs_0_
  332.9 42.2 %gather_ga.1 = bf16[8,128,2048]{2,1,0:T(8,128)(2,1)} custom-call(bf16[128,2048]{1,0:T(8,128)(2,1)} %fusion.13.refs_0_), custom_call_target="tpu_custom_call" | custom-call | flops 46000001024 | bytes 144000000 | tf_op jit(solution)/shard_map/gather_ga/pallas_call | solution.py:884
  375.1 0.6 copy-done.28
  375.7 127.6 %scatter_gn1.1 = (f32[128,2048]{1,0:T(8,128)}, bf16[64,8192]{1,0:T(8,128)(2,1)}, bf16[64,8192]{1,0:T(8,128)(2,1)}, bf16[64,2048]{1,0:T(8,128)(2,1)}, bf16[512,76...) custom-call(bf16[2048,768]{1,0:T(8,128)(2,1)} %bitcast.60, bf16[8,64,2048]{2,1,0:T(8,128)(2,1)} %bitcast.57, ...), custom_call_target="tpu_custom_call" | custom-call | flops 1150000000 | bytes 3600000 | tf_op jit(solution)/shard_map/scatter_gn1/pallas_call | solution.py:884
  503.3 1.6 fusion.7
  505.0 0.7 select_maximum_fusion
  505.6 6.7 %bitcast_convert_fusion.1 = f32[256,8192]{1,0:T(8,128)} fusion(bf16[4,64,8192]{2,1,0:T(8,128)(2,1)} %get-tuple-element.135), kind=kLoop, calls=%fused_computation.7 | loop fusion | flops 2097152 | bytes 12582912 | tf_op jit(solution)/shard_map/convert_element_type | solution.py:1192
  512.3 3.9 all-reduce.5.cloned.1.call-done
  516.2 83.1 %rows_attn.1 = (f32[128,2048]{1,0:T(8,128)}, bf16[192,2048]{1,0:T(8,128)(2,1)}, f32[8,16,256]{2,1,0:T(8,128)}, bf16[4,64,8192]{2,1,0:T(8,128)(2,1)}, bf16[4,64,2...) custom-call(bf16[1024,1024]{1,0:T(8,128)(2,1)} %get-tuple-element.114.refs_4_.refs_0_, ...), custom_call_target="tpu_custom_call" | custom-call | flops 80499998720 | bytes 252000000 | tf_op jit(solution)/shard_map/rows_attn/pallas_call | solution.py:884
  599.3 1.2 reduce_sum.79
  600.6 0.6 fusion.16
  601.1 2.8 bitcast_convert_fusion.2
  603.9 3.4 fusion.14
  607.3 1.0 copy-done.16
  608.3 4.7 bitcast_convert_fusion
  613.1 4.4 convert_element_type.84
  617.6 1.6 fusion.10
  (73 shorter events, 0.8 us)
Async XLA Ops:
  7.2 202.2 %all-gather.2.cloned.1.call-start = ((), (), s32[]{:S(2)}) async-start(), calls=%async_computation.1 | async-start | bytes 4718592 | tf_op jit(solution)/shard_map/all_gather | solution.py:1078
  12.2 0.6 copy-start.25
  12.8 0.6 copy-start.22
  124.3 250.8 %reduce-scatter.2.cloned.1.call-start = ((), (), s32[]{:S(2)}) async-start(), calls=%async_computation.2 | async-start | bytes 10485760 | tf_op jit(solution)/shard_map/reduce_scatter | solution.py:1026
  126.7 203.3 %copy-start.19 = (f32[8,1,256]{2,1,0:T(1,128)}, f32[8,1,256]{2,1,0:T(1,128)S(1)}, u32[]{:S(2)}) copy-start(f32[8,1,256]{2,1,0:T(1,128)S(1)} %get-tuple-element.153) | copy-start | bytes 24580
  126.9 5.1 copy-start.7
  135.4 8.8 %copy-start = (f32[1024,128]{1,0:T(8,128)}, f32[1024,128]{1,0:T(8,128)S(1)}, u32[]{:S(2)}) copy-start(f32[1024,128]{1,0:T(8,128)S(1)} %get-tuple-element.161.cosine.refs_9_) | copy-start | bytes 1572868
  135.5 8.8 %copy-start.1 = (f32[1024,128]{1,0:T(8,128)}, f32[1024,128]{1,0:T(8,128)S(1)}, u32[]{:S(2)}) copy-start(f32[1024,128]{1,0:T(8,128)S(1)} %get-tuple-element.162.sine.refs_10_) | copy-start | bytes 1572868
  135.7 8.6 %copy-start.2 = (s32[1024,1]{1,0:T(8,128)}, s32[1024,1]{1,0:T(8,128)S(1)}, u32[]{:S(2)}) copy-start(s32[1024,1]{1,0:T(8,128)S(1)} %copy.32.piece.refs_11_) | copy-start | bytes 12292
  151.5 1.1 copy-start.3
  152.7 0.8 copy-start.4
  153.5 52.4 %copy-start.10 = (bf16[128,2048]{1,0:T(8,128)(2,1)S(1)}, bf16[128,2048]{1,0:T(8,128)(2,1)}, u32[]{:S(2)}) copy-start(bf16[128,2048]{1,0:T(8,128)(2,1)} %param.21) | copy-start | bytes 1572868
  207.9 122.2 %copy-start.5 = (f32[128,2048]{1,0:T(8,128)}, f32[128,2048]{1,0:T(8,128)S(1)}, u32[]{:S(2)}) copy-start(f32[128,2048]{1,0:T(8,128)S(1)} %get-tuple-element.144) | copy-start | bytes 3145732
  207.9 122.2 %copy-start.23 = (f32[128]{0:T(128)}, f32[128]{0:T(128)S(1)}, u32[]{:S(2)}) copy-start(f32[128]{0:T(128)S(1)} %add_rsqrt_fusion.2) | copy-start | bytes 1540
  276.5 239.7 %all-reduce.5.cloned.1.call-start = ((), (), s32[]{:S(2)}) async-start(), calls=%async_computation.3 | async-start | bytes 8388608 | tf_op jit(solution)/shard_map/psum | solution.py:1125
  276.6 54.0 %copy-start.13 = (bf16[128,2048]{1,0:T(8,128)(2,1)S(1)}, bf16[128,2048]{1,0:T(8,128)(2,1)}, u32[]{:S(2)}) copy-start(bf16[128,2048]{1,0:T(8,128)(2,1)} %param.33) | copy-start | bytes 1572868
  330.0 0.5 copy-start.26
  375.1 0.7 copy-start.28
  375.7 127.6 %copy-start.11 = (bf16[128,2048]{1,0:T(8,128)(2,1)S(1)}, bf16[128,2048]{1,0:T(8,128)(2,1)}, u32[]{:S(2)}) copy-start(bf16[128,2048]{1,0:T(8,128)(2,1)} %param.21) | copy-start | bytes 1572868
  375.7 127.6 %copy-start.21 = (f32[8,1,256]{2,1,0:T(1,128)S(1)}, f32[8,1,256]{2,1,0:T(1,128)}, u32[]{:S(2)}) copy-start(f32[8,1,256]{2,1,0:T(1,128)} %get-tuple-element.151) | copy-start | bytes 24580
  599.3 4.6 copy-start.8
  603.9 4.4 copy-start.16
  608.3 4.7 copy-start.15
  613.0 4.5 copy-start.6
  613.0 4.5 copy-start.9
  613.0 4.5 copy-start.12
  613.0 4.5 copy-start.14
  613.0 4.5 copy-start.17
  613.0 4.5 copy-start.18
  613.0 4.5 copy-start.20
  613.0 4.5 copy-start.24
  613.0 4.5 copy-start.27
Sparse Core Ops, SparseCore 0:
  124.4 49.3 all-gather.1
  276.6 85.2 reduce-scatter.1
  375.2 140.9 all-reduce.4

commit v8 on v7

--- a/solution.py
+++ b/solution.py
@@ -719,7 +719,7 @@
         else:
             self.w = ins[2:]
         self.rows = 2 * gather.x.shape[0]
-        self.tile = min(256, self.hid.shape[1])
+        self.tile = min(512, self.hid.shape[1])
 
     def load(self, i, k):
         q = self.blocks[k]
@@ -1153,11 +1153,10 @@
         )
         gn1 = gn1 if tidy else owners_first(gn1)
         qkv_back = rows_back(qkv_share.reshape(n, -1, 3 * heads_width), (0, heads_width), 3)
-        up_rows, grad_down = after((up_rows, grad_down))
         mlp, _, _, grad_up, grad_out, grad_qkv, gains = line_comm(
             7,
             "rows_attn",
-            70,
+            1,
             rs=[[(hid, w_down, False, 0)]],
             a2a=[qkv_back, gain_parts(gn1)],
             spread=[(up_rows, (1, 2)), (out_share, (1, 2))],

time: 635 us -> 629 us (level)
  transfers between devices with their start and end apart: 3 -> 3, of which waited for: 1 -> 0; matrix products, arithmetic and copies ran while one was open for 6% -> 8% of each run, Pallas kernels for 45% -> 59%
where the time goes in v8:
time: 629 us; the launch traced here: 621 us
  Pallas kernels  526 us (84%)
  other arithmetic  41.8 us (7%)
  matrix products  22.6 us (4%)
  local copies, waits for them, and re-layouts  15.3 us (2%)
  between operations  14.5 us (2%)
    pallas_call x8, Pallas kernels, line_comm(): pl.pallas_call(functools.partial(line_body, n, len(ag), products, [(len(t...  519 us
    dot_general x1, matrix products, t_dot(): return lax.dot_general(a, b, dims_cols, preferred_element_type=f32)  14 us
  transfers between devices with their start and end apart: 3, of which 0 were waited for; matrix products, arithmetic and copies ran while one was open for 8% of the time, Pallas kernels for 59%

profile of v8, /device:TPU:0, one launch (start us, length us, event | category | flops | bytes accessed | tf_op | source)
XLA Modules:
  0.0 620.8 jit_solution(15747913205376866996)
XLA Ops:
  7.2 0.7 reshape.228
  7.9 0.7 convert.11
  8.5 1.3 copy.28
  9.9 1.0 copy.30.refs_0_
  10.9 0.7 scatter.16
  11.6 0.7 scatter.19.refs_3_
  12.3 0.6 copy-done.18
  12.8 0.6 copy-done.17
  13.4 26.1 %load_attn.1 = (bf16[8,64,256]{2,1,0:T(8,128)(2,1)}, bf16[8,64,256]{2,1,0:T(8,128)(2,1)}, bf16[8,64,256]{2,1,0:T(8,128)(2,1)}, s32[8,8,128]{2,1,0:T(8,128)}, f32[8,8,256]{2,1,0:T(8,128)}) custom-call(bf16[256,2048]{1,0:T(8,128)(2,1)} %refs_0_.1, bf16[256,2048]{1,0:T(8,128)(2,1)} %refs_1_.4, bf16[256,2048]{1,0:T(8,128)(2,1)} %refs_2_.2, s32[8,128]{1,0:T(8,128)} %copy-done.18, ...), custom_call_target="tpu_custom_call" | custom-call | flops 28750000128 | bytes 90000000 | tf_op jit(solution)/shard_map/load_attn/pallas_call | solution.py:884
  39.6 2.0 pad_maximum_fusion.refs_3_
  41.6 82.7 %load_ffn.1 = (bf16[8,128,2048]{2,1,0:T(8,128)(2,1)}, bf16[8,64,1024]{2,1,0:T(8,128)(2,1)}, bf16[8,64,1024]{2,1,0:T(8,128)(2,1)}, bf16[4,8,64,768]{3,2,1,0:T(8,128)(2,1)}) custom-call(bf16[128,2048]{1,0:T(8,128)(2,1)} %copy.30.refs_0_, bf16[256,8192]{1,0:T(8,128)(2,1)} %refs_1_.5, bf16[256,8192]{1,0:T(8,128)(2,1)} %refs_2_.3, ...), custom_call_target="tpu_custom_call" | custom-call | flops 92000002048 | bytes 288000000 | tf_op jit(solution)/shard_map/load_ffn/pallas_call | solution.py:884
  124.4 0.8 slice_bitcast_fusion
  125.2 1.5 fusion.15
  126.8 0.1 reshape_reshape_squeeze.3
  126.8 0.1 mul.128
  126.9 3.2 fusion
  130.2 1.9 fusion.12
  132.1 3.0 fusion.2.refs_5_
  135.1 0.3 pad_maximum_fusion.1
  135.5 0.2 copy.32.piece.refs_11_
  135.7 8.6 %fusion.17.lin = f32[1024,768]{1,0:T(8,128)} fusion(bf16[1024,2048]{1,0:T(8,128)(2,1)} %fusion.2.refs_5_, bf16[2048,768]{1,0:T(8,128)(2,1)} %bitcast.59), kind=kOutput, calls=%fused_computation.50 | convolution fusion | flops 3221225472 | bytes 10485760 | tf_op jit(solution)/shard_map/dot_general | solution.py:22
  144.3 7.2 %attention.1 = (bf16[1024,256]{1,0:T(8,128)(2,1)S(1)}, bf16[1024,768]{1,0:T(8,128)(2,1)S(1)}) custom-call(f32[1024,768]{1,0:T(8,128)} %fusion.17.lin, f32[1024,128]{1,0:T(8,128)S(1)} %get-tuple-element.157.cosine.refs_9_, f32[1024,128]{1,0:T(8,128)S(1)} %get-tuple-element.158.sine.refs_10_, s32[1024,1]{1,0:T(8,128)S(1)} %copy.32.piece.refs_11_), custom_call_target="tpu_custom_call" | custom-call | flops 536870912 | bytes 6291456 | tf_op jit(solution)/shard_map/attention/pallas_call | solution.py:957
  151.6 1.1 copy-done.3
  152.7 0.8 copy-done.4
  153.5 52.4 %attn_out.1 = (f32[128,2048]{1,0:T(8,128)}, bf16[4,8,64,1024]{3,2,1,0:T(8,128)(2,1)}, bf16[4,8,64,1024]{3,2,1,0:T(8,128)(2,1)}) custom-call(bf16[1024,256]{1,0:T(8,128)(2,1)} %copy-done.4, bf16[256,2048]{1,0:T(8,128)(2,1)} %refs_7_.1, bf16[8,64,1024]{2,1,0:T(8,128)(2,1)} %get-tuple-element.106.refs_2_, bf16[8,64,1024]{2,1,0:T(8,128)(2,1)} %get-tuple-element.107.refs_3_), custom_call_target="tpu_custom_call" | custom-call | flops 57500000256 | bytes 180000000 | tf_op jit(solution)/shard_map/attn_out/pallas_call | solution.py:884
  205.9 1.5 multiply_reduce_fusion.2
  207.4 0.2 multiply_convert_fusion
  207.6 0.3 copy.33
  207.9 1.0 copy.35.refs_0_
  208.9 51.9 %ffn_forward.1 = (bf16[8,128,2048]{2,1,0:T(8,128)(2,1)}, bf16[4,8,64,1024]{3,2,1,0:T(8,128)(2,1)}, bf16[4,8,64,1024]{3,2,1,0:T(8,128)(2,1)}, bf16[1024,1024]{1,0:T(8,128)(2,1)}, bf16[1024,2048]{1,0:T(8,128)(2,1)}) custom-call(bf16[128,2048]{1,0:T(8,128)(2,1)} %copy.35.refs_0_, ...), custom_call_target="tpu_custom_call", output_to_operand_aliasing={{1}: (1, {}), {2}: (2, {})} | custom-call | flops 69000003584 | bytes 216000000 | tf_op jit(solution)/shard_map/ffn_forward/pallas_call | solution.py:884
  260.8 14.0 %convolution_convert_fusion = bf16[2048,2048]{1,0:T(8,128)(2,1)} fusion(bf16[1024,2048]{1,0:T(8,128)(2,1)} %bitcast.87, bf16[1024,2048]{1,0:T(8,128)(2,1)} %get-tuple-element.115.refs_0_.refs_2_), kind=kOutput, calls=%fused_computation.5 | convolution fusion | flops 8594128896 | bytes 16777216 | tf_op jit(solution)/shard_map/dot_general | solution.py:30
  274.9 51.8 %scatter_gn2.1 = (f32[128,2048]{1,0:T(8,128)}, bf16[1024,2048]{1,0:T(8,128)(2,1)}) custom-call(bf16[1024,2048]{1,0:T(8,128)(2,1)} %get-tuple-element.115.refs_0_.refs_2_, bf16[2048,1024]{1,0:T(8,128)(2,1)} %bitcast.85, bf16[1024,2048]{1,0:T(8,128)(2,1)} %get-tuple-element.115.refs_0_.refs_2_, bf16[2048,1024]{1,0:T(8,128)(2,1)} %bitcast.86, ...), custom_call_target="tpu_custom_call" | custom-call | flops 50600001536 | bytes 158400000 | tf_op jit(solution)/shard_map/scatter_gn2/pallas_call | solution.py:884
  326.7 1.6 multiply_reduce_fusion
  328.3 2.4 fusion.13.refs_0_
  330.7 41.5 %gather_ga.1 = bf16[8,128,2048]{2,1,0:T(8,128)(2,1)} custom-call(bf16[128,2048]{1,0:T(8,128)(2,1)} %fusion.13.refs_0_), custom_call_target="tpu_custom_call" | custom-call | flops 46000001024 | bytes 144000000 | tf_op jit(solution)/shard_map/gather_ga/pallas_call | solution.py:884
  372.3 128.0 %scatter_gn1.1 = (f32[128,2048]{1,0:T(8,128)}, bf16[64,8192]{1,0:T(8,128)(2,1)}, bf16[64,8192]{1,0:T(8,128)(2,1)}, bf16[64,2048]{1,0:T(8,128)(2,1)}, bf16[512,76...) custom-call(bf16[2048,768]{1,0:T(8,128)(2,1)} %bitcast.60, bf16[8,64,2048]{2,1,0:T(8,128)(2,1)} %bitcast.57, ...), custom_call_target="tpu_custom_call" | custom-call | flops 1150000000 | bytes 3600000 | tf_op jit(solution)/shard_map/scatter_gn1/pallas_call | solution.py:884
  500.3 1.6 fusion.7
  502.0 0.7 select_maximum_fusion
  502.7 84.8 %rows_attn.1 = (f32[128,2048]{1,0:T(8,128)}, bf16[192,2048]{1,0:T(8,128)(2,1)}, f32[8,16,256]{2,1,0:T(8,128)}, bf16[4,64,8192]{2,1,0:T(8,128)(2,1)}, bf16[4,64,2...) custom-call(bf16[1024,1024]{1,0:T(8,128)(2,1)} %get-tuple-element.112.refs_4_.refs_0_, ...), custom_call_target="tpu_custom_call" | custom-call | flops 1150000000 | bytes 3600000 | tf_op jit(solution)/shard_map/rows_attn/pallas_call | solution.py:884
  587.5 1.1 reduce_sum.79
  588.6 0.6 fusion.16
  589.2 3.1 bitcast_convert_fusion.2
  592.2 3.3 fusion.14
  595.5 0.7 copy-done.15
  596.3 1.6 fusion.10
  597.9 4.7 bitcast_convert_fusion
  602.5 4.7 bitcast_convert_fusion.1
  607.2 6.7 %convert_element_type.84 = f32[1024,2048]{1,0:T(8,128)} convert(bf16[1024,2048]{1,0:T(8,128)(2,1)} %all-reduce.5.cloned.1.call-done) | non-fusion elementwise | flops 2097152 | bytes 12582912 | tf_op jit(solution)/shard_map/convert_element_type | solution.py:1193
  (53 shorter events, 0.4 us)
Async XLA Ops:
  7.2 201.8 %all-gather.2.cloned.1.call-start = ((), (), s32[]{:S(2)}) async-start(), calls=%async_computation.1 | async-start | bytes 4718592 | tf_op jit(solution)/shard_map/all_gather | solution.py:1078
  12.2 0.6 copy-start.18
  12.8 0.6 copy-start.17
  124.3 247.9 %reduce-scatter.2.cloned.1.call-start = ((), (), s32[]{:S(2)}) async-start(), calls=%async_computation.2 | async-start | bytes 10485760 | tf_op jit(solution)/shard_map/reduce_scatter | solution.py:1026
  126.9 5.1 copy-start.5
  135.5 8.8 %copy-start = (f32[1024,128]{1,0:T(8,128)}, f32[1024,128]{1,0:T(8,128)S(1)}, u32[]{:S(2)}) copy-start(f32[1024,128]{1,0:T(8,128)S(1)} %get-tuple-element.157.cosine.refs_9_) | copy-start | bytes 1572868
  135.5 8.8 %copy-start.1 = (f32[1024,128]{1,0:T(8,128)}, f32[1024,128]{1,0:T(8,128)S(1)}, u32[]{:S(2)}) copy-start(f32[1024,128]{1,0:T(8,128)S(1)} %get-tuple-element.158.sine.refs_10_) | copy-start | bytes 1572868
  135.7 8.6 %copy-start.2 = (s32[1024,1]{1,0:T(8,128)}, s32[1024,1]{1,0:T(8,128)S(1)}, u32[]{:S(2)}) copy-start(s32[1024,1]{1,0:T(8,128)S(1)} %copy.32.piece.refs_11_) | copy-start | bytes 12292
  151.6 1.1 copy-start.3
  152.7 0.8 copy-start.4
  153.5 52.4 %copy-start.8 = (bf16[128,2048]{1,0:T(8,128)(2,1)S(1)}, bf16[128,2048]{1,0:T(8,128)(2,1)}, u32[]{:S(2)}) copy-start(bf16[128,2048]{1,0:T(8,128)(2,1)} %param.21) | copy-start | bytes 1572868
  274.9 332.3 %all-reduce.5.cloned.1.call-start = ((), (), s32[]{:S(2)}) async-start(), calls=%async_computation.3 | async-start | bytes 8388608 | tf_op jit(solution)/shard_map/psum | solution.py:1125
  274.9 53.4 %copy-start.10 = (bf16[128,2048]{1,0:T(8,128)(2,1)S(1)}, bf16[128,2048]{1,0:T(8,128)(2,1)}, u32[]{:S(2)}) copy-start(bf16[128,2048]{1,0:T(8,128)(2,1)} %param.33) | copy-start | bytes 1572868
  372.3 128.1 %copy-start.9 = (bf16[128,2048]{1,0:T(8,128)(2,1)S(1)}, bf16[128,2048]{1,0:T(8,128)(2,1)}, u32[]{:S(2)}) copy-start(bf16[128,2048]{1,0:T(8,128)(2,1)} %param.21) | copy-start | bytes 1572868
  372.3 128.1 %copy-start.16 = (f32[8,1,256]{2,1,0:T(1,128)S(1)}, f32[8,1,256]{2,1,0:T(1,128)}, u32[]{:S(2)}) copy-start(f32[8,1,256]{2,1,0:T(1,128)} %get-tuple-element.147) | copy-start | bytes 24580
  588.6 3.7 copy-start.6
  592.2 3.3 copy-start.7
  592.2 3.3 copy-start.11
  592.2 3.3 copy-start.14
  592.2 4.0 copy-start.15
  595.5 2.4 copy-start.13
  597.9 4.7 copy-start.12
Sparse Core Ops, SparseCore 0:
  124.4 49.4 all-gather.1
  275.0 85.4 reduce-scatter.1
  372.4 142.8 all-reduce.4

commit v9 on v8

--- a/solution.py
+++ b/solution.py
@@ -1007,7 +1007,7 @@
 def sum_blocks(g):
     n = lax.axis_size("inner")
     cols = g.shape[1]
-    return ((g,), (n,) + (g.shape[0] // n, cols), lambda refs, other, m: refs[0].at[pl.ds(pl.multiple_of(other * 16, 16), 16)], lambda ref, other, m: ref.at[other], 1, False)
+    return ((g,), (n,) + (g.shape[0] // n, cols), lambda refs, other, m: refs[0].at[pl.ds(pl.multiple_of(other * 8, 8), 8)], lambda ref, other, m: ref.at[other], 1, False)
 
 
 def shares_first(x):
@@ -1133,7 +1133,7 @@
 
     def gain_parts(gn1):
         both = jnp.stack([jnp.sum(gn1 * u1, axis=0).reshape(n, rows), ffn_gain_part.reshape(n, rows)], axis=1)
-        return sum_blocks(jnp.pad(both, ((0, 0), (0, 14), (0, 0))).reshape(n * 16, rows))
+        return sum_blocks(jnp.pad(both, ((0, 0), (0, 6), (0, 0))).reshape(n * 8, rows))
 
     held = [pltpu.VMEM((length, heads_width), bf16)] + [pltpu.VMEM((length, HEAD_DIM), f32)] * 2
     work = (Backward, [ga, w_out, rot, cosine, sine, pieces], [rot.shape], held)

time: 629 us -> 627 us (level)
  no operation moved by 1% of the time
where the time goes in v9:
time: 627 us; the launch traced here: 619 us
  Pallas kernels  524 us (84%)
  other arithmetic  41.7 us (7%)
  matrix products  22.6 us (4%)
  local copies, waits for them, and re-layouts  15.3 us (2%)
  between operations  14.5 us (2%)
    pallas_call x8, Pallas kernels, line_comm(): pl.pallas_call(functools.partial(line_body, n, len(ag), products, [(len(t...  517 us
    dot_general x1, matrix products, t_dot(): return lax.dot_general(a, b, dims_cols, preferred_element_type=f32)  14 us
  transfers between devices with their start and end apart: 3, of which 0 were waited for; matrix products, arithmetic and copies ran while one was open for 8% of the time, Pallas kernels for 59%

profile of v9, /device:TPU:0, one launch (start us, length us, event | category | flops | bytes accessed | tf_op | source)
XLA Modules:
  0.0 618.7 jit_solution(6789647465484315775)
XLA Ops:
  7.2 0.7 reshape.228
  7.9 0.7 convert.11
  8.5 1.3 copy.28
  9.9 1.0 copy.30.refs_0_
  10.9 0.7 scatter.16
  11.6 0.7 scatter.19.refs_3_
  12.3 0.6 copy-done.18
  12.8 0.6 copy-done.17
  13.4 26.1 %load_attn.1 = (bf16[8,64,256]{2,1,0:T(8,128)(2,1)}, bf16[8,64,256]{2,1,0:T(8,128)(2,1)}, bf16[8,64,256]{2,1,0:T(8,128)(2,1)}, s32[8,8,128]{2,1,0:T(8,128)}, f32[8,8,256]{2,1,0:T(8,128)}) custom-call(bf16[256,2048]{1,0:T(8,128)(2,1)} %refs_0_.1, bf16[256,2048]{1,0:T(8,128)(2,1)} %refs_1_.4, bf16[256,2048]{1,0:T(8,128)(2,1)} %refs_2_.2, s32[8,128]{1,0:T(8,128)} %copy-done.18, ...), custom_call_target="tpu_custom_call" | custom-call | flops 28750000128 | bytes 90000000 | tf_op jit(solution)/shard_map/load_attn/pallas_call | solution.py:884
  39.6 2.0 pad_maximum_fusion.refs_3_
  41.6 82.7 %load_ffn.1 = (bf16[8,128,2048]{2,1,0:T(8,128)(2,1)}, bf16[8,64,1024]{2,1,0:T(8,128)(2,1)}, bf16[8,64,1024]{2,1,0:T(8,128)(2,1)}, bf16[4,8,64,768]{3,2,1,0:T(8,128)(2,1)}) custom-call(bf16[128,2048]{1,0:T(8,128)(2,1)} %copy.30.refs_0_, bf16[256,8192]{1,0:T(8,128)(2,1)} %refs_1_.5, bf16[256,8192]{1,0:T(8,128)(2,1)} %refs_2_.3, ...), custom_call_target="tpu_custom_call" | custom-call | flops 92000002048 | bytes 288000000 | tf_op jit(solution)/shard_map/load_ffn/pallas_call | solution.py:884
  124.4 0.8 slice_bitcast_fusion
  125.2 1.5 fusion.16
  126.8 0.1 reshape_reshape_squeeze.3
  126.8 0.1 mul.128
  126.9 3.2 fusion
  130.2 1.9 fusion.12
  132.1 3.0 fusion.2.refs_5_
  135.1 0.3 pad_maximum_fusion.1
  135.5 0.2 copy.32.piece.refs_11_
  135.7 8.6 %fusion.18.lin = f32[1024,768]{1,0:T(8,128)} fusion(bf16[1024,2048]{1,0:T(8,128)(2,1)} %fusion.2.refs_5_, bf16[2048,768]{1,0:T(8,128)(2,1)} %bitcast.60), kind=kOutput, calls=%fused_computation.51 | convolution fusion | flops 3221225472 | bytes 10485760 | tf_op jit(solution)/shard_map/dot_general | solution.py:22
  144.3 7.2 %attention.1 = (bf16[1024,256]{1,0:T(8,128)(2,1)S(1)}, bf16[1024,768]{1,0:T(8,128)(2,1)S(1)}) custom-call(f32[1024,768]{1,0:T(8,128)} %fusion.18.lin, f32[1024,128]{1,0:T(8,128)S(1)} %get-tuple-element.157.cosine.refs_9_, f32[1024,128]{1,0:T(8,128)S(1)} %get-tuple-element.158.sine.refs_10_, s32[1024,1]{1,0:T(8,128)S(1)} %copy.32.piece.refs_11_), custom_call_target="tpu_custom_call" | custom-call | flops 536870912 | bytes 6291456 | tf_op jit(solution)/shard_map/attention/pallas_call | solution.py:957
  151.6 1.1 copy-done.3
  152.7 0.8 copy-done.4
  153.5 52.4 %attn_out.1 = (f32[128,2048]{1,0:T(8,128)}, bf16[4,8,64,1024]{3,2,1,0:T(8,128)(2,1)}, bf16[4,8,64,1024]{3,2,1,0:T(8,128)(2,1)}) custom-call(bf16[1024,256]{1,0:T(8,128)(2,1)} %copy-done.4, bf16[256,2048]{1,0:T(8,128)(2,1)} %refs_7_.1, bf16[8,64,1024]{2,1,0:T(8,128)(2,1)} %get-tuple-element.106.refs_2_, bf16[8,64,1024]{2,1,0:T(8,128)(2,1)} %get-tuple-element.107.refs_3_), custom_call_target="tpu_custom_call" | custom-call | flops 57500000256 | bytes 180000000 | tf_op jit(solution)/shard_map/attn_out/pallas_call | solution.py:884
  205.9 1.5 multiply_reduce_fusion.2
  207.4 0.2 multiply_convert_fusion
  207.6 0.3 copy.33
  207.9 1.0 copy.35.refs_0_
  208.9 51.9 %ffn_forward.1 = (bf16[8,128,2048]{2,1,0:T(8,128)(2,1)}, bf16[4,8,64,1024]{3,2,1,0:T(8,128)(2,1)}, bf16[4,8,64,1024]{3,2,1,0:T(8,128)(2,1)}, bf16[1024,1024]{1,0:T(8,128)(2,1)}, bf16[1024,2048]{1,0:T(8,128)(2,1)}) custom-call(bf16[128,2048]{1,0:T(8,128)(2,1)} %copy.35.refs_0_, ...), custom_call_target="tpu_custom_call", output_to_operand_aliasing={{1}: (1, {}), {2}: (2, {})} | custom-call | flops 69000003584 | bytes 216000000 | tf_op jit(solution)/shard_map/ffn_forward/pallas_call | solution.py:884
  260.8 14.0 %convolution_convert_fusion = bf16[2048,2048]{1,0:T(8,128)(2,1)} fusion(bf16[1024,2048]{1,0:T(8,128)(2,1)} %bitcast.87, bf16[1024,2048]{1,0:T(8,128)(2,1)} %get-tuple-element.115.refs_0_.refs_2_), kind=kOutput, calls=%fused_computation.5 | convolution fusion | flops 8594128896 | bytes 16777216 | tf_op jit(solution)/shard_map/dot_general | solution.py:30
  274.9 51.8 %scatter_gn2.1 = (f32[128,2048]{1,0:T(8,128)}, bf16[1024,2048]{1,0:T(8,128)(2,1)}) custom-call(bf16[1024,2048]{1,0:T(8,128)(2,1)} %get-tuple-element.115.refs_0_.refs_2_, bf16[2048,1024]{1,0:T(8,128)(2,1)} %bitcast.85, bf16[1024,2048]{1,0:T(8,128)(2,1)} %get-tuple-element.115.refs_0_.refs_2_, bf16[2048,1024]{1,0:T(8,128)(2,1)} %bitcast.86, ...), custom_call_target="tpu_custom_call" | custom-call | flops 50600001536 | bytes 158400000 | tf_op jit(solution)/shard_map/scatter_gn2/pallas_call | solution.py:884
  326.7 1.6 multiply_reduce_fusion
  328.3 2.4 fusion.14.refs_0_
  330.7 41.5 %gather_ga.1 = bf16[8,128,2048]{2,1,0:T(8,128)(2,1)} custom-call(bf16[128,2048]{1,0:T(8,128)(2,1)} %fusion.14.refs_0_), custom_call_target="tpu_custom_call" | custom-call | flops 46000001024 | bytes 144000000 | tf_op jit(solution)/shard_map/gather_ga/pallas_call | solution.py:884
  372.3 128.0 %scatter_gn1.1 = (f32[128,2048]{1,0:T(8,128)}, bf16[64,8192]{1,0:T(8,128)(2,1)}, bf16[64,8192]{1,0:T(8,128)(2,1)}, bf16[64,2048]{1,0:T(8,128)(2,1)}, bf16[512,76...) custom-call(bf16[2048,768]{1,0:T(8,128)(2,1)} %bitcast.61, bf16[8,64,2048]{2,1,0:T(8,128)(2,1)} %bitcast.58, ...), custom_call_target="tpu_custom_call" | custom-call | flops 1150000000 | bytes 3600000 | tf_op jit(solution)/shard_map/scatter_gn1/pallas_call | solution.py:884
  500.3 1.6 fusion.7
  502.0 0.7 fusion.13.refs_3_
  502.6 82.8 %rows_attn.1 = (f32[128,2048]{1,0:T(8,128)}, bf16[192,2048]{1,0:T(8,128)(2,1)}, f32[8,8,256]{2,1,0:T(8,128)}, bf16[4,64,8192]{2,1,0:T(8,128)(2,1)}, bf16[4,64,20...) custom-call(bf16[1024,1024]{1,0:T(8,128)(2,1)} %get-tuple-element.112.refs_4_.refs_0_, ...), custom_call_target="tpu_custom_call" | custom-call | flops 1150000000 | bytes 3600000 | tf_op jit(solution)/shard_map/rows_attn/pallas_call | solution.py:884
  585.5 1.0 reduce_sum.79
  586.5 0.6 fusion.17
  587.1 3.1 bitcast_convert_fusion.2
  590.1 3.3 fusion.15
  593.4 0.7 copy-done.15
  594.2 1.6 fusion.10
  595.8 4.7 bitcast_convert_fusion
  600.4 4.7 bitcast_convert_fusion.1
  605.1 6.7 %convert_element_type.84 = f32[1024,2048]{1,0:T(8,128)} convert(bf16[1024,2048]{1,0:T(8,128)(2,1)} %all-reduce.5.cloned.1.call-done) | non-fusion elementwise | flops 2097152 | bytes 12582912 | tf_op jit(solution)/shard_map/convert_element_type | solution.py:1193
  (53 shorter events, 0.4 us)
Async XLA Ops:
  7.2 201.8 %all-gather.2.cloned.1.call-start = ((), (), s32[]{:S(2)}) async-start(), calls=%async_computation.1 | async-start | bytes 4718592 | tf_op jit(solution)/shard_map/all_gather | solution.py:1078
  12.2 0.6 copy-start.18
  12.8 0.6 copy-start.17
  124.3 247.9 %reduce-scatter.2.cloned.1.call-start = ((), (), s32[]{:S(2)}) async-start(), calls=%async_computation.2 | async-start | bytes 10485760 | tf_op jit(solution)/shard_map/reduce_scatter | solution.py:1026
  126.9 5.1 copy-start.5
  135.5 8.8 %copy-start = (f32[1024,128]{1,0:T(8,128)}, f32[1024,128]{1,0:T(8,128)S(1)}, u32[]{:S(2)}) copy-start(f32[1024,128]{1,0:T(8,128)S(1)} %get-tuple-element.157.cosine.refs_9_) | copy-start | bytes 1572868
  135.5 8.8 %copy-start.1 = (f32[1024,128]{1,0:T(8,128)}, f32[1024,128]{1,0:T(8,128)S(1)}, u32[]{:S(2)}) copy-start(f32[1024,128]{1,0:T(8,128)S(1)} %get-tuple-element.158.sine.refs_10_) | copy-start | bytes 1572868
  135.7 8.6 %copy-start.2 = (s32[1024,1]{1,0:T(8,128)}, s32[1024,1]{1,0:T(8,128)S(1)}, u32[]{:S(2)}) copy-start(s32[1024,1]{1,0:T(8,128)S(1)} %copy.32.piece.refs_11_) | copy-start | bytes 12292
  151.6 1.1 copy-start.3
  152.7 0.8 copy-start.4
  153.5 52.4 %copy-start.8 = (bf16[128,2048]{1,0:T(8,128)(2,1)S(1)}, bf16[128,2048]{1,0:T(8,128)(2,1)}, u32[]{:S(2)}) copy-start(bf16[128,2048]{1,0:T(8,128)(2,1)} %param.21) | copy-start | bytes 1572868
  274.9 330.2 %all-reduce.5.cloned.1.call-start = ((), (), s32[]{:S(2)}) async-start(), calls=%async_computation.3 | async-start | bytes 8388608 | tf_op jit(solution)/shard_map/psum | solution.py:1125
  274.9 53.4 %copy-start.10 = (bf16[128,2048]{1,0:T(8,128)(2,1)S(1)}, bf16[128,2048]{1,0:T(8,128)(2,1)}, u32[]{:S(2)}) copy-start(bf16[128,2048]{1,0:T(8,128)(2,1)} %param.33) | copy-start | bytes 1572868
  372.3 128.1 %copy-start.9 = (bf16[128,2048]{1,0:T(8,128)(2,1)S(1)}, bf16[128,2048]{1,0:T(8,128)(2,1)}, u32[]{:S(2)}) copy-start(bf16[128,2048]{1,0:T(8,128)(2,1)} %param.21) | copy-start | bytes 1572868
  372.3 128.1 %copy-start.16 = (f32[8,1,256]{2,1,0:T(1,128)S(1)}, f32[8,1,256]{2,1,0:T(1,128)}, u32[]{:S(2)}) copy-start(f32[8,1,256]{2,1,0:T(1,128)} %get-tuple-element.147) | copy-start | bytes 24580
  586.5 3.7 copy-start.6
  590.1 3.3 copy-start.7
  590.1 3.3 copy-start.11
  590.1 3.3 copy-start.14
  590.1 4.0 copy-start.15
  593.4 2.4 copy-start.13
  595.8 4.7 copy-start.12
Sparse Core Ops, SparseCore 0:
  124.4 49.4 all-gather.1
  275.0 85.4 reduce-scatter.1
  372.4 142.8 all-reduce.4
